TPU v7x, 32 devices: a whole 2x2x4 slice. The times are simulated.
32 devices in a mesh: seq: 2 (over y), batch: 16 (over z, x, core).
Axes of the slice: x: 2, y: 2, z: 4, core: 2. Of those that a mesh axis runs over, the one named last changes fastest.
Arguments:
- layer_input: bfloat16 [32, 2, 256, 768], P('batch', 'seq'), may hold values from -6 to 6
- cotangent: bfloat16 [32, 2, 256, 768], P('batch', 'seq'), may hold values from -6 to 6
- timesteps: int32 [32], P('batch'), may hold values from 0 to 1999
- src_len: int32 [32], P('batch'), may hold values from 64 to 256, as said below
- seq_len: int32 [32], P('batch'), may hold values from 128 to 512, as said below
- key_keep: int32 [32, 2, 256], P('batch'), may hold values 0 or 1
- query_weight: bfloat16 [768, 768], replicated, may hold values from -0.21875 to 0.21875
- query_bias: float32 [768], replicated, may hold values from -3 to 3
- key_weight: bfloat16 [768, 768], replicated, may hold values from -0.21875 to 0.21875
- value_weight: bfloat16 [768, 768], replicated, may hold values from -0.21875 to 0.21875
- value_bias: float32 [768], replicated, may hold values from -3 to 3
- output_weight: bfloat16 [768, 768], replicated, may hold values from -6 to 6
- output_bias: float32 [768], replicated, may hold values from -3 to 3
- first_gain: float32 [768], replicated, may hold values from 0.5 to 1.5
- first_shift: float32 [768], replicated, may hold values from -2 to 2
- expand_weight: bfloat16 [768, 3072], replicated, may hold values from -0.21875 to 0.21875
- expand_bias: float32 [3072], replicated, may hold values from -3 to 3
- reduce_weight: bfloat16 [3072, 768], replicated, may hold values from -0.109375 to 0.109375
- reduce_bias: float32 [768], replicated, may hold values from -3 to 3
- second_gain: float32 [768], replicated, may hold values from 0.5 to 1.5
- second_shift: float32 [768], replicated, may hold values from -2 to 2
- time_inner: bfloat16 [128, 512], replicated, may hold values from -0.5 to 0.5
- time_inner_bias: float32 [512], replicated, may hold values from -3 to 3
- time_outer: bfloat16 [512, 768], replicated, may hold values from -0.25 to 0.25
- time_outer_bias: float32 [768], replicated, may hold values from -3 to 3
Outputs:
- output: bfloat16 [32, 2, 256, 768], P('batch', 'seq')
- input_grad: bfloat16 [32, 2, 256, 768], P('batch', 'seq')
- grad_query_weight: float32 [768, 768], replicated
- grad_query_bias: float32 [768], replicated
- grad_key_weight: float32 [768, 768], replicated
- grad_value_weight: float32 [768, 768], replicated
- grad_value_bias: float32 [768], replicated
- grad_output_weight: float32 [768, 768], replicated
- grad_output_bias: float32 [768], replicated
- grad_first_gain: float32 [768], replicated
- grad_first_shift: float32 [768], replicated
- grad_expand_weight: float32 [768, 3072], P(None, ('seq', 'batch'))
- grad_expand_bias: float32 [3072], replicated
- grad_reduce_weight: float32 [3072, 768], P(('seq', 'batch'))
- grad_reduce_bias: float32 [768], replicated
- grad_second_gain: float32 [768], replicated
- grad_second_shift: float32 [768], replicated
- grad_time_inner: float32 [128, 512], replicated
- grad_time_inner_bias: float32 [512], replicated
- grad_time_outer: float32 [512, 768], replicated
- grad_time_outer_bias: float32 [768], replicated
Inputs may be any that keep to these rules, and one draw needn't show every extreme that they name: Some sequence has src_len = 256 and another src_len = 64. seq_len - src_len lies in 64 to 256; some sequence has both parts 256 long, another both 256 // 4.
All inputs are finite; a program needn't handle non-finite values. No bound on the sum of `key_keep` on one device may be relied on, other than what follows from the above.
Results may differ from a plain program's by a relative error of at most 0.018.
The roundings to bfloat16 on the way count: a program that leaves them out, or rounds other values in their place, can miss the bound.
Values may be sent and summed in bfloat16 or wider, within the bound.
No kernel may reach another device: no remote copies, remote signals or barrier semaphores. Data moves between devices by JAX's collectives and lax.ppermute only.
A program may use at most 192 MiB of HBM per device.

v0:
```python
import functools
import math

import jax
import jax.numpy as jnp
from jax import lax
from jax.experimental import pallas as pl
from jax.experimental.pallas import tpu as pltpu
from jax.sharding import PartitionSpec as P

D = 768
HEADS = 12
HEAD_DIM = 64
FF = 3072
TDIM = 128
TFF = 512
CAP = 256
ROWS = 2 * CAP

f32 = jnp.float32
bf16 = jnp.bfloat16
highest = lax.Precision.HIGHEST
norm_epsilon = 1e-12
masked_score = -1000000000.0
root_half = 0.7071067811865476
density_scale = 0.3989422804014327


core, near, side = ("c", 0), ("x", 0), ("y", 0)


def swapped(value, stage):
    axis, bit = stage
    return lax.ppermute(value, axis, [(i, i ^ (1 << bit)) for i in range(lax.axis_size(axis))])


def own_bit(stage):
    axis, bit = stage
    return (lax.axis_index(axis) >> bit) & 1


def stage_lists():
    bits = lax.axis_size("z").bit_length() - 1
    far = [("z", k) for k in range(bits)]
    return [side] + far[::-1] + [near, core], far


def added(kept, received):
    return lax.reduce_precision(kept.astype(f32) + received.astype(f32), 8, 7).astype(bf16)


def halves(buffer, labels, stage):
    at = labels.index(stage)
    bit = own_bit(stage)
    kept = lax.dynamic_index_in_dim(buffer, bit, axis=at, keepdims=False)
    sent = lax.dynamic_index_in_dim(buffer, 1 - bit, axis=at, keepdims=False)
    return kept, sent, labels[:at] + labels[at + 1 :]


def exchange(buffer, labels, stage, riders=None):
    kept, sent, labels = halves(buffer, labels, stage)
    rows = sent.reshape(-1, D)
    if riders is None:
        return added(kept, swapped(rows, stage).reshape(kept.shape)), labels, None
    received = swapped(jnp.concatenate([rows, riders], axis=0), stage)
    return (
        added(kept, received[: rows.shape[0]].reshape(kept.shape)),
        labels,
        added(riders, received[rows.shape[0] :]),
    )


def scattered_sum(shares, riders=None):
    slow_first, far = stage_lists()
    rows = shares.shape[1]
    buffer = shares.reshape((2,) * len(slow_first) + (rows, D))
    buffer, labels, riders = exchange(buffer, slow_first, core, riders)
    cut = rows // 2
    first, first_labels, riders = exchange(buffer[..., :cut, :], labels, near, riders)
    second, second_labels, _ = exchange(buffer[..., cut:, :], labels, side)
    first, first_labels, riders = exchange(first, first_labels, side, riders)
    second, second_labels, _ = exchange(second, second_labels, near)
    buffer = jnp.concatenate([first, second], axis=-2)
    labels = first_labels
    for stage in far:
        buffer, labels, riders = exchange(buffer, labels, stage, riders)
    return buffer, riders


def gathered(share):
    slow_first, far = stage_lists()
    order = [core, near, side] + far
    buffer = share[None]
    done = []
    for stage in reversed(order):
        buffer = jnp.concatenate([buffer, swapped(buffer, stage)], axis=0)
        done.append(stage)
    bits = len(order)
    buffer = buffer.reshape((2,) * bits + share.shape)
    current = list(reversed(done))
    return jnp.transpose(buffer, [current.index(stage) for stage in slow_first] + [bits, bits + 1]).reshape(
        (1 << bits,) + share.shape
    )


def matmul(left, right):
    return jnp.dot(left, right, preferred_element_type=f32)


def column_sum(values):
    return jnp.sum(values.astype(f32), axis=0)


def dot(left, right, dims):
    return lax.dot_general(left, right, (((dims[0],), (dims[1],)), ((), ())), preferred_element_type=f32)


def nn(left, right):
    return dot(left, right, (1, 0))


def nt(left, right):
    return dot(left, right, (1, 1))


def tn(left, right):
    return dot(left, right, (0, 0))


def whole(*shape):
    return pl.BlockSpec(shape, lambda *at: (0,) * len(shape))


def vector(size):
    return pl.BlockSpec((size,), lambda *at: (0,))


def vector_tile(width):
    return pl.BlockSpec((width,), lambda j, *at: (j,))


def row(ref):
    return ref[...].reshape(1, -1)


def column_tile(rows, width):
    return pl.BlockSpec((rows, width), lambda j, *at: (0, j))


def row_tile(height, width):
    return pl.BlockSpec((height, width), lambda j, *at: (j, 0))


def run(body, grid, operands, in_specs, outs, out_specs, flops, scratch=(), scalars=(), after=(), aliases=None):
    shapes = [jax.ShapeDtypeStruct(shape, dtype) for shape, dtype in outs]
    sizes = [x.size * x.dtype.itemsize for x in list(operands) + shapes]
    used = len(scalars) + len(operands)

    def wrapped(*refs):
        body(*refs[:used], *refs[used + len(after) :])

    return pl.pallas_call(
        wrapped,
        grid_spec=pltpu.PrefetchScalarGridSpec(
            num_scalar_prefetch=len(scalars),
            grid=grid,
            in_specs=in_specs + [pl.BlockSpec(memory_space=pl.ANY)] * len(after),
            out_specs=out_specs,
            scratch_shapes=scratch,
        ),
        out_shape=shapes,
        input_output_aliases=aliases or {},
        compiler_params=pltpu.CompilerParams(vmem_limit_bytes=63 << 20),
        cost_estimate=pl.CostEstimate(flops=int(flops), bytes_accessed=sum(sizes), transcendentals=0),
    )(*scalars, *operands, *after)


def nothing(*refs):
    pass


def tie(values, after):
    anywhere = pl.BlockSpec(memory_space=pl.ANY)
    return pl.pallas_call(
        nothing,
        in_specs=[anywhere] * (len(values) + len(after)),
        out_specs=[anywhere] * len(values),
        out_shape=[jax.ShapeDtypeStruct(value.shape, value.dtype) for value in values],
        input_output_aliases={k: k for k in range(len(values))},
    )(*values, *after)


def normalized(values):
    center = values - jnp.mean(values, axis=-1, keepdims=True)
    spread = jnp.mean(center * center, axis=-1, keepdims=True)
    inverse = lax.rsqrt(spread + norm_epsilon)
    return center * inverse, inverse


def norm_backward(upstream, normed, inverse):
    first_mean = jnp.mean(upstream, axis=-1, keepdims=True)
    second_mean = jnp.mean(upstream * normed, axis=-1, keepdims=True)
    return inverse * (upstream - first_mean - normed * second_mean)


def row_sum(values):
    return jnp.sum(values, axis=0, keepdims=True)


def prepare_body(bits, stamps, src_len, seq_len, flags, inner, inner_bias, outer, outer_bias, *outs):
    features, inner_sum, middle, stamp, allowed, valid, masked = outs
    y = bits[2]
    lane = lax.broadcasted_iota(jnp.int32, (1, TDIM), 1)
    half = TDIM // 2
    frequency = jnp.exp(-math.log(10000.0) * lax.rem(lane, half).astype(f32) / half)
    angles = jnp.broadcast_to(stamps[y].astype(f32), (1, TDIM)) * frequency
    waves = jnp.where(lane < half, jnp.cos(angles), jnp.sin(angles))
    features[...] = waves
    total = jnp.dot(waves, inner[...].astype(f32), precision=highest) + row(inner_bias)
    inner_sum[...] = total
    gated = total * (1.0 / (1.0 + jnp.exp(-total)))
    middle[...] = gated
    stamp[...] = jnp.dot(gated, outer[...].astype(f32), precision=highest) + row(outer_bias)
    source, target = src_len[y], seq_len[y] - src_len[y]
    slots = lax.broadcasted_iota(jnp.int32, (CAP, 1), 0)
    lengths = jnp.where(y == 0, source, target), jnp.where(y == 0, target, source)
    for at, (length, stream) in enumerate(zip(lengths, (y, 1 - y))):
        inside = jnp.where(slots < length, 1.0, 0.0)
        kept = jnp.where(flags[y, pl.ds(stream, 1)] == 1, 1.0, 0.0)
        kept = jnp.broadcast_to(kept, (8, CAP)).T[:, :1]
        here = slice(at * CAP, (at + 1) * CAP)
        valid[here] = inside
        allowed[here] = inside * kept
        masked[here] = (1.0 - inside * kept) * masked_score


def prepare(bits, stamps, src_len, seq_len, flags, inner, inner_bias, outer, outer_bias):
    return run(
        prepare_body,
        (1,),
        (flags, inner, inner_bias, outer, outer_bias),
        [whole(2, 2, CAP), whole(TDIM, TFF), vector(TFF), whole(TFF, D), vector(D)],
        [((1, size), f32) for size in (TDIM, TFF, TFF, D)] + [((ROWS, 1), f32)] * 3,
        [whole(1, size) for size in (TDIM, TFF, TFF, D)] + [whole(ROWS, 1)] * 3,
        0,
        scalars=(bits, stamps, src_len, seq_len),
    )


def project_body(rows, stamp, keep, qw, qb, kw, vw, vb, q, k, v, low_out):
    low = (rows[...].astype(f32) + stamp[...]).astype(bf16)
    low_out[...] = low
    q[...] = ((nn(low, qw[...]) + row(qb)).astype(bf16).astype(f32) * 0.125).astype(bf16)
    k[...] = (nn(low, kw[...]) * keep[...]).astype(bf16)
    v[...] = (nn(low, vw[...]) + row(vb)).astype(bf16)


def project(rows, half, stamp, keep, qw, qb, kw, vw, vb):
    tile = 256
    return run(
        project_body,
        (D // tile,),
        (rows, stamp, keep, qw, qb, kw, vw, vb),
        [whole(CAP, D), whole(1, D), pl.BlockSpec((CAP, 1), lambda *at: (half, 0))]
        + [column_tile(D, tile), vector_tile(tile), column_tile(D, tile), column_tile(D, tile), vector_tile(tile)],
        [((CAP, D), bf16)] * 4,
        [column_tile(CAP, tile)] * 3 + [whole(CAP, D)],
        6 * CAP * D * D,
    )


def lanes_of(shape):
    return lax.broadcasted_iota(jnp.int32, shape, 1)


def both(own, far):
    return jnp.concatenate([own[...], far[...]], axis=0)


def attend_body(qo, qf, ko, kf, vo, vf, lo, lf, masked, attended, for_core, probs):
    q, k, v = both(qo, qf), both(ko, kf), both(vo, vf)
    lane = lanes_of(q.shape)
    flag = jnp.broadcast_to(masked[...], q.shape).astype(bf16)
    v_turned = v.T
    pieces = []
    for head in range(2):
        mine = (lane // HEAD_DIM) == head
        spare = lane == (1 - head) * HEAD_DIM
        k_head = jnp.where(mine, k, jnp.where(spare, flag, 0))
        q_head = jnp.where(mine, q, jnp.where(spare, 1, 0).astype(bf16))
        scores = nt(k_head, q_head)
        top = jnp.max(scores, axis=0, keepdims=True)
        exponent = jnp.exp(scores - top)
        inverse = 1.0 / jnp.sum(exponent, axis=0, keepdims=True)
        low = (exponent * inverse).astype(bf16)
        probs[head] = low
        pieces.append(nn(v_turned[head * HEAD_DIM : (head + 1) * HEAD_DIM], low))
    low = jnp.concatenate(pieces, axis=0).T.astype(bf16)
    attended[...] = low
    for_core[0], for_core[1] = both(lo, lf), low


def attend(q, k, v, low, masked):
    pair = 2 * HEAD_DIM
    return run(
        attend_body,
        (D // pair,),
        (*q, *k, *v, *low, masked),
        [column_tile(CAP, pair)] * 8 + [whole(ROWS, 1)],
        [((ROWS, D), bf16), ((2, ROWS, D), bf16), ((HEADS, ROWS, ROWS), bf16)],
        [column_tile(ROWS, pair), pl.BlockSpec((2, ROWS, pair), lambda j: (0, 0, j))]
        + [pl.BlockSpec((2, ROWS, ROWS), lambda j: (j, 0, 0))],
        4 * HEADS * ROWS * ROWS * 256,
    )


SHARE = 96
COLOUR = 48


half_tile = pl.BlockSpec((ROWS, D // 2), lambda j, *at: (0, j))


FOR_CORE = (ROWS, FF + 2 * D)


def by_core(values):
    return [
        jnp.concatenate([values[:, at : at + SHARE] for at in range(start, D, 2 * SHARE)], axis=1) for start in (0, SHARE)
    ]


def store_by_core(bits, values, other, own):
    zero, one = by_core(values)

    @pl.when(bits[0] == 0)
    def _():
        own[...], other[...] = zero, one

    @pl.when(bits[0] == 1)
    def _():
        own[...], other[...] = one, zero


def feed_forward_body(
    bits, attended, own, far, stamp, ow, ob, gain, shift, ew, eb, rw, rb, gain2, shift2, valid, cot_own, cot_far,
    output, for_core, activated_own, slope, mixed_low, normed, inverse, d_second, d_reduced, sums, mixed, total,
    activated,
):
    step = pl.program_id(0)

    @pl.when(step == 0)
    def _():
        hidden = both(own, far).astype(f32) + stamp[...]
        n1, inv = normalized(hidden + nn(attended[...], ow[...]) + row(ob))
        value = n1 * row(gain) + row(shift)
        normed[...] = n1
        inverse[...] = inv
        mixed[...] = value
        mixed_low[...] = value.astype(bf16)
        total[...] = value + row(rb)

    added_up = None
    bias = eb[pl.ds(pl.multiple_of(step * D, D), D)].reshape(1, -1)
    for part in range(D // SUB):
        cut = slice(part * SUB, (part + 1) * SUB)
        expanded = nn(mixed_low[...], ew[:, cut]) + bias[:, cut]
        chance = 0.5 * (1.0 + lax.erf(expanded * root_half))
        slope[:, cut] = chance + expanded * jnp.exp(-0.5 * expanded * expanded) * density_scale
        low = (expanded * chance).astype(bf16)
        activated[:, cut] = low
        product = nn(low, rw[cut, :])
        added_up = product if added_up is None else added_up + product
    total[...] += added_up
    here = pl.ds(pl.multiple_of(step * (D // 2), D // 2), D // 2)
    store_by_core(bits, activated[...], for_core.at[:, here], activated_own)

    @pl.when(step == pl.num_programs(0) - 1)
    def _():
        n2, inv = normalized(total[...])
        weight = valid[...]
        output[...] = ((n2 * row(gain2) + row(shift2)) * weight).astype(bf16)
        d_out = both(cot_own, cot_far).astype(f32) * weight
        back = norm_backward(d_out * row(gain2), n2, inv)
        low = back.astype(bf16)
        d_second[...] = back
        d_reduced[...] = low
        for_core[:, 2 * D : 3 * D] = low
        for_core[:, 3 * D :] = mixed_low[...]
        sums[...] = jnp.concatenate(
            [jnp.zeros((5, D), f32), row_sum(low.astype(f32)), row_sum(d_out * n2), row_sum(d_out)], axis=0
        )


SUB = 256


def feed_forward(
    bits, attended, own, far, stamp, ow, ob, gain, shift, ew, eb, rw, rb, gain2, shift2, valid, cot_own, cot_far
):
    line, square, half = vector(D), whole(ROWS, D), whole(CAP, D)
    return run(
        feed_forward_body,
        (FF // D,),
        (attended, own, far, stamp, ow, ob, gain, shift, ew, eb, rw, rb, gain2, shift2, valid, cot_own, cot_far),
        [square, half, half, whole(1, D), whole(D, D), line, line, line, column_tile(D, D), vector(FF), row_tile(D, D)]
        + [line, line, line, whole(ROWS, 1), half, half],
        [
            ((ROWS, D), bf16),
            (FOR_CORE, bf16),
            ((ROWS, FF // 2), bf16),
            ((ROWS, FF), f32),
            ((ROWS, D), bf16),
            ((ROWS, D), f32),
            ((ROWS, 1), f32),
            ((ROWS, D), f32),
            ((ROWS, D), bf16),
            ((8, D), f32),
        ],
        [square, whole(ROWS, 4 * D), half_tile, column_tile(ROWS, D), square, square, whole(ROWS, 1), square, square, whole(8, D)],
        2 * ROWS * D * (D + 2 * FF),
        scratch=[pltpu.VMEM((ROWS, D), f32)] * 2 + [pltpu.VMEM((ROWS, D), bf16)],
        scalars=(bits,),
    )


def hidden_grad_body(bits, activated, d_reduced, d_expanded, mixed, activated_got, reduced_got, mixed_got, expanded_got, kept, sent):
    step = pl.program_id(0)
    tile = step % 2

    def store(kind, grad):
        low = grad.astype(bf16)
        for at in range(8):
            x, z = at % 2, at // 2
            here = jnp.where(bits[0] == 0, tile, x) * 4 + (z % 2 * 2 + z // 2)
            block = low[at * SHARE : (at + 1) * SHARE]
            mine = jnp.where(bits[0] == 0, x, tile) == bits[5]

            @pl.when(mine)
            def _():
                kept[here, kind] = block

            @pl.when(jnp.logical_not(mine))
            def _():
                sent[here, kind] = block

    @pl.when(step < 2)
    def _():
        store(0, tn(activated[...], d_reduced[...]) + tn(activated_got[...], reduced_got[...]))

    @pl.when(step >= 2)
    def _():
        store(1, tn(d_expanded[...], mixed[...]) + tn(expanded_got[...], mixed_got[...]))


def hidden_grad(bits, activated, d_reduced, d_expanded, mixed, got, after):
    first = lambda start: pl.BlockSpec((ROWS, D), lambda j, bits: (0, start + jnp.minimum(j, 1)))
    second = lambda start: pl.BlockSpec((ROWS, D), lambda j, bits: (0, start + jnp.maximum(j - 2, 0)))
    square = lambda at: pl.BlockSpec((ROWS, D), lambda j, bits: (0, at))
    return run(
        hidden_grad_body,
        (4,),
        (activated, d_reduced, d_expanded, mixed, got, got, got, got),
        [first(0), square(0), second(0), square(0), first(0), square(2), square(3), second(4)],
        [((8, 2, SHARE, D), bf16)] * 2,
        [whole(8, 2, SHARE, D)] * 2,
        4 * ROWS * D * FF,
        scalars=(bits,),
        after=after,
    )


def expand_back_body(
    bits, d_reduced, rw, slope, ew, d_second, normed, inverse, gain, for_core,
    expanded_other, expanded_own, bias, d_first, d_branch, sums, total,
):
    step = pl.program_id(0)
    d_expanded = (nt(d_reduced[...], rw[...]) * slope[...]).astype(bf16)
    bias[0] = row_sum(d_expanded.astype(f32))
    store_by_core(bits, d_expanded, expanded_other, expanded_own)
    product = nt(d_expanded, ew[...])

    @pl.when(step == 0)
    def _():
        total[...] = d_second[...] + product

    @pl.when(step > 0)
    def _():
        total[...] += product

    @pl.when(step == pl.num_programs(0) - 1)
    def _():
        d_mixed = total[...]
        n1 = normed[...]
        back = norm_backward(d_mixed * row(gain), n1, inverse[...])
        low = back.astype(bf16)
        d_first[...] = back
        d_branch[...] = low
        sums[...] = jnp.concatenate(
            [jnp.zeros((2, D), f32), row_sum(low.astype(f32)), row_sum(d_mixed * n1), row_sum(d_mixed), jnp.zeros((3, D), f32)],
            axis=0,
        )


def expand_back(bits, d_reduced, rw, slope, ew, d_second, normed, inverse, gain, for_core, after):
    steps = FF // D
    square = whole(ROWS, D)
    return run(
        expand_back_body,
        (steps,),
        (d_reduced, rw, slope, ew, d_second, normed, inverse, gain, for_core),
        [square, row_tile(D, D), column_tile(ROWS, D), column_tile(D, D), square, square, whole(ROWS, 1), vector(D)]
        + [pl.BlockSpec(memory_space=pl.ANY)],
        [(FOR_CORE, bf16), ((ROWS, FF // 2), bf16)] + [((steps, 1, D), f32), ((ROWS, D), f32), ((ROWS, D), bf16), ((8, D), f32)],
        [pl.BlockSpec((ROWS, D // 2), lambda j, *at: (0, 8 + j)), half_tile]
        + [pl.BlockSpec((1, 1, D), lambda j, *at: (j, 0, 0)), square, square, whole(8, D)],
        4 * ROWS * D * FF,
        scratch=[pltpu.VMEM((ROWS, D), f32)],
        aliases={9: 0},
        scalars=(bits,),
        after=after,
    )


def attend_back_body(bits, d_branch, branch, ow, probs, qo, qf, ko, kf, vo, vf, keep, grads, kept, sent, sums):
    q, k, v = both(qo, qf), both(ko, kf), both(vo, vf)
    lane = lanes_of(q.shape)
    low_half = lane < HEAD_DIM
    upstream = nt(d_branch[...], ow[...]).astype(bf16)
    k_turned = k.T
    d_q, d_k, d_v = [], [], []
    for head in range(2):
        rows = slice(head * HEAD_DIM, (head + 1) * HEAD_DIM)
        mine = low_half if head == 0 else jnp.logical_not(low_half)
        low = probs[head]
        wide = low.astype(f32)
        weighted = wide * nt(jnp.where(mine, v, 0), upstream)
        d_scores = (weighted - wide * row_sum(weighted)).astype(bf16)
        d_v.append(nn(low, upstream))
        d_k.append(nn(d_scores, q))
        d_q.append(nn(k_turned[rows], d_scores))
    q_low = (jnp.concatenate(d_q, axis=0).T * 0.125).astype(bf16)
    v_low = jnp.where(low_half, d_v[0], d_v[1]).astype(bf16)
    k_low = (jnp.where(low_half, d_k[0], d_k[1]) * keep[...]).astype(bf16)
    grads[0], grads[1], grads[2] = q_low, k_low, v_low

    def share(first, second):
        first[0], first[1] = q_low, k_low
        second[0], second[1] = v_low, branch[...]

    @pl.when(bits[0] == 0)
    def _():
        share(kept, sent)

    @pl.when(bits[0] == 1)
    def _():
        share(sent, kept)

    sums[...] = jnp.concatenate(
        [row_sum(q_low.astype(f32)), row_sum(v_low.astype(f32)), jnp.zeros((6, q.shape[1]), f32)], axis=0
    )


def attend_back(bits, d_branch, ow, probs, q, k, v, keep, after):
    pair = 2 * HEAD_DIM
    return run(
        attend_back_body,
        (D // pair,),
        (d_branch, d_branch, ow, probs, *q, *k, *v, keep),
        [whole(ROWS, D), column_tile(ROWS, pair), row_tile(pair, D), pl.BlockSpec((2, ROWS, ROWS), lambda j, *at: (j, 0, 0))]
        + [column_tile(CAP, pair)] * 6
        + [whole(ROWS, 1)],
        [((count, ROWS, D), bf16) for count in (3, 2, 2)] + [((8, D), f32)],
        [pl.BlockSpec((count, ROWS, pair), lambda j, *at: (0, 0, j)) for count in (3, 2, 2)] + [column_tile(8, pair)],
        10 * HEADS * ROWS * ROWS * 256,
        scalars=(bits,),
        after=after,
    )


def pair_grad_body(bits, left, right, left_got, right_got, kept, sent):
    low = (tn(left[0], right[0]) + tn(left_got[0], right_got[0])).astype(bf16)
    zero, one = [low[at * D // 2 : (at + 1) * D // 2].reshape(8, COLOUR, D) for at in range(2)]
    kept[:, 0] = jnp.where(bits[5] == 0, zero, one)
    sent[:, 0] = jnp.where(bits[5] == 0, one, zero)


def pair_grad(bits, left, right, left_got, right_got, after):
    lefts = pl.BlockSpec((1, ROWS, D), lambda j, bits: (j * bits[0], 0, 0))
    rights = pl.BlockSpec((1, ROWS, D), lambda j, bits: (j, 0, 0))
    return run(
        pair_grad_body,
        (2,),
        (left, right, left_got, right_got),
        [lefts, rights] * 2,
        [((8, 2, COLOUR, D), bf16)] * 2,
        [pl.BlockSpec((8, 1, COLOUR, D), lambda j, *at: (0, j, 0, 0))] * 2,
        8 * ROWS * D * D,
        scalars=(bits,),
        after=after,
    )


def input_grad_body(grads, qw, kw, vw, d_first, d_rows, d_time):
    total = d_first[...] + nt(grads[0], qw[...]) + nt(grads[1], kw[...]) + nt(grads[2], vw[...])
    d_rows[...] = total.astype(bf16)
    d_time[...] = row_sum(total)


def input_grad(grads, qw, kw, vw, d_first, after):
    tile = 256
    return run(
        input_grad_body,
        (D // tile,),
        (grads, qw, kw, vw, d_first),
        [whole(3, ROWS, D)] + [row_tile(tile, D)] * 3 + [column_tile(ROWS, tile)],
        [((ROWS, D), bf16), ((1, D), f32)],
        [column_tile(ROWS, tile), column_tile(1, tile)],
        6 * ROWS * D * D,
        after=after,
    )


everywhere = ("y", "z", "x", "c")
low_far, high_far = ("z", 0), ("z", 1)


def crossed(value, first):
    sizes = [lax.axis_size(axis) for axis in everywhere]
    pairs = []
    for at in range(math.prod(sizes)):
        c, x = at % 2, at // 2 % 2
        along_x = (c == 0) == first
        step = 2 * (1 - 2 * x) if along_x else (math.prod(sizes) // 2) * (1 - 2 * (at // (math.prod(sizes) // 2)))
        pairs.append((at, at + step))
    return lax.ppermute(value, everywhere, pairs)


def plus(left, right):
    return (left.astype(f32) + right.astype(f32)).astype(bf16)


def halved(own, got, bit):
    own, got = [value.reshape((2, -1) + value.shape[1:]) for value in (own, got)]
    at = lambda place: [lax.dynamic_index_in_dim(value, place, 0, keepdims=False) for value in (own, got)]
    return plus(*at(bit)), plus(*at(1 - bit))


BLOCK = 32


def block_body(bits, first, second, third, bias, d_time, inner_sum, middle, features, outer, out):
    riders = first[...] + second[...] + third[...]
    total = inner_sum[...]
    gate = 1.0 / (1.0 + jnp.exp(-total))
    d_middle = lax.dot_general(
        d_time[...], outer[...].astype(f32), (((1,), (1,)), ((), ())), precision=highest, preferred_element_type=f32
    )
    d_inner = d_middle * (gate * (1.0 + total * (1.0 - gate)))
    wide = D - TFF
    rows = [jnp.concatenate([d_time[:, at * wide : (at + 1) * wide], middle[...]], axis=1) for at in range(3)]
    rows.append(jnp.concatenate([d_inner, features[...], jnp.zeros((1, wide - TDIM), f32)], axis=1))
    index = lax.broadcasted_iota(jnp.int32, (16, D), 0)
    factors = jnp.zeros((16, D), f32)
    for at, values in enumerate(rows):
        factors = jnp.where(index == 4 * (bits[3] + 2 * bits[4]) + at, values, factors)
    biases = jnp.zeros((8, D), f32)
    index = lax.broadcasted_iota(jnp.int32, (8, D), 0)
    for at in range(4):
        biases = jnp.where(index == at, bias[at], biases)
    out[...] = jnp.concatenate([riders, biases, factors], axis=0).astype(bf16)


def block_rows(bits, *operands):
    return run(
        block_body,
        (1,),
        operands,
        [whole(*operand.shape) for operand in operands],
        [((BLOCK, D), bf16)],
        [whole(BLOCK, D)],
        0,
        scalars=(bits,),
    )[0]


def sum_rows(own, got):
    return lax.reduce_precision(own.astype(f32) + got.astype(f32), 8, 7).astype(bf16)


def longer(data, block, send, join):
    got = send(jnp.concatenate([data, block]))
    size = data.shape[0]
    data, got = jnp.concatenate([data, got[:size]]), got[size:]
    if not join:
        return data, sum_rows(block, got)
    return data, jnp.concatenate([sum_rows(block[:16], got[:16]), block[16:], got[16:]])


def unpack_body(bits, own, got, *refs):
    outs = refs[-4:]
    for at in range(8):
        here, there = (bits[6] % 8) ^ at, (bits[7] % 8) ^ at
        for matrix in range(2):
            rows = slice(at * SHARE + matrix * COLOUR, at * SHARE + (matrix + 1) * COLOUR)
            mine, other = own[rows].astype(f32), got[rows].astype(f32)
            outs[matrix][here] = jnp.where(bits[0] == 0, mine, other)
            outs[2 + matrix][there] = jnp.where(bits[0] == 0, other, mine)


def unpack(bits, own, got, turn, outs):
    shape = (16, COLOUR, D)
    blocks = [pl.BlockSpec((8, COLOUR, D), lambda j, bits, at=at: ((bits[at] // 8) ^ turn, 0, 0)) for at in (6, 7)]
    return run(
        unpack_body,
        (1,),
        (own, got, *outs),
        [whole(D, D)] * 2 + [pl.BlockSpec(memory_space=pl.ANY)] * len(outs),
        [(shape, f32)] * 4,
        [blocks[0]] * 2 + [blocks[1]] * 2,
        0,
        scalars=(bits,),
        aliases={3 + k: k for k in range(len(outs))},
    )


def finish_body(own, turned, own_far, turned_far, *outs):
    blocks = [ref[...].astype(f32) for ref in (own, turned, own_far, turned_far)]
    sums = (blocks[0][:16] + blocks[1][:16]) + (blocks[2][:16] + blocks[3][:16])
    for at in range(8):
        outs[at][...] = sums[at]
    for at in range(4):
        outs[8][at] = sums[8 + at : 9 + at]
    factors = jnp.concatenate([block[16:] for block in blocks], axis=0)
    index = lax.broadcasted_iota(jnp.int32, factors.shape, 0) % 4
    wide = D - TFF
    inner, inner_bias, outer, outer_bias = outs[9:]
    for at in range(3):
        rows = jnp.where(index == at, factors, 0.0)
        d_time = rows[:, :wide]
        here = slice(at * wide, (at + 1) * wide)
        outer[:, here] = tn(rows[:, wide:].astype(bf16), d_time.astype(bf16))
        outer_bias[here] = jnp.sum(d_time, axis=0)
    rows = jnp.where(index == 3, factors, 0.0)
    d_inner = rows[:, :TFF]
    inner[...] = tn(rows[:, TFF : TFF + TDIM].astype(bf16), d_inner.astype(bf16))
    inner_bias[...] = jnp.sum(d_inner, axis=0)


def finish(*messages):
    last = pl.BlockSpec((48, D), lambda j, *at: (D // 48, 0))
    shapes = [(D,)] * 8 + [(4, 1, D), (TDIM, TFF), (TFF,), (TFF, D), (D,)]
    return run(finish_body, (1,), messages, [last] * 4, [(shape, f32) for shape in shapes], [whole(*shape) for shape in shapes], 0)


def plain_rows(first_class, second_class):
    zero = jnp.concatenate(first_class).reshape(2, 2, 2, 2, SHARE, D)
    one = jnp.concatenate(second_class).reshape(2, 2, 2, 2, SHARE, D)
    classes = jnp.stack([jnp.transpose(zero, (1, 3, 2, 0, 4, 5)), jnp.transpose(one, (0, 3, 2, 1, 4, 5))], axis=4)
    return classes.reshape(FF, D)


def everyones(sums, bias, d_time, inner_sum, middle, features, outer):
    gate = jax.nn.sigmoid(inner_sum)
    d_inner = jnp.dot(d_time, outer.astype(f32).T, precision=highest) * (gate * (1.0 + inner_sum * (1.0 - gate)))
    riders = jnp.concatenate([sums, bias.reshape(4, D), jnp.zeros((4, D), f32)])
    factors = jnp.concatenate([d_time, d_inner, middle, features], axis=1)
    for stage in stage_lists()[0]:
        riders = riders + swapped(riders, stage)
        factors = jnp.concatenate([factors, swapped(factors, stage)])
    cuts = (0, D, D + TFF, D + 2 * TFF, D + 2 * TFF + TDIM)
    d_time, d_inner, middle, features = [factors[:, a:b] for a, b in zip(cuts, cuts[1:])]
    inner, outer = matmul(features.T, d_inner), matmul(middle.T, d_time)
    return list(riders[:8]), riders[8:12], inner, column_sum(d_inner), outer, column_sum(d_time)


def on_device(
    layer_input,
    cotangent,
    timesteps,
    src_len,
    seq_len,
    key_keep,
    query_weight,
    query_bias,
    key_weight,
    value_weight,
    value_bias,
    output_weight,
    output_bias,
    first_gain,
    first_shift,
    expand_weight,
    expand_bias,
    reduce_weight,
    reduce_bias,
    second_gain,
    second_shift,
    time_inner,
    time_inner_bias,
    time_outer,
    time_outer_bias,
):
    stream = lax.axis_index("y")
    sizes = [lax.axis_size(axis) for axis in ("y", "z", "x", "c")]
    devices = math.prod(sizes)
    tuned = sizes == [2, 4, 2, 2]
    c, x, z = lax.axis_index("c") if tuned else 0, lax.axis_index("x"), lax.axis_index("z")
    first, second = jnp.where(c == 0, x, stream), jnp.where(c == 0, stream, x)
    wanted = first if tuned else 0
    places = [one * 8 + two * 4 + (z & 1) * 2 + (z >> 1) for one, two in ((x, stream), (stream, x))]
    bits = jnp.stack([c, x, stream, z & 1, z >> 1, wanted, *places]).astype(jnp.int32)

    def whole_sequence(rows):
        own = lax.dynamic_index_in_dim(rows[:, 0], stream, axis=0, keepdims=False)
        other = lax.dynamic_index_in_dim(rows[:, 0], 1 - stream, axis=0, keepdims=False)
        return own, swapped(other, side)

    def both_sequences(rows, far):
        own = rows[:CAP]
        return jnp.where(stream == 0, jnp.stack([own, far]), jnp.stack([far, own]))[:, None]

    own, far = whole_sequence(layer_input)
    cotangent, far = lax.optimization_barrier((cotangent, far))
    cot_own, cot_far = whole_sequence(cotangent)
    features, inner_sum, middle, stamp, allowed, valid, masked = prepare(
        bits, timesteps, src_len, seq_len, key_keep, time_inner, time_inner_bias, time_outer, time_outer_bias
    )
    weights = (query_weight, query_bias, key_weight, value_weight, value_bias)
    *first_rows, own_low = project(own, 0, stamp, allowed, *weights)
    (far,) = tie([far], first_rows[:1])
    *other_rows, far_low = project(far, 1, stamp, allowed, *weights)
    q, k, v = zip(first_rows, other_rows)
    low = (own_low, far_low)
    attended, lefts, probs = attend(q, k, v, low, masked)
    (lefts,) = tie([lefts], [cot_far])
    output, for_core, activated, slope, mixed_low, normed, inverse, d_second, d_reduced, second_sums = feed_forward(
        bits,
        attended,
        own,
        far,
        stamp,
        output_weight,
        output_bias,
        first_gain,
        first_shift,
        expand_weight,
        expand_bias,
        reduce_weight,
        reduce_bias,
        second_gain,
        second_shift,
        valid,
        cot_own,
        cot_far,
    )
    lefts_got = swapped(lefts, core)
    (output,) = tie([output], [lefts_got])
    output_got = swapped(output[CAP:], side)
    for_core, d_expanded, expand_bias_grad, d_first, d_branch, first_sums = expand_back(
        bits,
        d_reduced,
        reduce_weight,
        slope,
        expand_weight,
        d_second,
        normed,
        inverse,
        first_gain,
        for_core,
        [lefts_got],
    )
    (for_core,) = tie([for_core], [output_got])
    grads, kept, sent, attend_sums = attend_back(bits, d_branch, output_weight, probs, q, k, v, allowed, [for_core])
    block_parts = (inner_sum, middle, features, time_outer)
    if tuned:
        (hidden_got,) = tie([swapped(for_core, core)], [grads])
        (sent,) = tie([sent], [hidden_got])
        small, small_sent = pair_grad(bits, lefts, kept, lefts_got, swapped(sent, core), [])
        small_got = crossed(small_sent, True)
        hidden, hidden_sent = hidden_grad(bits, activated, d_reduced, d_expanded, mixed_low, hidden_got, [small])
        (small_got,) = tie([small_got], [hidden])
        small, small_sent = halved(small, small_got, second)
        small_got = crossed(small_sent, False)
        d_rows, d_time = input_grad(grads, query_weight, key_weight, value_weight, d_first, [small_sent])
        (small_got,) = tie([small_got], [d_rows])
        small, small_sent = halved(small, small_got, z & 1)
        small_got = swapped(small_sent, low_far)
        hidden_sent, d_rows, d_time = tie([hidden_sent, d_rows, d_time], [small_sent])
        hidden_got = crossed(hidden_sent, True)
        input_got = swapped(d_rows[CAP:], side)
        block = block_rows(bits, attend_sums, first_sums, second_sums, expand_bias_grad, d_time, *block_parts)
        small, small_sent = halved(small, small_got, z >> 1)
        share = plus(small, swapped(small_sent, high_far)).reshape(SHARE, D)
        data, block = longer(share, block, lambda value: swapped(value, high_far), False)
        data, block = longer(data, block, lambda value: swapped(value, low_far), False)
        hidden, hidden_sent = halved(hidden, hidden_got, second)
        hidden_got = crossed(hidden_sent, False)
        (data,) = tie([data], [hidden_sent])
        data, block = longer(data, block, lambda value: crossed(value, False), True)
        hidden, hidden_sent = halved(hidden, hidden_got, z & 1)
        hidden_got = swapped(hidden_sent, low_far)
        (data,) = tie([data], [hidden_sent])
        message = jnp.concatenate([data, block])
        turned = crossed(message, True)
        message_far = swapped(message, core)
        outs = unpack(bits, message, message_far, 0, ())
        hidden, hidden_sent = halved(hidden, hidden_got, z >> 1)
        hidden_got = swapped(hidden_sent, high_far)
        turned_far = swapped(turned, core)
        outs = unpack(bits, turned, turned_far, 1, outs)
        *vectors, expand_bias_grad, inner, inner_bias, outer, outer_bias = finish(message, turned, message_far, turned_far)
        grad_query, grad_key, grad_value, grad_output = [out.reshape(D, D) for out in outs]
        shares = (hidden.astype(f32) + hidden_got.astype(f32))[0]
        reduce_share, expand_share = shares[0], shares[1]
        input_grad_rows = both_sequences(d_rows, input_got)
    else:
        d_rows, d_time = input_grad(grads, query_weight, key_weight, value_weight, d_first, ())
        reduce_parts, expand_parts, pairs = [], [], []
        nothing_got = jnp.zeros_like(for_core)
        for core_bit, pair, left, right in (
            (0, kept, activated, d_expanded),
            (1, sent, for_core[:, : 2 * D], for_core[:, 4 * D :]),
        ):
            as_core = bits.at[0].set(core_bit)
            hidden = hidden_grad(as_core, left, d_reduced, right, mixed_low, nothing_got, ())
            reduce_parts.append([part[:, 0] for part in hidden])
            expand_parts.append([part[:, 1] for part in hidden])
            grad = pair_grad(as_core, lefts, pair, lefts, jnp.zeros_like(pair), ())
            pairs.append(jnp.moveaxis(jnp.concatenate(grad), 1, 0).reshape(2, D, D))
        per = FF // devices
        reduce_share, _ = scattered_sum(plain_rows(*reduce_parts).reshape(devices, per, D))
        expand_share, _ = scattered_sum(plain_rows(*expand_parts).reshape(devices, per, D))
        small_share, _ = scattered_sum(jnp.concatenate(pairs).reshape(devices, per, D))
        me = ((stream * sizes[1] + z) * 2 + x) * 2 + lax.axis_index("c")
        small = gathered(small_share)[jnp.arange(devices) ^ me].astype(f32).reshape(4, D, D)
        grad_query, grad_key, grad_value, grad_output = [small[at] for at in range(4)]
        vectors, expand_bias_grad, inner, inner_bias, outer, outer_bias = everyones(
            attend_sums + first_sums + second_sums, expand_bias_grad, d_time, *block_parts
        )
        input_grad_rows = both_sequences(d_rows, swapped(d_rows[CAP:], side))
    return (
        both_sequences(output, output_got),
        input_grad_rows,
        grad_query,
        vectors[0],
        grad_key,
        grad_value,
        vectors[1],
        grad_output,
        vectors[2],
        vectors[3],
        vectors[4],
        expand_share.astype(f32).T,
        expand_bias_grad.reshape(FF),
        reduce_share.astype(f32),
        vectors[5],
        vectors[6],
        vectors[7],
        inner,
        inner_bias,
        outer,
        outer_bias,
    )


def solution(mesh):
    seq, batch = mesh.devices.shape
    mesh = jax.sharding.Mesh(mesh.devices.reshape(seq, batch // 4, 2, 2), ("y", "z", "x", "c"))
    sequences, everyone = ("z", "x", "c"), ("y", "z", "x", "c")
    rows = P(sequences, "y", None, None)
    in_specs = (rows, rows) + (P(sequences),) * 3 + (P(sequences, None, None),) + (P(),) * 19
    out_specs = (rows, rows) + (P(),) * 9 + (P(None, everyone), P(), P(everyone, None)) + (P(),) * 7
    return jax.shard_map(on_device, mesh=mesh, in_specs=in_specs, out_specs=out_specs, check_vma=False)
```

profile of v0, /device:TPU:0, one launch (start us, length us, event | category | flops | bytes accessed | tf_op | source)
XLA Modules:
  0.0 254.6 jit_solution(8299366612824593376)
XLA Ops:
  6.1 3.7 %shard_map.400 = (f32[1,128]{1,0:T(1,128)}, f32[1,512]{1,0:T(1,128)}, f32[1,512]{1,0:T(1,128)}, f32[1,768]{1,0:T(1,128)}, f32[512,1]{1,0:T(8,128)}, /*index=5*/f32[512,1]{1,0:T(8,128)}, f32[512,1]{1,0:T(8,128)}) custom-call(s32[8]{0:T(128)} %stack.63.refs_0_, s32[2]{0:T(128)} %refs_1_.2, s32[2]{0:T(128)} %refs_2_.3, s32[2]{0:T(128)} %refs_3_.5, ...), custom_call_target="tpu_custom_call" | custom-call | bytes 940544 | tf_op jit(solution)/shard_map/pallas_call | solution.py:162
  9.9 4.8 %collective-permute-done.refs_0_ = bf16[256,768]{1,0:T(8,128)(2,1)S(1)} collective-permute-done((bf16[256,768]{1,0:T(8,128)(2,1)S(1)}, bf16[256,768]{1,0:T(8,128)(2,1)S(1)}, u32[]{:S(2)}, u32[]{:S(2)}) %collective-permute-start) | collective-permute-done | bytes 393248 | tf_op jit(solution)/shard_map/ppermute | solution.py:34
  18.6 4.7 %shard_map.401 = (bf16[256,768]{1,0:T(8,128)(2,1)}, bf16[256,768]{1,0:T(8,128)(2,1)}, bf16[256,768]{1,0:T(8,128)(2,1)}, bf16[256,768]{1,0:T(8,128)(2,1)}) custom-call(bf16[256,768]{1,0:T(8,128)(2,1)} %get-tuple-element.176.refs_0_.refs_2_, f32[1,768]{1,0:T(1,128)} %get-tuple-element.91.refs_1_.refs_4_, f32[512,1]{1,0:T(8,128)} %get-tuple-element.92.refs_2_.refs_11_, ...), custom_call_target="tpu_custom_call" | custom-call | flops 905969664 | bytes 5516288 | tf_op jit(solution)/shard_map/pallas_call | solution.py:162
  23.3 4.9 %shard_map.403 = (bf16[256,768]{1,0:T(8,128)(2,1)}, bf16[256,768]{1,0:T(8,128)(2,1)}, bf16[256,768]{1,0:T(8,128)(2,1)}, bf16[256,768]{1,0:T(8,128)(2,1)}) custom-call(bf16[256,768]{1,0:T(8,128)(2,1)} %shard_map.402.refs_0_.refs_3_, f32[1,768]{1,0:T(1,128)} %get-tuple-element.91.refs_1_.refs_4_, f32[512,1]{1,0:T(8,128)} %get-tuple-element.92.refs_2_.refs_11_, ...), custom_call_target="tpu_custom_call" | custom-call | flops 905969664 | bytes 5516288 | tf_op jit(solution)/shard_map/pallas_call | solution.py:162
  28.2 11.5 %shard_map.404 = (bf16[512,768]{1,0:T(8,128)(2,1)}, bf16[2,512,768]{2,1,0:T(8,128)(2,1)}, bf16[12,512,512]{2,1,0:T(8,128)(2,1)}) custom-call(bf16[256,768]{1,0:T(8,128)(2,1)} %get-tuple-element.93.refs_1_.refs_0_.refs_5_, bf16[256,768]{1,0:T(8,128)(2,1)} %get-tuple-element.95.refs_1_.refs_6_, bf16[256,768]{1,0:T(8,128)(2,1)} %get-tuple-element.96.refs_2_.refs_7_, ...), custom_call_target="tpu_custom_call" | custom-call | flops 3221225472 | bytes 11798528 | tf_op jit(solution)/shard_map/pallas_call | solution.py:162
  40.5 19.1 %shard_map.405 = (bf16[512,768]{1,0:T(8,128)(2,1)}, bf16[512,4608]{1,0:T(8,128)(2,1)}, bf16[512,1536]{1,0:T(8,128)(2,1)}, f32[512,3072]{1,0:T(8,128)}, bf16[512,...) custom-call(s32[8]{0:T(128)} %stack.63.refs_0_, ...), custom_call_target="tpu_custom_call" | custom-call | flops 5435817984 | bytes 31126528 | tf_op jit(solution)/shard_map/pallas_call | solution.py:162
  61.8 16.6 %shard_map.408 = (bf16[512,4608]{1,0:T(8,128)(2,1)}, bf16[512,1536]{1,0:T(8,128)(2,1)}, f32[4,1,768]{2,1,0:T(1,128)}, f32[512,768]{1,0:T(8,128)}, bf16[512,768]{1,0:T(8,128)(2,1)}, /*index=5*/f32[8,768]{1,0:T(8,128)}) custom-call(s32[8]{0:T(128)} %stack.63.refs_0_, ...), custom_call_target="tpu_custom_call", output_to_operand_aliasing={{0}: (9, {})} | custom-call | flops 4831838208 | bytes 33072128 | tf_op jit(solution)/shard_map/pallas_call | solution.py:162
  79.3 15.8 %shard_map.410 = (bf16[3,512,768]{2,1,0:T(8,128)(2,1)}, bf16[2,512,768]{2,1,0:T(8,128)(2,1)}, bf16[2,512,768]{2,1,0:T(8,128)(2,1)}, f32[8,768]{1,0:T(8,128)}) custom-call(s32[8]{0:T(128)} %stack.63.refs_0_, bf16[512,768]{1,0:T(8,128)(2,1)} %get-tuple-element.118.refs_1_.refs_2_, bf16[512,768]{1,0:T(8,128)(2,1)} %get-tuple-element.118.refs_1_.refs_2_, ...), custom_call_target="tpu_custom_call" | custom-call | flops 8053063680 | bytes 16934912 | tf_op jit(solution)/shard_map/pallas_call | solution.py:162
  95.7 3.4 %collective-permute-done.5.refs_4_ = bf16[2,512,768]{2,1,0:T(8,128)(2,1)} collective-permute-done((bf16[2,512,768]{2,1,0:T(8,128)(2,1)}, bf16[2,512,768]{2,1,0:T(8,128)(2,1)}, u32[]{:S(2)}, u32[]{:S(2)}) %collective-permute-start.5) | collective-permute-done | bytes 1572896 | tf_op jit(solution)/shard_map/ppermute | solution.py:34
  99.0 6.7 %shard_map.413 = (bf16[8,2,48,768]{3,2,1,0:T(8,128)(2,1)}, bf16[8,2,48,768]{3,2,1,0:T(8,128)(2,1)}) custom-call(s32[8]{0:T(128)} %stack.63.refs_0_, bf16[2,512,768]{2,1,0:T(8,128)(2,1)} %shard_map.406.refs_1_, bf16[2,512,768]{2,1,0:T(8,128)(2,1)} %get-tuple-element.121.refs_2_, bf16[2,512,768]{2,1,0:T(8,128)(2,1)} %collective-permute-done.2.refs_1_.refs_10_.refs_3_, ...), custom_call_target="tpu_custom_call" | custom-call | flops 2415919104 | bytes 8650752 | tf_op jit(solution)/shard_map/pallas_call | solution.py:162
  107.4 12.4 %shard_map.414 = (bf16[8,2,96,768]{3,2,1,0:T(8,128)(2,1)}, bf16[8,2,96,768]{3,2,1,0:T(8,128)(2,1)}) custom-call(s32[8]{0:T(128)} %stack.63.refs_0_, bf16[512,1536]{1,0:T(8,128)(2,1)} %get-tuple-element.108.refs_1_, bf16[512,768]{1,0:T(8,128)(2,1)} %get-tuple-element.109.refs_1_.refs_2_, bf16[512,1536]{1,0:T(8,128)(2,1)} %get-tuple-element.115.refs_3_, ...), custom_call_target="tpu_custom_call" | custom-call | flops 4831838208 | bytes 28311552 | tf_op jit(solution)/shard_map/pallas_call | solution.py:162
  127.6 6.3 %shard_map.416 = (bf16[512,768]{1,0:T(8,128)(2,1)}, f32[1,768]{1,0:T(1,128)}) custom-call(bf16[3,512,768]{2,1,0:T(8,128)(2,1)} %get-tuple-element.120.refs_1_.refs_0_, bf16[768,768]{1,0:T(8,128)(2,1)} %refs_1_.3, bf16[768,768]{1,0:T(8,128)(2,1)} %refs_2_.5, bf16[768,768]{1,0:T(8,128)(2,1)} %refs_3_.9, f32[512,768]{1,0:T(8,128)} %get-tuple-element.125.refs_4_, ...), custom_call_target="tpu_custom_call" | custom-call | flops 1811939328 | bytes 8260608 | tf_op jit(solution)/shard_map/pallas_call | solution.py:162
  141.2 5.7 %collective-permute-done.9 = bf16[2,2,48,768]{3,2,1,0:T(8,128)(2,1)S(1)} collective-permute-done((bf16[2,2,48,768]{3,2,1,0:T(8,128)(2,1)S(1)}, bf16[2,2,48,768]{3,2,1,0:T(8,128)(2,1)S(1)}, u32[]{:S(2)}, u32[]{:S(2)}) %collective-permute-start.9) | collective-permute-done | bytes 294944 | tf_op jit(solution)/shard_map/ppermute | solution.py:34
  149.7 3.9 %shard_map.419 = bf16[32,768]{1,0:T(8,128)(2,1)} custom-call(s32[8]{0:T(128)} %stack.63.refs_0_, f32[8,768]{1,0:T(8,128)} %get-tuple-element.131.refs_1_, f32[8,768]{1,0:T(8,128)} %get-tuple-element.132.refs_2_, f32[8,768]{1,0:T(8,128)} %get-tuple-element.133.refs_3_, f32[4,1,768]{2,1,0:T(1,128)} %get-tuple-element.134.refs_4_, ...), custom_call_target="tpu_custom_call" | custom-call | bytes 929280 | tf_op jit(solution)/shard_map/pallas_call | solution.py:162
  156.9 5.5 %collective-permute-done.11 = bf16[128,768]{1,0:T(8,128)(2,1)S(1)} collective-permute-done((bf16[128,768]{1,0:T(8,128)(2,1)S(1)}, bf16[128,768]{1,0:T(8,128)(2,1)S(1)}, u32[]{:S(2)}, u32[]{:S(2)}) %collective-permute-start.11) | collective-permute-done | bytes 196640 | tf_op jit(solution)/shard_map/ppermute | solution.py:34
  162.5 3.6 %collective-permute-start.12 = (bf16[224,768]{1,0:T(8,128)(2,1)S(1)}, bf16[224,768]{1,0:T(8,128)(2,1)S(1)}, u32[]{:S(2)}, u32[]{:S(2)}) collective-permute-start(bf16[224,768]{1,0:T(8,128)(2,1)S(1)} %pad_maximum_fusion.4), channel_id=1, source_target_pairs={{0,4},{4,0},{8,12},{12,8},{1,5},{5,1},{9,13},{13,9},{2,6},{6,2},{1... | collective-permute-start | bytes 1032200 | tf_op jit(solution)/shard_map/ppermute | solution.py:34
  166.1 5.2 %collective-permute-done.12 = bf16[224,768]{1,0:T(8,128)(2,1)S(1)} collective-permute-done((bf16[224,768]{1,0:T(8,128)(2,1)S(1)}, bf16[224,768]{1,0:T(8,128)(2,1)S(1)}, u32[]{:S(2)}, u32[]{:S(2)}) %collective-permute-start.12) | collective-permute-done | bytes 344096 | tf_op jit(solution)/shard_map/ppermute | solution.py:34
  178.6 18.8 %collective-permute-done.14 = bf16[416,768]{1,0:T(8,128)(2,1)S(1)} collective-permute-done((bf16[416,768]{1,0:T(8,128)(2,1)S(1)}, bf16[416,768]{1,0:T(8,128)(2,1)S(1)}, u32[]{:S(2)}, u32[]{:S(2)}) %collective-permute-start.14) | collective-permute-done | bytes 639008 | tf_op jit(solution)/shard_map/ppermute | solution.py:636
  202.6 3.2 %collective-permute-start.16 = (bf16[816,768]{1,0:T(8,128)(2,1)S(1)}, bf16[816,768]{1,0:T(8,128)(2,1)}, u32[]{:S(2)}, u32[]{:S(2)}) collective-permute-start(bf16[816,768]{1,0:T(8,128)(2,1)S(1)} %pad_maximum_fusion.refs_1_.refs_0_), channel_id=1, source_target_pairs={{0,2},{1,17},{2,0},{3,19},{4,6},{5,21},{6,4},{7,23},{8,10},{9,25},... | collective-permute-start | bytes 3760136 | tf_op jit(solution)/shard_map/ppermute | solution.py:636
  206.3 14.5 %collective-permute-done.16.refs_1_ = bf16[816,768]{1,0:T(8,128)(2,1)} collective-permute-done((bf16[816,768]{1,0:T(8,128)(2,1)S(1)}, bf16[816,768]{1,0:T(8,128)(2,1)}, u32[]{:S(2)}, u32[]{:S(2)}) %collective-permute-start.16) | collective-permute-done | bytes 1253408 | tf_op jit(solution)/shard_map/ppermute | solution.py:636
  227.1 5.5 %collective-permute-done.8 = bf16[256,768]{1,0:T(8,128)(2,1)} collective-permute-done((bf16[256,768]{1,0:T(8,128)(2,1)S(1)}, bf16[256,768]{1,0:T(8,128)(2,1)}, u32[]{:S(2)}, u32[]{:S(2)}) %collective-permute-start.8) | collective-permute-done | bytes 393248 | tf_op jit(solution)/shard_map/ppermute | solution.py:34
  234.7 5.4 %collective-permute-done.20 = bf16[1,2,96,768]{3,2,1,0:T(8,128)(2,1)} collective-permute-done((bf16[1,2,96,768]{3,2,1,0:T(8,128)(2,1)}, bf16[1,2,96,768]{3,2,1,0:T(8,128)(2,1)}, u32[]{:S(2)}, u32[]{:S(2)}) %collective-permute-start.20) | collective-permute-done | bytes 294944 | tf_op jit(solution)/shard_map/ppermute | solution.py:34
  242.1 4.9 %shard_map.422 = (f32[16,48,768]{2,1,0:T(8,128)}, f32[16,48,768]{2,1,0:T(8,128)}, f32[16,48,768]{2,1,0:T(8,128)}, f32[16,48,768]{2,1,0:T(8,128)}) custom-call(s32[8]{0:T(128)} %stack.63.refs_0_, bf16[816,768]{1,0:T(8,128)(2,1)} %copy-done, bf16[816,768]{1,0:T(8,128)(2,1)} %collective-permute-done.18.refs_2_), custom_call_target="tpu_custom_call" | custom-call | bytes 11943936 | tf_op jit(solution)/shard_map/pallas_call | solution.py:162
  249.7 4.9 %shard_map.423 = (f32[16,48,768]{2,1,0:T(8,128)}, f32[16,48,768]{2,1,0:T(8,128)}, f32[16,48,768]{2,1,0:T(8,128)}, f32[16,48,768]{2,1,0:T(8,128)}) custom-call(s32[8]{0:T(128)} %stack.63.refs_0_, bf16[816,768]{1,0:T(8,128)(2,1)} %collective-permute-done.16.refs_1_, ...), custom_call_target="tpu_custom_call", output_to_operand_aliasing={{0}: (3, {}), {1}: (4, {}), {2}: (5, {}), {3}: (6, {})} | custom-call | bytes 21381120 | tf_op jit(solution)/shard_map/pallas_call | solution.py:162
  (113 shorter events, 62.8 us)
Async XLA Ops:
  2.6 12.1 %collective-permute-start = (bf16[256,768]{1,0:T(8,128)(2,1)S(1)}, bf16[256,768]{1,0:T(8,128)(2,1)S(1)}, u32[]{:S(2)}, u32[]{:S(2)}) collective-permute-start(bf16[256,768]{1,0:T(8,128)(2,1)S(1)} %get-tuple-element.175), channel_id=1, source_target_pairs={{0,16},{16,0},{1,17},{17,1},{2,18},{18,2},{3,19},{19,3},{4,20},{20... | collective-permute-start | bytes 1179656 | tf_op jit(solution)/shard_map/ppermute | solution.py:34
  16.9 22.8 %collective-permute-start.1 = (bf16[256,768]{1,0:T(8,128)(2,1)}, bf16[256,768]{1,0:T(8,128)(2,1)S(1)}, u32[]{:S(2)}, u32[]{:S(2)}) collective-permute-start(bf16[256,768]{1,0:T(8,128)(2,1)} %get-tuple-element.173), channel_id=1, source_target_pairs={{0,16},{16,0},{1,17},{17,1},{2,18},{18,2},{3,19},{19,3},{4,20},{20... | collective-permute-start | bytes 1179656 | tf_op jit(solution)/shard_map/ppermute | solution.py:34
  40.5 19.1 %collective-permute-start.2 = (bf16[2,512,768]{2,1,0:T(8,128)(2,1)}, bf16[2,512,768]{2,1,0:T(8,128)(2,1)}, u32[]{:S(2)}, u32[]{:S(2)}) collective-permute-start(bf16[2,512,768]{2,1,0:T(8,128)(2,1)} %shard_map.406.refs_1_), channel_id=1, source_target_pairs={{0,1},{1,0},{2,3},{3,2},{4,5},{5,4},{6,7},{7,6},{8,9},{9,8},{10,11... | collective-permute-start | bytes 4718600 | tf_op jit(solution)/shard_map/ppermute | solution.py:34
  61.5 16.9 %collective-permute-start.3 = (bf16[256,768]{1,0:T(8,128)(2,1)S(1)}, bf16[256,768]{1,0:T(8,128)(2,1)S(1)}, u32[]{:S(2)}, u32[]{:S(2)}) collective-permute-start(bf16[256,768]{1,0:T(8,128)(2,1)S(1)} %get-tuple-element.172), channel_id=1, source_target_pairs={{0,16},{16,0},{1,17},{17,1},{2,18},{18,2},{3,19},{19,3},{4,20},{20... | collective-permute-start | bytes 1179656 | tf_op jit(solution)/shard_map/ppermute | solution.py:34
  79.1 16.0 %collective-permute-start.4 = (bf16[512,4608]{1,0:T(8,128)(2,1)}, bf16[512,4608]{1,0:T(8,128)(2,1)}, u32[]{:S(2)}, u32[]{:S(2)}) collective-permute-start(bf16[512,4608]{1,0:T(8,128)(2,1)} %shard_map.409.refs_12_), channel_id=1, source_target_pairs={{0,1},{1,0},{2,3},{3,2},{4,5},{5,4},{6,7},{7,6},{8,9},{9,8},{10,11... | collective-permute-start | bytes 14155784 | tf_op jit(solution)/shard_map/ppermute | solution.py:34
  95.1 3.9 %collective-permute-start.5 = (bf16[2,512,768]{2,1,0:T(8,128)(2,1)}, bf16[2,512,768]{2,1,0:T(8,128)(2,1)}, u32[]{:S(2)}, u32[]{:S(2)}) collective-permute-start(bf16[2,512,768]{2,1,0:T(8,128)(2,1)} %shard_map.412), channel_id=1, source_target_pairs={{0,1},{1,0},{2,3},{3,2},{4,5},{5,4},{6,7},{7,6},{8,9},{9,8},{10,11... | collective-permute-start | bytes 4718600 | tf_op jit(solution)/shard_map/ppermute | solution.py:34
  105.7 16.5 %collective-permute-start.6 = (bf16[8,2,48,768]{3,2,1,0:T(8,128)(2,1)}, bf16[8,2,48,768]{3,2,1,0:T(8,128)(2,1)}, u32[]{:S(2)}, u32[]{:S(2)}) collective-permute-start(bf16[8,2,48,768]{3,2,1,0:T(8,128)(2,1)} %get-tuple-element.126), channel_id=1, source_target_pairs={{0,2},{1,17},{2,0},{3,19},{4,6},{5,21},{6,4},{7,23},{8,10},{9,25},... | collective-permute-start | bytes 3538952 | tf_op jit(solution)/shard_map/ppermute | solution.py:636
  125.8 10.2 %collective-permute-start.7 = (bf16[4,2,48,768]{3,2,1,0:T(8,128)(2,1)}, bf16[4,2,48,768]{3,2,1,0:T(8,128)(2,1)}, u32[]{:S(2)}, u32[]{:S(2)}) collective-permute-start(bf16[4,2,48,768]{3,2,1,0:T(8,128)(2,1)} %get-tuple-element.166.refs_5_), channel_id=1, source_target_pairs={{0,16},{1,3},{2,18},{3,1},{4,20},{5,7},{6,22},{7,5},{8,24},{9,11},... | collective-permute-start | bytes 1769480 | tf_op jit(solution)/shard_map/ppermute | solution.py:636
  137.9 34.0 %collective-permute-start.13 = (bf16[8,2,96,768]{3,2,1,0:T(8,128)(2,1)}, bf16[8,2,96,768]{3,2,1,0:T(8,128)(2,1)}, u32[]{:S(2)}, u32[]{:S(2)}) collective-permute-start(bf16[8,2,96,768]{3,2,1,0:T(8,128)(2,1)} %get-tuple-element.139), channel_id=1, source_target_pairs={{0,2},{1,17},{2,0},{3,19},{4,6},{5,21},{6,4},{7,23},{8,10},{9,25},... | collective-permute-start | bytes 7077896 | tf_op jit(solution)/shard_map/ppermute | solution.py:636
  139.7 7.3 %collective-permute-start.9 = (bf16[2,2,48,768]{3,2,1,0:T(8,128)(2,1)S(1)}, bf16[2,2,48,768]{3,2,1,0:T(8,128)(2,1)S(1)}, u32[]{:S(2)}, u32[]{:S(2)}) collective-permute-start(bf16[2,2,48,768]{3,2,1,0:T(8,128)(2,1)S(1)} %copy-done.11), channel_id=1, source_target_pairs={{0,4},{4,0},{8,12},{12,8},{1,5},{5,1},{9,13},{13,9},{2,6},{6,2},{1... | collective-permute-start | bytes 884744 | tf_op jit(solution)/shard_map/ppermute | solution.py:34
  147.0 7.7 %collective-permute-start.10 = (bf16[1,2,48,768]{3,2,1,0:T(8,128)(2,1)S(1)}, bf16[1,2,48,768]{3,2,1,0:T(8,128)(2,1)S(1)}, u32[]{:S(2)}, u32[]{:S(2)}) collective-permute-start(bf16[1,2,48,768]{3,2,1,0:T(8,128)(2,1)S(1)} %fusion.6), channel_id=1, source_target_pairs={{0,8},{4,12},{8,0},{12,4},{1,9},{5,13},{9,1},{13,5},{2,10},{6,14},... | collective-permute-start | bytes 442376 | tf_op jit(solution)/shard_map/ppermute | solution.py:34
  155.8 6.6 %collective-permute-start.11 = (bf16[128,768]{1,0:T(8,128)(2,1)S(1)}, bf16[128,768]{1,0:T(8,128)(2,1)S(1)}, u32[]{:S(2)}, u32[]{:S(2)}) collective-permute-start(bf16[128,768]{1,0:T(8,128)(2,1)S(1)} %pad_maximum_fusion.5), channel_id=1, source_target_pairs={{0,8},{4,12},{8,0},{12,4},{1,9},{5,13},{9,1},{13,5},{2,10},{6,14},... | collective-permute-start | bytes 589832 | tf_op jit(solution)/shard_map/ppermute | solution.py:34
  162.5 8.8 %collective-permute-start.12 = (bf16[224,768]{1,0:T(8,128)(2,1)S(1)}, bf16[224,768]{1,0:T(8,128)(2,1)S(1)}, u32[]{:S(2)}, u32[]{:S(2)}) collective-permute-start(bf16[224,768]{1,0:T(8,128)(2,1)S(1)} %pad_maximum_fusion.4), channel_id=1, source_target_pairs={{0,4},{4,0},{8,12},{12,8},{1,5},{5,1},{9,13},{13,9},{2,6},{6,2},{1... | collective-permute-start | bytes 1032200 | tf_op jit(solution)/shard_map/ppermute | solution.py:34
  174.3 25.0 %collective-permute-start.15 = (bf16[4,2,96,768]{3,2,1,0:T(8,128)(2,1)S(1)}, bf16[4,2,96,768]{3,2,1,0:T(8,128)(2,1)S(1)}, u32[]{:S(2)}, u32[]{:S(2)}) collective-permute-start(bf16[4,2,96,768]{3,2,1,0:T(8,128)(2,1)S(1)} %get-tuple-element.162.refs_1_), channel_id=1, source_target_pairs={{0,16},{1,3},{2,18},{3,1},{4,20},{5,7},{6,22},{7,5},{8,24},{9,11},... | collective-permute-start | bytes 3538952 | tf_op jit(solution)/shard_map/ppermute | solution.py:636
  178.2 19.2 %collective-permute-start.14 = (bf16[416,768]{1,0:T(8,128)(2,1)S(1)}, bf16[416,768]{1,0:T(8,128)(2,1)S(1)}, u32[]{:S(2)}, u32[]{:S(2)}) collective-permute-start(bf16[416,768]{1,0:T(8,128)(2,1)S(1)} %pad_maximum_fusion.2), channel_id=1, source_target_pairs={{0,16},{1,3},{2,18},{3,1},{4,20},{5,7},{6,22},{7,5},{8,24},{9,11},... | collective-permute-start | bytes 1916936 | tf_op jit(solution)/shard_map/ppermute | solution.py:636
  202.6 24.5 %copy-start = (bf16[816,768]{1,0:T(8,128)(2,1)}, bf16[816,768]{1,0:T(8,128)(2,1)S(1)}, u32[]{:S(2)}) copy-start(bf16[816,768]{1,0:T(8,128)(2,1)S(1)} %pad_maximum_fusion.refs_1_.refs_0_) | copy-start | bytes 3760132
  202.6 23.5 %copy-start.8 = (bf16[256,768]{1,0:T(8,128)(2,1)S(1)}, bf16[256,768]{1,0:T(8,128)(2,1)}, u32[]{:S(2)}) copy-start(bf16[256,768]{1,0:T(8,128)(2,1)} %copy-done.7) | copy-start | bytes 1179652
  202.6 23.5 %copy-start.10 = (bf16[1,1,256,768]{3,2,1,0:T(8,128)(2,1)S(1)}, bf16[1,1,256,768]{3,2,1,0:T(8,128)(2,1)}, u32[]{:S(2)}) copy-start(bf16[1,1,256,768]{3,2,1,0:T(8,128)(2,1)} %get-tuple-element.171) | copy-start | bytes 1179652
  202.6 18.2 %collective-permute-start.16 = (bf16[816,768]{1,0:T(8,128)(2,1)S(1)}, bf16[816,768]{1,0:T(8,128)(2,1)}, u32[]{:S(2)}, u32[]{:S(2)}) collective-permute-start(bf16[816,768]{1,0:T(8,128)(2,1)S(1)} %pad_maximum_fusion.refs_1_.refs_0_), channel_id=1, source_target_pairs={{0,2},{1,17},{2,0},{3,19},{4,6},{5,21},{6,4},{7,23},{8,10},{9,25},... | collective-permute-start | bytes 3760136 | tf_op jit(solution)/shard_map/ppermute | solution.py:636
  205.8 16.0 %collective-permute-start.19 = (bf16[2,2,96,768]{3,2,1,0:T(8,128)(2,1)S(1)}, bf16[2,2,96,768]{3,2,1,0:T(8,128)(2,1)S(1)}, u32[]{:S(2)}, u32[]{:S(2)}) collective-permute-start(bf16[2,2,96,768]{3,2,1,0:T(8,128)(2,1)S(1)} %copy-done.6), channel_id=1, source_target_pairs={{0,4},{4,0},{8,12},{12,8},{1,5},{5,1},{9,13},{13,9},{2,6},{6,2},{1... | collective-permute-start | bytes 1769480 | tf_op jit(solution)/shard_map/ppermute | solution.py:34
  206.3 35.7 %collective-permute-start.18 = (bf16[816,768]{1,0:T(8,128)(2,1)S(1)}, bf16[816,768]{1,0:T(8,128)(2,1)}, u32[]{:S(2)}, u32[]{:S(2)}) collective-permute-start(bf16[816,768]{1,0:T(8,128)(2,1)S(1)} %pad_maximum_fusion.refs_1_.refs_0_), channel_id=1, source_target_pairs={{0,1},{1,0},{2,3},{3,2},{4,5},{5,4},{6,7},{7,6},{8,9},{9,8},{10,11... | collective-permute-start | bytes 3760136 | tf_op jit(solution)/shard_map/ppermute | solution.py:34
  220.9 26.2 %collective-permute-start.17 = (bf16[816,768]{1,0:T(8,128)(2,1)}, bf16[816,768]{1,0:T(8,128)(2,1)}, u32[]{:S(2)}, u32[]{:S(2)}) collective-permute-start(bf16[816,768]{1,0:T(8,128)(2,1)} %collective-permute-done.16.refs_1_), channel_id=1, source_target_pairs={{0,1},{1,0},{2,3},{3,2},{4,5},{5,4},{6,7},{7,6},{8,9},{9,8},{10,11... | collective-permute-start | bytes 3760136 | tf_op jit(solution)/shard_map/ppermute | solution.py:34
  220.9 11.7 %collective-permute-start.8 = (bf16[256,768]{1,0:T(8,128)(2,1)S(1)}, bf16[256,768]{1,0:T(8,128)(2,1)}, u32[]{:S(2)}, u32[]{:S(2)}) collective-permute-start(bf16[256,768]{1,0:T(8,128)(2,1)S(1)} %get-tuple-element.170), channel_id=1, source_target_pairs={{0,16},{16,0},{1,17},{17,1},{2,18},{18,2},{3,19},{19,3},{4,20},{20... | collective-permute-start | bytes 1179656 | tf_op jit(solution)/shard_map/ppermute | solution.py:34
  223.3 16.8 %collective-permute-start.20 = (bf16[1,2,96,768]{3,2,1,0:T(8,128)(2,1)}, bf16[1,2,96,768]{3,2,1,0:T(8,128)(2,1)}, u32[]{:S(2)}, u32[]{:S(2)}) collective-permute-start(bf16[1,2,96,768]{3,2,1,0:T(8,128)(2,1)} %fusion.3), channel_id=1, source_target_pairs={{0,8},{4,12},{8,0},{12,4},{1,9},{5,13},{9,1},{13,5},{2,10},{6,14},... | collective-permute-start | bytes 884744 | tf_op jit(solution)/shard_map/ppermute | solution.py:34
  (18 other events, 106.3 us)
where the time goes:
time: 256 us; the launch traced here: 255 us
  Pallas kernels  118 us (46%)
  waiting for transfers between devices  74.6 us (29%)
  starting transfers between devices  29.4 us (11%)
  other arithmetic  19.6 us (8%)
  local copies, waits for them, and re-layouts  12 us (5%)
    pallas_call x14, Pallas kernels, run(): pl.pallas_call(wrapped, grid_spec=pltpu.PrefetchScalarGridSpec(num_scalar...  118 us
    ppermute x6, waiting for transfers between devices, crossed(): return lax.ppermute(value, everywhere, pairs)  37.9 us
    ppermute x15, waiting for transfers between devices, swapped(): lax.ppermute(value, axis, [(i, i ^ 1 << bit) for i in range(lax.axis_size...  36.7 us
    ppermute x15, starting transfers between devices, swapped(): lax.ppermute(value, axis, [(i, i ^ 1 << bit) for i in range(lax.axis_size...  18.9 us
    ppermute x6, starting transfers between devices, crossed(): return lax.ppermute(value, everywhere, pairs)  10.6 us
    convert_element_type x7, other arithmetic, plus(): return (left.astype(f32) + right.astype(f32)).astype(bf16)  8.52 us
  transfers between devices with their start and end apart: 21, of which 12 were waited for; matrix products, arithmetic and copies ran while one was open for 5% of the time, Pallas kernels for 41%

commit v1 on v0

--- a/solution.py
+++ b/solution.py
@@ -330,24 +330,28 @@
     ]
 
 
-def store_by_core(bits, values, other, own):
-    zero, one = by_core(values)
-
-    @pl.when(bits[0] == 0)
-    def _():
-        own[...], other[...] = zero, one
-
-    @pl.when(bits[0] == 1)
-    def _():
-        own[...], other[...] = one, zero
+SUB = 256
 
 
 def feed_forward_body(
     bits, attended, own, far, stamp, ow, ob, gain, shift, ew, eb, rw, rb, gain2, shift2, valid, cot_own, cot_far,
-    output, for_core, activated_own, slope, mixed_low, normed, inverse, d_second, d_reduced, sums, mixed, total,
-    activated,
+    output, for_core, activated_own, expanded_own, mixed_low, d_reduced, bias_grad, d_first, d_branch, sums,
+    total, normed, inverse, slope, columns,
 ):
     step = pl.program_id(0)
+    tiles = FF // D
+
+    def store(own_out, offset):
+        zero, one = by_core(columns[...])
+        here = pl.ds(pl.multiple_of(offset, D // 2), D // 2)
+
+        @pl.when(bits[0] == 0)
+        def _():
+            own_out[...], for_core[:, here] = zero, one
+
+        @pl.when(bits[0] == 1)
+        def _():
+            own_out[...], for_core[:, here] = one, zero
 
     @pl.when(step == 0)
     def _():
@@ -356,26 +360,26 @@
         value = n1 * row(gain) + row(shift)
         normed[...] = n1
         inverse[...] = inv
-        mixed[...] = value
         mixed_low[...] = value.astype(bf16)
         total[...] = value + row(rb)
 
-    added_up = None
-    bias = eb[pl.ds(pl.multiple_of(step * D, D), D)].reshape(1, -1)
-    for part in range(D // SUB):
-        cut = slice(part * SUB, (part + 1) * SUB)
-        expanded = nn(mixed_low[...], ew[:, cut]) + bias[:, cut]
-        chance = 0.5 * (1.0 + lax.erf(expanded * root_half))
-        slope[:, cut] = chance + expanded * jnp.exp(-0.5 * expanded * expanded) * density_scale
-        low = (expanded * chance).astype(bf16)
-        activated[:, cut] = low
-        product = nn(low, rw[cut, :])
-        added_up = product if added_up is None else added_up + product
-    total[...] += added_up
-    here = pl.ds(pl.multiple_of(step * (D // 2), D // 2), D // 2)
-    store_by_core(bits, activated[...], for_core.at[:, here], activated_own)
-
-    @pl.when(step == pl.num_programs(0) - 1)
+    @pl.when(step < tiles)
+    def _():
+        added_up = None
+        bias = eb[pl.ds(pl.multiple_of(step * D, D), D)].reshape(1, -1)
+        for part in range(D // SUB):
+            cut = slice(part * SUB, (part + 1) * SUB)
+            expanded = nn(mixed_low[...], ew[:, cut]) + bias[:, cut]
+            chance = 0.5 * (1.0 + lax.erf(expanded * root_half))
+            slope[step, :, cut] = chance + expanded * jnp.exp(-0.5 * expanded * expanded) * density_scale
+            low = (expanded * chance).astype(bf16)
+            columns[:, cut] = low
+            product = nn(low, rw[cut, :])
+            added_up = product if added_up is None else added_up + product
+        total[...] += added_up
+        store(activated_own, step * (D // 2))
+
+    @pl.when(step == tiles - 1)
     def _():
         n2, inv = normalized(total[...])
         weight = valid[...]
@@ -383,43 +387,54 @@
         d_out = both(cot_own, cot_far).astype(f32) * weight
         back = norm_backward(d_out * row(gain2), n2, inv)
         low = back.astype(bf16)
-        d_second[...] = back
+        total[...] = back
         d_reduced[...] = low
         for_core[:, 2 * D : 3 * D] = low
-        for_core[:, 3 * D :] = mixed_low[...]
+        for_core[:, 3 * D : 4 * D] = mixed_low[...]
         sums[...] = jnp.concatenate(
             [jnp.zeros((5, D), f32), row_sum(low.astype(f32)), row_sum(d_out * n2), row_sum(d_out)], axis=0
         )
 
-
-SUB = 256
+    @pl.when(step >= tiles)
+    def _():
+        d_expanded = (nt(d_reduced[...], rw[...]) * slope[step - tiles]).astype(bf16)
+        columns[...] = d_expanded
+        bias_grad[0] = row_sum(d_expanded.astype(f32))
+        total[...] += nt(d_expanded, ew[...])
+        store(expanded_own, 4 * D + (step - tiles) * (D // 2))
+
+    @pl.when(step == 2 * tiles - 1)
+    def _():
+        d_mixed = total[...]
+        n1 = normed[...]
+        back = norm_backward(d_mixed * row(gain), n1, inverse[...])
+        low = back.astype(bf16)
+        d_first[...] = back
+        d_branch[...] = low
+        sums[2:5] = jnp.concatenate([row_sum(low.astype(f32)), row_sum(d_mixed * n1), row_sum(d_mixed)], axis=0)
 
 
 def feed_forward(
     bits, attended, own, far, stamp, ow, ob, gain, shift, ew, eb, rw, rb, gain2, shift2, valid, cot_own, cot_far
 ):
+    tiles = FF // D
     line, square, half = vector(D), whole(ROWS, D), whole(CAP, D)
+    forward = pl.BlockSpec((ROWS, D // 2), lambda j, *at: (0, jnp.minimum(j, tiles - 1)))
+    backward = pl.BlockSpec((ROWS, D // 2), lambda j, *at: (0, jnp.maximum(j - tiles, 0)))
     return run(
         feed_forward_body,
-        (FF // D,),
+        (2 * tiles,),
         (attended, own, far, stamp, ow, ob, gain, shift, ew, eb, rw, rb, gain2, shift2, valid, cot_own, cot_far),
-        [square, half, half, whole(1, D), whole(D, D), line, line, line, column_tile(D, D), vector(FF), row_tile(D, D)]
+        [square, half, half, whole(1, D), whole(D, D), line, line, line]
+        + [pl.BlockSpec((D, D), lambda j, *at: (0, j % tiles)), vector(FF), pl.BlockSpec((D, D), lambda j, *at: (j % tiles, 0))]
         + [line, line, line, whole(ROWS, 1), half, half],
-        [
-            ((ROWS, D), bf16),
-            (FOR_CORE, bf16),
-            ((ROWS, FF // 2), bf16),
-            ((ROWS, FF), f32),
-            ((ROWS, D), bf16),
-            ((ROWS, D), f32),
-            ((ROWS, 1), f32),
-            ((ROWS, D), f32),
-            ((ROWS, D), bf16),
-            ((8, D), f32),
-        ],
-        [square, whole(ROWS, 4 * D), half_tile, column_tile(ROWS, D), square, square, whole(ROWS, 1), square, square, whole(8, D)],
-        2 * ROWS * D * (D + 2 * FF),
-        scratch=[pltpu.VMEM((ROWS, D), f32)] * 2 + [pltpu.VMEM((ROWS, D), bf16)],
+        [((ROWS, D), bf16), (FOR_CORE, bf16), ((ROWS, FF // 2), bf16), ((ROWS, FF // 2), bf16), ((ROWS, D), bf16)]
+        + [((ROWS, D), bf16), ((tiles, 1, D), f32), ((ROWS, D), f32), ((ROWS, D), bf16), ((8, D), f32)],
+        [square, whole(*FOR_CORE), forward, backward, square, square]
+        + [pl.BlockSpec((1, 1, D), lambda j, *at: (jnp.maximum(j - tiles, 0), 0, 0)), square, square, whole(8, D)],
+        2 * ROWS * D * (D + 4 * FF),
+        scratch=[pltpu.VMEM((ROWS, D), f32)] * 2
+        + [pltpu.VMEM((ROWS, 1), f32), pltpu.VMEM((tiles, ROWS, D), f32), pltpu.VMEM((ROWS, D), bf16)],
         scalars=(bits,),
     )
 
@@ -432,7 +447,7 @@
         low = grad.astype(bf16)
         for at in range(8):
             x, z = at % 2, at // 2
-            here = jnp.where(bits[0] == 0, tile, x) * 4 + (z % 2 * 2 + z // 2)
+            here = jnp.where(bits[0] == 0, tile * 4 + (z % 2 * 2 + z // 2), x * 4 + z)
             block = low[at * SHARE : (at + 1) * SHARE]
             mine = jnp.where(bits[0] == 0, x, tile) == bits[5]
 
@@ -465,58 +480,6 @@
         [((8, 2, SHARE, D), bf16)] * 2,
         [whole(8, 2, SHARE, D)] * 2,
         4 * ROWS * D * FF,
-        scalars=(bits,),
-        after=after,
-    )
-
-
-def expand_back_body(
-    bits, d_reduced, rw, slope, ew, d_second, normed, inverse, gain, for_core,
-    expanded_other, expanded_own, bias, d_first, d_branch, sums, total,
-):
-    step = pl.program_id(0)
-    d_expanded = (nt(d_reduced[...], rw[...]) * slope[...]).astype(bf16)
-    bias[0] = row_sum(d_expanded.astype(f32))
-    store_by_core(bits, d_expanded, expanded_other, expanded_own)
-    product = nt(d_expanded, ew[...])
-
-    @pl.when(step == 0)
-    def _():
-        total[...] = d_second[...] + product
-
-    @pl.when(step > 0)
-    def _():
-        total[...] += product
-
-    @pl.when(step == pl.num_programs(0) - 1)
-    def _():
-        d_mixed = total[...]
-        n1 = normed[...]
-        back = norm_backward(d_mixed * row(gain), n1, inverse[...])
-        low = back.astype(bf16)
-        d_first[...] = back
-        d_branch[...] = low
-        sums[...] = jnp.concatenate(
-            [jnp.zeros((2, D), f32), row_sum(low.astype(f32)), row_sum(d_mixed * n1), row_sum(d_mixed), jnp.zeros((3, D), f32)],
-            axis=0,
-        )
-
-
-def expand_back(bits, d_reduced, rw, slope, ew, d_second, normed, inverse, gain, for_core, after):
-    steps = FF // D
-    square = whole(ROWS, D)
-    return run(
-        expand_back_body,
-        (steps,),
-        (d_reduced, rw, slope, ew, d_second, normed, inverse, gain, for_core),
-        [square, row_tile(D, D), column_tile(ROWS, D), column_tile(D, D), square, square, whole(ROWS, 1), vector(D)]
-        + [pl.BlockSpec(memory_space=pl.ANY)],
-        [(FOR_CORE, bf16), ((ROWS, FF // 2), bf16)] + [((steps, 1, D), f32), ((ROWS, D), f32), ((ROWS, D), bf16), ((8, D), f32)],
-        [pl.BlockSpec((ROWS, D // 2), lambda j, *at: (0, 8 + j)), half_tile]
-        + [pl.BlockSpec((1, 1, D), lambda j, *at: (j, 0, 0)), square, square, whole(8, D)],
-        4 * ROWS * D * FF,
-        scratch=[pltpu.VMEM((ROWS, D), f32)],
-        aliases={9: 0},
         scalars=(bits,),
         after=after,
     )
@@ -622,7 +585,6 @@
 
 
 everywhere = ("y", "z", "x", "c")
-low_far, high_far = ("z", 0), ("z", 1)
 
 
 def crossed(value, first):
@@ -636,6 +598,13 @@
     return lax.ppermute(value, everywhere, pairs)
 
 
+def lined(value, first):
+    sizes = [lax.axis_size(axis) for axis in everywhere]
+    turn = lambda c: 1 if (c == 0) == first else 2
+    pairs = [(at, at ^ (turn(at % 2) * 4)) for at in range(math.prod(sizes))]
+    return lax.ppermute(value, everywhere, pairs)
+
+
 def plus(left, right):
     return (left.astype(f32) + right.astype(f32)).astype(bf16)
 
@@ -649,8 +618,8 @@
 BLOCK = 32
 
 
-def block_body(bits, first, second, third, bias, d_time, inner_sum, middle, features, outer, out):
-    riders = first[...] + second[...] + third[...]
+def block_body(bits, first, second, bias, d_time, inner_sum, middle, features, outer, out):
+    riders = first[...] + second[...]
     total = inner_sum[...]
     gate = 1.0 / (1.0 + jnp.exp(-total))
     d_middle = lax.dot_general(
@@ -697,10 +666,9 @@
     return data, jnp.concatenate([sum_rows(block[:16], got[:16]), block[16:], got[16:]])
 
 
-def unpack_body(bits, own, got, *refs):
-    outs = refs[-4:]
-    for at in range(8):
-        here, there = (bits[6] % 8) ^ at, (bits[7] % 8) ^ at
+def unpack_body(bits, own, got, outs):
+    for at in range(4):
+        here, there = (bits[6] % 4) ^ at, (bits[7] % 4) ^ at
         for matrix in range(2):
             rows = slice(at * SHARE + matrix * COLOUR, at * SHARE + (matrix + 1) * COLOUR)
             mine, other = own[rows].astype(f32), got[rows].astype(f32)
@@ -708,23 +676,33 @@
             outs[2 + matrix][there] = jnp.where(bits[0] == 0, other, mine)
 
 
-def unpack(bits, own, got, turn, outs):
-    shape = (16, COLOUR, D)
-    blocks = [pl.BlockSpec((8, COLOUR, D), lambda j, bits, at=at: ((bits[at] // 8) ^ turn, 0, 0)) for at in (6, 7)]
-    return run(
-        unpack_body,
-        (1,),
-        (own, got, *outs),
-        [whole(D, D)] * 2 + [pl.BlockSpec(memory_space=pl.ANY)] * len(outs),
-        [(shape, f32)] * 4,
-        [blocks[0]] * 2 + [blocks[1]] * 2,
-        0,
-        scalars=(bits,),
-        aliases={3 + k: k for k in range(len(outs))},
-    )
-
-
-def finish_body(own, turned, own_far, turned_far, *outs):
+def unpack_specs(turn):
+    part = pl.BlockSpec((4 * SHARE, D), lambda j, bits: (j, 0))
+    spots = [
+        pl.BlockSpec((4, COLOUR, D), lambda j, bits, at=at: ((bits[at] // 4) ^ (2 * turn + j), 0, 0)) for at in (6, 6, 7, 7)
+    ]
+    return part, spots
+
+
+matrix_shapes = [((16, COLOUR, D), f32)] * 4
+
+
+def first_unpack(bits, own, got):
+    part, spots = unpack_specs(0)
+    body = lambda bits, own, got, *outs: unpack_body(bits, own, got, outs)
+    return run(body, (2,), (own, got), [part] * 2, matrix_shapes, spots, 0, scalars=(bits,))
+
+
+def finish_body(bits, turned, turned_far, own, far, turned_last, turned_far_last, *refs):
+    outs = refs[-17:]
+    unpack_body(bits, turned, turned_far, outs[:4])
+
+    @pl.when(pl.program_id(0) == 0)
+    def _():
+        vectors_body(own, turned_last, far, turned_far_last, *outs[4:])
+
+
+def vectors_body(own, turned, own_far, turned_far, *outs):
     blocks = [ref[...].astype(f32) for ref in (own, turned, own_far, turned_far)]
     sums = (blocks[0][:16] + blocks[1][:16]) + (blocks[2][:16] + blocks[3][:16])
     for at in range(8):
@@ -747,16 +725,27 @@
     inner_bias[...] = jnp.sum(d_inner, axis=0)
 
 
-def finish(*messages):
+def finish(bits, turned, turned_far, message, message_far, outs):
+    part, spots = unpack_specs(1)
     last = pl.BlockSpec((48, D), lambda j, *at: (D // 48, 0))
     shapes = [(D,)] * 8 + [(4, 1, D), (TDIM, TFF), (TFF,), (TFF, D), (D,)]
-    return run(finish_body, (1,), messages, [last] * 4, [(shape, f32) for shape in shapes], [whole(*shape) for shape in shapes], 0)
+    return run(
+        finish_body,
+        (2,),
+        (turned, turned_far, message, message_far, turned, turned_far, *outs),
+        [part] * 2 + [last] * 4 + [pl.BlockSpec(memory_space=pl.ANY)] * 4,
+        matrix_shapes + [(shape, f32) for shape in shapes],
+        spots + [whole(*shape) for shape in shapes],
+        0,
+        scalars=(bits,),
+        aliases={7 + k: k for k in range(4)},
+    )
 
 
 def plain_rows(first_class, second_class):
     zero = jnp.concatenate(first_class).reshape(2, 2, 2, 2, SHARE, D)
     one = jnp.concatenate(second_class).reshape(2, 2, 2, 2, SHARE, D)
-    classes = jnp.stack([jnp.transpose(zero, (1, 3, 2, 0, 4, 5)), jnp.transpose(one, (0, 3, 2, 1, 4, 5))], axis=4)
+    classes = jnp.stack([jnp.transpose(zero, (1, 3, 2, 0, 4, 5)), jnp.transpose(one, (0, 2, 3, 1, 4, 5))], axis=4)
     return classes.reshape(FF, D)
 
 
@@ -808,7 +797,9 @@
     c, x, z = lax.axis_index("c") if tuned else 0, lax.axis_index("x"), lax.axis_index("z")
     first, second = jnp.where(c == 0, x, stream), jnp.where(c == 0, stream, x)
     wanted = first if tuned else 0
-    places = [one * 8 + two * 4 + (z & 1) * 2 + (z >> 1) for one, two in ((x, stream), (stream, x))]
+    near_z, across_z = z & 1, z >> 1
+    third, fourth = jnp.where(c == 0, near_z, across_z), jnp.where(c == 0, across_z, near_z)
+    places = [x * 8 + stream * 4 + near_z * 2 + across_z, stream * 8 + x * 4 + across_z * 2 + near_z]
     bits = jnp.stack([c, x, stream, z & 1, z >> 1, wanted, *places]).astype(jnp.int32)
 
     def whole_sequence(rows):
@@ -821,20 +812,20 @@
         return jnp.where(stream == 0, jnp.stack([own, far]), jnp.stack([far, own]))[:, None]
 
     own, far = whole_sequence(layer_input)
-    cotangent, far = lax.optimization_barrier((cotangent, far))
-    cot_own, cot_far = whole_sequence(cotangent)
     features, inner_sum, middle, stamp, allowed, valid, masked = prepare(
         bits, timesteps, src_len, seq_len, key_keep, time_inner, time_inner_bias, time_outer, time_outer_bias
     )
     weights = (query_weight, query_bias, key_weight, value_weight, value_bias)
     *first_rows, own_low = project(own, 0, stamp, allowed, *weights)
     (far,) = tie([far], first_rows[:1])
+    cotangent, far = lax.optimization_barrier((cotangent, far))
+    cot_own, cot_far = whole_sequence(cotangent)
     *other_rows, far_low = project(far, 1, stamp, allowed, *weights)
     q, k, v = zip(first_rows, other_rows)
     low = (own_low, far_low)
     attended, lefts, probs = attend(q, k, v, low, masked)
     (lefts,) = tie([lefts], [cot_far])
-    output, for_core, activated, slope, mixed_low, normed, inverse, d_second, d_reduced, second_sums = feed_forward(
+    output, for_core, activated, d_expanded, mixed_low, d_reduced, expand_bias_grad, d_first, d_branch, layer_sums = feed_forward(
         bits,
         attended,
         own,
@@ -857,63 +848,59 @@
     lefts_got = swapped(lefts, core)
     (output,) = tie([output], [lefts_got])
     output_got = swapped(output[CAP:], side)
-    for_core, d_expanded, expand_bias_grad, d_first, d_branch, first_sums = expand_back(
-        bits,
-        d_reduced,
-        reduce_weight,
-        slope,
-        expand_weight,
-        d_second,
-        normed,
-        inverse,
-        first_gain,
-        for_core,
-        [lefts_got],
-    )
-    (for_core,) = tie([for_core], [output_got])
-    grads, kept, sent, attend_sums = attend_back(bits, d_branch, output_weight, probs, q, k, v, allowed, [for_core])
+    grads, kept, sent, attend_sums = attend_back(bits, d_branch, output_weight, probs, q, k, v, allowed, [output])
     block_parts = (inner_sum, middle, features, time_outer)
     if tuned:
-        (hidden_got,) = tie([swapped(for_core, core)], [grads])
-        (sent,) = tie([sent], [hidden_got])
-        small, small_sent = pair_grad(bits, lefts, kept, lefts_got, swapped(sent, core), [])
+        (sent,) = tie([sent], [output_got])
+        sent_got = swapped(sent, core)
+        (for_core,) = tie([for_core], [sent_got])
+        hidden_got = swapped(for_core, core)
+        small, small_sent = pair_grad(bits, lefts, kept, lefts_got, sent_got, [for_core])
+        (small_sent,) = tie([small_sent], [hidden_got])
         small_got = crossed(small_sent, True)
-        hidden, hidden_sent = hidden_grad(bits, activated, d_reduced, d_expanded, mixed_low, hidden_got, [small])
+        hidden, hidden_sent = hidden_grad(bits, activated, d_reduced, d_expanded, mixed_low, hidden_got, [small_sent])
         (small_got,) = tie([small_got], [hidden])
+        hidden_got = crossed(hidden_sent, True)
         small, small_sent = halved(small, small_got, second)
         small_got = crossed(small_sent, False)
         d_rows, d_time = input_grad(grads, query_weight, key_weight, value_weight, d_first, [small_sent])
         (small_got,) = tie([small_got], [d_rows])
-        small, small_sent = halved(small, small_got, z & 1)
-        small_got = swapped(small_sent, low_far)
-        hidden_sent, d_rows, d_time = tie([hidden_sent, d_rows, d_time], [small_sent])
-        hidden_got = crossed(hidden_sent, True)
+        small, small_sent = halved(small, small_got, third)
+        small_got = lined(small_sent, True)
+        d_rows, d_time = tie([d_rows, d_time], [small_sent])
         input_got = swapped(d_rows[CAP:], side)
-        block = block_rows(bits, attend_sums, first_sums, second_sums, expand_bias_grad, d_time, *block_parts)
-        small, small_sent = halved(small, small_got, z >> 1)
-        share = plus(small, swapped(small_sent, high_far)).reshape(SHARE, D)
-        data, block = longer(share, block, lambda value: swapped(value, high_far), False)
-        data, block = longer(data, block, lambda value: swapped(value, low_far), False)
+        block = block_rows(bits, attend_sums, layer_sums, expand_bias_grad, d_time, *block_parts)
+        small, small_sent = halved(small, small_got, fourth)
+        small_got = lined(small_sent, False)
+        hidden_got, input_got = tie([hidden_got, input_got], [small_sent])
         hidden, hidden_sent = halved(hidden, hidden_got, second)
         hidden_got = crossed(hidden_sent, False)
-        (data,) = tie([data], [hidden_sent])
+        (small_got,) = tie([small_got], [hidden_sent])
+        share = plus(small, small_got).reshape(SHARE, D)
+        data, block = longer(share, block, lambda value: lined(value, False), False)
+        (hidden_got,) = tie([hidden_got], [data])
+        hidden, hidden_sent = halved(hidden, hidden_got, third)
+        hidden_got = lined(hidden_sent, True)
+        wait = lambda value: tie([value], [hidden_sent])[0]
+        data, block = longer(data, block, lambda value: wait(lined(value, True)), False)
         data, block = longer(data, block, lambda value: crossed(value, False), True)
-        hidden, hidden_sent = halved(hidden, hidden_got, z & 1)
-        hidden_got = swapped(hidden_sent, low_far)
-        (data,) = tie([data], [hidden_sent])
         message = jnp.concatenate([data, block])
         turned = crossed(message, True)
         message_far = swapped(message, core)
-        outs = unpack(bits, message, message_far, 0, ())
-        hidden, hidden_sent = halved(hidden, hidden_got, z >> 1)
-        hidden_got = swapped(hidden_sent, high_far)
-        turned_far = swapped(turned, core)
-        outs = unpack(bits, turned, turned_far, 1, outs)
-        *vectors, expand_bias_grad, inner, inner_bias, outer, outer_bias = finish(message, turned, message_far, turned_far)
-        grad_query, grad_key, grad_value, grad_output = [out.reshape(D, D) for out in outs]
+        hidden_got, output, output_got, d_rows, input_got = tie([hidden_got, output, output_got, d_rows, input_got], [message])
+        hidden, hidden_sent = halved(hidden, hidden_got, fourth)
+        hidden_got = lined(hidden_sent, False)
+        outs = first_unpack(bits, message, message_far)
+        output, input_grad_rows = both_sequences(output, output_got), both_sequences(d_rows, input_got)
         shares = (hidden.astype(f32) + hidden_got.astype(f32))[0]
         reduce_share, expand_share = shares[0], shares[1]
-        input_grad_rows = both_sequences(d_rows, input_got)
+        (turned,) = tie([turned], [outs[0], output, input_grad_rows, shares])
+        turned_far = swapped(turned, core)
+        *matrices, expand_bias_grad, inner, inner_bias, outer, outer_bias = finish(
+            bits, turned, turned_far, message, message_far, outs
+        )
+        grad_query, grad_key, grad_value, grad_output = [out.reshape(D, D) for out in matrices[:4]]
+        vectors = matrices[4:]
     else:
         d_rows, d_time = input_grad(grads, query_weight, key_weight, value_weight, d_first, ())
         reduce_parts, expand_parts, pairs = [], [], []
@@ -936,11 +923,12 @@
         small = gathered(small_share)[jnp.arange(devices) ^ me].astype(f32).reshape(4, D, D)
         grad_query, grad_key, grad_value, grad_output = [small[at] for at in range(4)]
         vectors, expand_bias_grad, inner, inner_bias, outer, outer_bias = everyones(
-            attend_sums + first_sums + second_sums, expand_bias_grad, d_time, *block_parts
+            attend_sums + layer_sums, expand_bias_grad, d_time, *block_parts
         )
         input_grad_rows = both_sequences(d_rows, swapped(d_rows[CAP:], side))
+        output = both_sequences(output, output_got)
     return (
-        both_sequences(output, output_got),
+        output,
         input_grad_rows,
         grad_query,
         vectors[0],

time: 256 us -> 224 us (0.88)
  waiting for transfers between devices: 74.6 us -> 49.2 us
  local copies, waits for them, and re-layouts: 12 us -> 23.6 us
  Pallas kernels: 118 us -> 107 us
  starting transfers between devices: 29.4 us -> 24.1 us
    ppermute x15 -> x9, waiting for transfers between devices: 36.7 us -> 6.06 us  [swapped(): lax.ppermute(value, axis, [(i, i ^ 1 << bit) for i in range(lax.axis_size...]
    ppermute x0 -> x6, waiting for transfers between devices: none -> 23.1 us  [lined(): return lax.ppermute(value, everywhere, pairs)]
    ppermute x6, waiting for transfers between devices: 37.9 us -> 20 us  [crossed(): return lax.ppermute(value, everywhere, pairs)]
    ppermute x15 -> x9, starting transfers between devices: 18.9 us -> 7.43 us  [swapped(): lax.ppermute(value, axis, [(i, i ^ 1 << bit) for i in range(lax.axis_size...]
    pallas_call x14 -> x12, Pallas kernels: 118 us -> 107 us  [run(): pl.pallas_call(wrapped, grid_spec=pltpu.PrefetchScalarGridSpec(num_scalar...]
    unnamed x38 -> x58, local copies, waits for them, and re-layouts: 3.65 us -> 13.8 us
    ppermute x0 -> x6, starting transfers between devices: none -> 9.53 us  [lined(): return lax.ppermute(value, everywhere, pairs)]
    convert_element_type x7, other arithmetic: 8.52 us -> 12 us  [plus(): return (left.astype(f32) + right.astype(f32)).astype(bf16)]
  transfers between devices with their start and end apart: 21 -> 21, of which waited for: 12 -> 13; matrix products, arithmetic and copies ran while one was open for 5% -> 11% of each run, Pallas kernels for 41% -> 45%
where the time goes in v1:
time: 224 us; the launch traced here: 223 us
  Pallas kernels  107 us (48%)
  waiting for transfers between devices  49.2 us (22%)
  starting transfers between devices  24.1 us (11%)
  local copies, waits for them, and re-layouts  23.6 us (11%)
  other arithmetic  18 us (8%)
    pallas_call x12, Pallas kernels, run(): pl.pallas_call(wrapped, grid_spec=pltpu.PrefetchScalarGridSpec(num_scalar...  107 us
    ppermute x6, waiting for transfers between devices, lined(): return lax.ppermute(value, everywhere, pairs)  23.1 us
    ppermute x6, waiting for transfers between devices, crossed(): return lax.ppermute(value, everywhere, pairs)  20 us
    unnamed x58, local copies, waits for them, and re-layouts  13.8 us
    convert_element_type x7, other arithmetic, plus(): return (left.astype(f32) + right.astype(f32)).astype(bf16)  12 us
    ppermute x6, starting transfers between devices, lined(): return lax.ppermute(value, everywhere, pairs)  9.53 us
    ppermute x9, starting transfers between devices, swapped(): lax.ppermute(value, axis, [(i, i ^ 1 << bit) for i in range(lax.axis_size...  7.43 us
    ppermute x6, starting transfers between devices, crossed(): return lax.ppermute(value, everywhere, pairs)  7.12 us
  transfers between devices with their start and end apart: 21, of which 13 were waited for; matrix products, arithmetic and copies ran while one was open for 11% of the time, Pallas kernels for 45%

profile of v1, /device:TPU:0, one launch (start us, length us, event | category | flops | bytes accessed | tf_op | source)
XLA Modules:
  0.0 222.8 jit_solution(5784290056588083468)
XLA Ops:
  2.6 3.0 %collective-permute-start = (bf16[256,768]{1,0:T(8,128)(2,1)S(1)}, bf16[256,768]{1,0:T(8,128)(2,1)S(1)}, u32[]{:S(2)}, u32[]{:S(2)}) collective-permute-start(bf16[256,768]{1,0:T(8,128)(2,1)S(1)} %get-tuple-element.171), channel_id=1, source_target_pairs={{0,16},{16,0},{1,17},{17,1},{2,18},{18,2},{3,19},{19,3},{4,20},{20... | collective-permute-start | bytes 1179656 | tf_op jit(solution)/shard_map/ppermute | solution.py:34
  6.1 3.7 %shard_map.400 = (f32[1,128]{1,0:T(1,128)}, f32[1,512]{1,0:T(1,128)}, f32[1,512]{1,0:T(1,128)}, f32[1,768]{1,0:T(1,128)}, f32[512,1]{1,0:T(8,128)}, /*index=5*/f32[512,1]{1,0:T(8,128)}, f32[512,1]{1,0:T(8,128)}) custom-call(s32[8]{0:T(128)} %stack.63.refs_0_, s32[2]{0:T(128)} %refs_1_.2, s32[2]{0:T(128)} %refs_2_.2, s32[2]{0:T(128)} %refs_3_.5, ...), custom_call_target="tpu_custom_call" | custom-call | bytes 940544 | tf_op jit(solution)/shard_map/pallas_call | solution.py:162
  9.9 4.7 %shard_map.401 = (bf16[256,768]{1,0:T(8,128)(2,1)}, bf16[256,768]{1,0:T(8,128)(2,1)}, bf16[256,768]{1,0:T(8,128)(2,1)}, bf16[256,768]{1,0:T(8,128)(2,1)}) custom-call(bf16[256,768]{1,0:T(8,128)(2,1)} %get-tuple-element.172.refs_0_.refs_2_, f32[1,768]{1,0:T(1,128)} %get-tuple-element.91.refs_1_.refs_4_, f32[512,1]{1,0:T(8,128)} %get-tuple-element.92.refs_2_.refs_11_, ...), custom_call_target="tpu_custom_call" | custom-call | flops 905969664 | bytes 5516288 | tf_op jit(solution)/shard_map/pallas_call | solution.py:162
  18.0 4.9 %shard_map.403 = (bf16[256,768]{1,0:T(8,128)(2,1)}, bf16[256,768]{1,0:T(8,128)(2,1)}, bf16[256,768]{1,0:T(8,128)(2,1)}, bf16[256,768]{1,0:T(8,128)(2,1)}) custom-call(bf16[256,768]{1,0:T(8,128)(2,1)} %shard_map.402.refs_0_.refs_3_, f32[1,768]{1,0:T(1,128)} %get-tuple-element.91.refs_1_.refs_4_, f32[512,1]{1,0:T(8,128)} %get-tuple-element.92.refs_2_.refs_11_, ...), custom_call_target="tpu_custom_call" | custom-call | flops 905969664 | bytes 5516288 | tf_op jit(solution)/shard_map/pallas_call | solution.py:162
  22.9 11.5 %shard_map.404 = (bf16[512,768]{1,0:T(8,128)(2,1)}, bf16[2,512,768]{2,1,0:T(8,128)(2,1)}, bf16[12,512,512]{2,1,0:T(8,128)(2,1)}) custom-call(bf16[256,768]{1,0:T(8,128)(2,1)} %get-tuple-element.93.refs_1_.refs_0_.refs_5_, bf16[256,768]{1,0:T(8,128)(2,1)} %get-tuple-element.95.refs_1_.refs_6_, bf16[256,768]{1,0:T(8,128)(2,1)} %get-tuple-element.96.refs_2_.refs_7_, ...), custom_call_target="tpu_custom_call" | custom-call | flops 3221225472 | bytes 11798528 | tf_op jit(solution)/shard_map/pallas_call | solution.py:162
  35.1 27.2 %shard_map.405 = (bf16[512,768]{1,0:T(8,128)(2,1)}, bf16[512,4608]{1,0:T(8,128)(2,1)}, bf16[512,1536]{1,0:T(8,128)(2,1)}, bf16[512,1536]{1,0:T(8,128)(2,1)}, bf1...) custom-call(s32[8]{0:T(128)} %stack.63.refs_0_, ...), custom_call_target="tpu_custom_call" | custom-call | flops 10267656192 | bytes 25631744 | tf_op jit(solution)/shard_map/pallas_call | solution.py:162
  64.2 15.8 %shard_map.408 = (bf16[3,512,768]{2,1,0:T(8,128)(2,1)}, bf16[2,512,768]{2,1,0:T(8,128)(2,1)}, bf16[2,512,768]{2,1,0:T(8,128)(2,1)}, f32[8,768]{1,0:T(8,128)}) custom-call(s32[8]{0:T(128)} %stack.63.refs_0_, bf16[512,768]{1,0:T(8,128)(2,1)} %get-tuple-element.111.refs_1_.refs_2_, bf16[512,768]{1,0:T(8,128)(2,1)} %get-tuple-element.111.refs_1_.refs_2_, ...), custom_call_target="tpu_custom_call" | custom-call | flops 8053063680 | bytes 16934912 | tf_op jit(solution)/shard_map/pallas_call | solution.py:162
  81.2 3.2 %collective-permute-done.4.refs_1_.refs_4_ = bf16[2,512,768]{2,1,0:T(8,128)(2,1)S(1)} collective-permute-done((bf16[2,512,768]{2,1,0:T(8,128)(2,1)}, bf16[2,512,768]{2,1,0:T(8,128)(2,1)S(1)}, u32[]{:S(2)}, u32[]{:S(2)}) %collective-permute-start.4) | collective-permute-done | bytes 1572896 | tf_op jit(solution)/shard_map/ppermute | solution.py:34
  85.9 6.6 %shard_map.411 = (bf16[8,2,48,768]{3,2,1,0:T(8,128)(2,1)}, bf16[8,2,48,768]{3,2,1,0:T(8,128)(2,1)}) custom-call(s32[8]{0:T(128)} %stack.63.refs_0_, bf16[2,512,768]{2,1,0:T(8,128)(2,1)} %shard_map.406.refs_1_, bf16[2,512,768]{2,1,0:T(8,128)(2,1)} %get-tuple-element.116.refs_2_, bf16[2,512,768]{2,1,0:T(8,128)(2,1)} %collective-permute-done.2.refs_1_.refs_3_, ...), custom_call_target="tpu_custom_call" | custom-call | flops 2415919104 | bytes 8650752 | tf_op jit(solution)/shard_map/pallas_call | solution.py:162
  95.2 12.4 %shard_map.413 = (bf16[8,2,96,768]{3,2,1,0:T(8,128)(2,1)}, bf16[8,2,96,768]{3,2,1,0:T(8,128)(2,1)}) custom-call(s32[8]{0:T(128)} %stack.63.refs_0_, bf16[512,1536]{1,0:T(8,128)(2,1)} %get-tuple-element.106.refs_1_, bf16[512,768]{1,0:T(8,128)(2,1)} %get-tuple-element.107.refs_2_, bf16[512,1536]{1,0:T(8,128)(2,1)} %get-tuple-element.108.refs_3_, ...), custom_call_target="tpu_custom_call" | custom-call | flops 4831838208 | bytes 28311552 | tf_op jit(solution)/shard_map/pallas_call | solution.py:162
  115.2 6.3 %shard_map.415 = (bf16[512,768]{1,0:T(8,128)(2,1)}, f32[1,768]{1,0:T(1,128)}) custom-call(bf16[3,512,768]{2,1,0:T(8,128)(2,1)} %get-tuple-element.120.refs_0_, bf16[768,768]{1,0:T(8,128)(2,1)} %refs_1_.3, bf16[768,768]{1,0:T(8,128)(2,1)} %refs_2_.3, bf16[768,768]{1,0:T(8,128)(2,1)} %refs_3_.9, f32[512,768]{1,0:T(8,128)} %get-tuple-element.121.refs_4_, ...), custom_call_target="tpu_custom_call" | custom-call | flops 1811939328 | bytes 8260608 | tf_op jit(solution)/shard_map/pallas_call | solution.py:162
  121.5 9.0 %collective-permute-done.8.refs_0_ = bf16[4,2,48,768]{3,2,1,0:T(8,128)(2,1)} collective-permute-done((bf16[4,2,48,768]{3,2,1,0:T(8,128)(2,1)}, bf16[4,2,48,768]{3,2,1,0:T(8,128)(2,1)}, u32[]{:S(2)}, u32[]{:S(2)}) %collective-permute-start.8) | collective-permute-done | bytes 589856 | tf_op jit(solution)/shard_map/ppermute | solution.py:598
  135.8 4.9 %collective-permute-done.10 = bf16[2,2,48,768]{3,2,1,0:T(8,128)(2,1)S(1)} collective-permute-done((bf16[2,2,48,768]{3,2,1,0:T(8,128)(2,1)S(1)}, bf16[2,2,48,768]{3,2,1,0:T(8,128)(2,1)S(1)}, u32[]{:S(2)}, u32[]{:S(2)}) %collective-permute-start.10) | collective-permute-done | bytes 294944 | tf_op jit(solution)/shard_map/ppermute | solution.py:605
  141.5 2.4 %collective-permute-start.12 = (bf16[1,2,48,768]{3,2,1,0:T(8,128)(2,1)}, bf16[1,2,48,768]{3,2,1,0:T(8,128)(2,1)}, u32[]{:S(2)}, u32[]{:S(2)}) collective-permute-start(bf16[1,2,48,768]{3,2,1,0:T(8,128)(2,1)} %fusion.7.refs_2_), channel_id=1, source_target_pairs={{0,8},{1,5},{2,10},{3,7},{4,12},{5,1},{6,14},{7,3},{8,0},{9,13},{1... | collective-permute-start | bytes 442376 | tf_op jit(solution)/shard_map/ppermute | solution.py:605
  143.9 3.9 %shard_map.420 = bf16[32,768]{1,0:T(8,128)(2,1)} custom-call(s32[8]{0:T(128)} %stack.63.refs_0_, f32[8,768]{1,0:T(8,128)} %get-tuple-element.127.refs_1_, f32[8,768]{1,0:T(8,128)} %get-tuple-element.128.refs_2_, f32[4,1,768]{2,1,0:T(1,128)} %get-tuple-element.129.refs_3_, f32[1,768]{1,0:T(1,128)} %get-tuple-element.130.refs_4_, ...), custom_call_target="tpu_custom_call" | custom-call | bytes 904704 | tf_op jit(solution)/shard_map/pallas_call | solution.py:162
  149.6 3.3 %add_convert_fusion.1 = (bf16[1,4,2,96,768]{4,3,2,1,0:T(8,128)(2,1)}, bf16[4,2,96,768]{3,2,1,0:T(8,128)(2,1)S(1)}) fusion(bf16[2,4,2,96,768]{4,3,2,1,0:T(8,128)(2,1)} %bitcast.20, s32[]{:T(128)S(6)} %select_n.95, bf16[2,4,2,96,768]{4,3,2,1,0:T(8,128)(2,1)S(1)} %bitcast.63, s32[]{:T(128)S(6)} %select_n.96), kind=kLoop, calls=%fused_computation.1 | loop fusion | flops 4718592 | bytes 7077896 | tf_op jit(solution)/shard_map/convert_element_type | solution.py:609
  156.5 6.0 %collective-permute-done.13 = bf16[128,768]{1,0:T(8,128)(2,1)S(1)} collective-permute-done((bf16[128,768]{1,0:T(8,128)(2,1)S(1)}, bf16[128,768]{1,0:T(8,128)(2,1)S(1)}, u32[]{:S(2)}, u32[]{:S(2)}) %collective-permute-start.13) | collective-permute-done | bytes 196640 | tf_op jit(solution)/shard_map/ppermute | solution.py:605
  163.9 3.8 %collective-permute-start.15 = (bf16[224,768]{1,0:T(8,128)(2,1)}, bf16[224,768]{1,0:T(8,128)(2,1)}, u32[]{:S(2)}, u32[]{:S(2)}) collective-permute-start(bf16[224,768]{1,0:T(8,128)(2,1)} %pad_maximum_fusion.1), channel_id=1, source_target_pairs={{0,4},{1,9},{2,6},{3,11},{4,0},{5,13},{6,2},{7,15},{8,12},{9,1},{1... | collective-permute-start | bytes 1032200 | tf_op jit(solution)/shard_map/ppermute | solution.py:605
  171.5 2.3 %add_convert_fusion.2 = (bf16[1,2,2,96,768]{4,3,2,1,0:T(8,128)(2,1)S(1)}, bf16[2,2,96,768]{3,2,1,0:T(8,128)(2,1)}) fusion(bf16[2,2,2,96,768]{4,3,2,1,0:T(8,128)(2,1)} %bitcast.71, s32[]{:T(128)S(6)} %select_n.99, bf16[2,2,2,96,768]{4,3,2,1,0:T(8,128)(2,1)S(1)} %bitcast.72, s32[]{:T(128)S(6)} %select_n.98), kind=kLoop, calls=%fused_computation.3 | loop fusion | flops 2359296 | bytes 3538952 | tf_op jit(solution)/shard_map/convert_element_type | solution.py:609
  173.8 2.5 %collective-permute-done.15.refs_0_ = bf16[224,768]{1,0:T(8,128)(2,1)} collective-permute-done((bf16[224,768]{1,0:T(8,128)(2,1)}, bf16[224,768]{1,0:T(8,128)(2,1)}, u32[]{:S(2)}, u32[]{:S(2)}) %collective-permute-start.15) | collective-permute-done | bytes 344096 | tf_op jit(solution)/shard_map/ppermute | solution.py:605
  181.2 8.2 %collective-permute-done.16 = bf16[416,768]{1,0:T(8,128)(2,1)S(1)} collective-permute-done((bf16[416,768]{1,0:T(8,128)(2,1)S(1)}, bf16[416,768]{1,0:T(8,128)(2,1)S(1)}, u32[]{:S(2)}, u32[]{:S(2)}) %collective-permute-start.16) | collective-permute-done | bytes 639008 | tf_op jit(solution)/shard_map/ppermute | solution.py:598
  201.0 7.5 %collective-permute-done.19 = bf16[1,2,96,768]{3,2,1,0:T(8,128)(2,1)S(1)} collective-permute-done((bf16[1,2,96,768]{3,2,1,0:T(8,128)(2,1)S(1)}, bf16[1,2,96,768]{3,2,1,0:T(8,128)(2,1)S(1)}, u32[]{:S(2)}, u32[]{:S(2)}) %collective-permute-start.19) | collective-permute-done | bytes 294944 | tf_op jit(solution)/shard_map/ppermute | solution.py:605
  209.4 4.3 %shard_map.424 = (f32[16,48,768]{2,1,0:T(8,128)}, f32[16,48,768]{2,1,0:T(8,128)}, f32[16,48,768]{2,1,0:T(8,128)}, f32[16,48,768]{2,1,0:T(8,128)}) custom-call(s32[8]{0:T(128)} %stack.63.refs_0_, bf16[816,768]{1,0:T(8,128)(2,1)} %slice_dynamic-update-slice_fusion.1.refs_5_.refs_1_.refs_3_, bf16[816,768]{1,0:T(8,128)(2,1)} %collective-permute-done.18.refs_2_.refs_4_), custom_call_target="tpu_custom_call" | custom-call | bytes 11943936 | tf_op jit(solution)/shard_map/pallas_call | solution.py:162
  217.1 5.5 %shard_map.426 = (f32[16,48,768]{2,1,0:T(8,128)}, f32[16,48,768]{2,1,0:T(8,128)}, f32[16,48,768]{2,1,0:T(8,128)}, f32[16,48,768]{2,1,0:T(8,128)}, f32[768]{0:T(1...) custom-call(s32[8]{0:T(128)} %stack.63.refs_0_, ...), custom_call_target="tpu_custom_call", output_to_operand_aliasing={{0}: (7, {}), {1}: (8, {}), {2}: (9, {}), {3}: (10, {})} | custom-call | bytes 28271616 | tf_op jit(solution)/shard_map/pallas_call | solution.py:162
  (129 shorter events, 58.8 us)
Async XLA Ops:
  2.6 12.1 %collective-permute-start = (bf16[256,768]{1,0:T(8,128)(2,1)S(1)}, bf16[256,768]{1,0:T(8,128)(2,1)S(1)}, u32[]{:S(2)}, u32[]{:S(2)}) collective-permute-start(bf16[256,768]{1,0:T(8,128)(2,1)S(1)} %get-tuple-element.171), channel_id=1, source_target_pairs={{0,16},{16,0},{1,17},{17,1},{2,18},{18,2},{3,19},{19,3},{4,20},{20... | collective-permute-start | bytes 1179656 | tf_op jit(solution)/shard_map/ppermute | solution.py:34
  16.7 17.7 %collective-permute-start.1 = (bf16[256,768]{1,0:T(8,128)(2,1)S(1)}, bf16[256,768]{1,0:T(8,128)(2,1)S(1)}, u32[]{:S(2)}, u32[]{:S(2)}) collective-permute-start(bf16[256,768]{1,0:T(8,128)(2,1)S(1)} %get-tuple-element.169), channel_id=1, source_target_pairs={{0,16},{16,0},{1,17},{17,1},{2,18},{18,2},{3,19},{19,3},{4,20},{20... | collective-permute-start | bytes 1179656 | tf_op jit(solution)/shard_map/ppermute | solution.py:34
  35.1 27.2 %collective-permute-start.2 = (bf16[2,512,768]{2,1,0:T(8,128)(2,1)}, bf16[2,512,768]{2,1,0:T(8,128)(2,1)}, u32[]{:S(2)}, u32[]{:S(2)}) collective-permute-start(bf16[2,512,768]{2,1,0:T(8,128)(2,1)} %shard_map.406.refs_1_), channel_id=1, source_target_pairs={{0,1},{1,0},{2,3},{3,2},{4,5},{5,4},{6,7},{7,6},{8,9},{9,8},{10,11... | collective-permute-start | bytes 4718600 | tf_op jit(solution)/shard_map/ppermute | solution.py:34
  63.4 16.6 %collective-permute-start.3 = (bf16[256,768]{1,0:T(8,128)(2,1)S(1)}, bf16[256,768]{1,0:T(8,128)(2,1)S(1)}, u32[]{:S(2)}, u32[]{:S(2)}) collective-permute-start(bf16[256,768]{1,0:T(8,128)(2,1)S(1)} %slice.65), channel_id=1, source_target_pairs={{0,16},{16,0},{1,17},{17,1},{2,18},{18,2},{3,19},{19,3},{4,20},{20... | collective-permute-start | bytes 1179656 | tf_op jit(solution)/shard_map/ppermute | solution.py:34
  80.7 3.7 %collective-permute-start.4 = (bf16[2,512,768]{2,1,0:T(8,128)(2,1)}, bf16[2,512,768]{2,1,0:T(8,128)(2,1)S(1)}, u32[]{:S(2)}, u32[]{:S(2)}) collective-permute-start(bf16[2,512,768]{2,1,0:T(8,128)(2,1)} %shard_map.409), channel_id=1, source_target_pairs={{0,1},{1,0},{2,3},{3,2},{4,5},{5,4},{6,7},{7,6},{8,9},{9,8},{10,11... | collective-permute-start | bytes 4718600 | tf_op jit(solution)/shard_map/ppermute | solution.py:34
  85.6 8.3 %collective-permute-start.5 = (bf16[512,4608]{1,0:T(8,128)(2,1)}, bf16[512,4608]{1,0:T(8,128)(2,1)}, u32[]{:S(2)}, u32[]{:S(2)}) collective-permute-start(bf16[512,4608]{1,0:T(8,128)(2,1)} %shard_map.410.refs_5_), channel_id=1, source_target_pairs={{0,1},{1,0},{2,3},{3,2},{4,5},{5,4},{6,7},{7,6},{8,9},{9,8},{10,11... | collective-permute-start | bytes 14155784 | tf_op jit(solution)/shard_map/ppermute | solution.py:34
  93.8 16.5 %collective-permute-start.7 = (bf16[8,2,48,768]{3,2,1,0:T(8,128)(2,1)}, bf16[8,2,48,768]{3,2,1,0:T(8,128)(2,1)}, u32[]{:S(2)}, u32[]{:S(2)}) collective-permute-start(bf16[8,2,48,768]{3,2,1,0:T(8,128)(2,1)} %shard_map.412.refs_9_), channel_id=1, source_target_pairs={{0,2},{1,17},{2,0},{3,19},{4,6},{5,21},{6,4},{7,23},{8,10},{9,25},... | collective-permute-start | bytes 3538952 | tf_op jit(solution)/shard_map/ppermute | solution.py:598
  107.5 40.2 %collective-permute-start.6 = (bf16[8,2,96,768]{3,2,1,0:T(8,128)(2,1)}, bf16[8,2,96,768]{3,2,1,0:T(8,128)(2,1)}, u32[]{:S(2)}, u32[]{:S(2)}) collective-permute-start(bf16[8,2,96,768]{3,2,1,0:T(8,128)(2,1)} %get-tuple-element.119), channel_id=1, source_target_pairs={{0,2},{1,17},{2,0},{3,19},{4,6},{5,21},{6,4},{7,23},{8,10},{9,25},... | collective-permute-start | bytes 7077896 | tf_op jit(solution)/shard_map/ppermute | solution.py:598
  113.9 16.6 %collective-permute-start.8 = (bf16[4,2,48,768]{3,2,1,0:T(8,128)(2,1)}, bf16[4,2,48,768]{3,2,1,0:T(8,128)(2,1)}, u32[]{:S(2)}, u32[]{:S(2)}) collective-permute-start(bf16[4,2,48,768]{3,2,1,0:T(8,128)(2,1)} %get-tuple-element.166.refs_5_), channel_id=1, source_target_pairs={{0,16},{1,3},{2,18},{3,1},{4,20},{5,7},{6,22},{7,5},{8,24},{9,11},... | collective-permute-start | bytes 1769480 | tf_op jit(solution)/shard_map/ppermute | solution.py:598
  131.7 9.0 %copy-start.18 = (bf16[1,2,2,48,768]{4,3,2,1,0:T(8,128)(2,1)}, bf16[1,2,2,48,768]{4,3,2,1,0:T(8,128)(2,1)S(1)}, u32[]{:S(2)}) copy-start(bf16[1,2,2,48,768]{4,3,2,1,0:T(8,128)(2,1)S(1)} %get-tuple-element.167) | copy-start | bytes 884740
  131.7 9.0 %collective-permute-start.10 = (bf16[2,2,48,768]{3,2,1,0:T(8,128)(2,1)S(1)}, bf16[2,2,48,768]{3,2,1,0:T(8,128)(2,1)S(1)}, u32[]{:S(2)}, u32[]{:S(2)}) collective-permute-start(bf16[2,2,48,768]{3,2,1,0:T(8,128)(2,1)S(1)} %get-tuple-element.168.refs_2_), channel_id=1, source_target_pairs={{0,4},{1,9},{2,6},{3,11},{4,0},{5,13},{6,2},{7,15},{8,12},{9,1},{1... | collective-permute-start | bytes 884744 | tf_op jit(solution)/shard_map/ppermute | solution.py:605
  134.3 13.5 %collective-permute-start.9 = (bf16[256,768]{1,0:T(8,128)(2,1)S(1)}, bf16[256,768]{1,0:T(8,128)(2,1)S(1)}, u32[]{:S(2)}, u32[]{:S(2)}) collective-permute-start(bf16[256,768]{1,0:T(8,128)(2,1)S(1)} %slice.51), channel_id=1, source_target_pairs={{0,16},{16,0},{1,17},{17,1},{2,18},{18,2},{3,19},{19,3},{4,20},{20... | collective-permute-start | bytes 1179656 | tf_op jit(solution)/shard_map/ppermute | solution.py:34
  141.5 12.9 %collective-permute-start.12 = (bf16[1,2,48,768]{3,2,1,0:T(8,128)(2,1)}, bf16[1,2,48,768]{3,2,1,0:T(8,128)(2,1)}, u32[]{:S(2)}, u32[]{:S(2)}) collective-permute-start(bf16[1,2,48,768]{3,2,1,0:T(8,128)(2,1)} %fusion.7.refs_2_), channel_id=1, source_target_pairs={{0,8},{1,5},{2,10},{3,7},{4,12},{5,1},{6,14},{7,3},{8,0},{9,13},{1... | collective-permute-start | bytes 442376 | tf_op jit(solution)/shard_map/ppermute | solution.py:605
  152.9 16.3 %collective-permute-start.11 = (bf16[4,2,96,768]{3,2,1,0:T(8,128)(2,1)S(1)}, bf16[4,2,96,768]{3,2,1,0:T(8,128)(2,1)S(1)}, u32[]{:S(2)}, u32[]{:S(2)}) collective-permute-start(bf16[4,2,96,768]{3,2,1,0:T(8,128)(2,1)S(1)} %get-tuple-element.162.refs_1_), channel_id=1, source_target_pairs={{0,16},{1,3},{2,18},{3,1},{4,20},{5,7},{6,22},{7,5},{8,24},{9,11},... | collective-permute-start | bytes 3538952 | tf_op jit(solution)/shard_map/ppermute | solution.py:598
  155.4 7.0 %collective-permute-start.13 = (bf16[128,768]{1,0:T(8,128)(2,1)S(1)}, bf16[128,768]{1,0:T(8,128)(2,1)S(1)}, u32[]{:S(2)}, u32[]{:S(2)}) collective-permute-start(bf16[128,768]{1,0:T(8,128)(2,1)S(1)} %pad_maximum_fusion.3), channel_id=1, source_target_pairs={{0,8},{1,5},{2,10},{3,7},{4,12},{5,1},{6,14},{7,3},{8,0},{9,13},{1... | collective-permute-start | bytes 589832 | tf_op jit(solution)/shard_map/ppermute | solution.py:605
  162.5 6.0 %copy-start.22 = (bf16[32,768]{1,0:T(8,128)(2,1)}, bf16[32,768]{1,0:T(8,128)(2,1)S(1)}, u32[]{:S(2)}) copy-start(bf16[32,768]{1,0:T(8,128)(2,1)S(1)} %reduce-precision_convert_fusion.1) | copy-start | bytes 147460
  163.9 12.4 %collective-permute-start.15 = (bf16[224,768]{1,0:T(8,128)(2,1)}, bf16[224,768]{1,0:T(8,128)(2,1)}, u32[]{:S(2)}, u32[]{:S(2)}) collective-permute-start(bf16[224,768]{1,0:T(8,128)(2,1)} %pad_maximum_fusion.1), channel_id=1, source_target_pairs={{0,4},{1,9},{2,6},{3,11},{4,0},{5,13},{6,2},{7,15},{8,12},{9,1},{1... | collective-permute-start | bytes 1032200 | tf_op jit(solution)/shard_map/ppermute | solution.py:605
  178.9 10.5 %collective-permute-start.16 = (bf16[416,768]{1,0:T(8,128)(2,1)S(1)}, bf16[416,768]{1,0:T(8,128)(2,1)S(1)}, u32[]{:S(2)}, u32[]{:S(2)}) collective-permute-start(bf16[416,768]{1,0:T(8,128)(2,1)S(1)} %pad_maximum_fusion), channel_id=1, source_target_pairs={{0,16},{1,3},{2,18},{3,1},{4,20},{5,7},{6,22},{7,5},{8,24},{9,11},... | collective-permute-start | bytes 1916936 | tf_op jit(solution)/shard_map/ppermute | solution.py:598
  179.9 15.9 %collective-permute-start.14 = (bf16[2,2,96,768]{3,2,1,0:T(8,128)(2,1)S(1)}, bf16[2,2,96,768]{3,2,1,0:T(8,128)(2,1)S(1)}, u32[]{:S(2)}, u32[]{:S(2)}) collective-permute-start(bf16[2,2,96,768]{3,2,1,0:T(8,128)(2,1)S(1)} %copy-done.12), channel_id=1, source_target_pairs={{0,4},{1,9},{2,6},{3,11},{4,0},{5,13},{6,2},{7,15},{8,12},{9,1},{1... | collective-permute-start | bytes 1769480 | tf_op jit(solution)/shard_map/ppermute | solution.py:605
  192.1 17.3 %collective-permute-start.18 = (bf16[816,768]{1,0:T(8,128)(2,1)}, bf16[816,768]{1,0:T(8,128)(2,1)}, u32[]{:S(2)}, u32[]{:S(2)}) collective-permute-start(bf16[816,768]{1,0:T(8,128)(2,1)} %slice_dynamic-update-slice_fusion.1.refs_5_.refs_1_.refs_3_), channel_id=1, source_target_pairs={{0,1},{1,0},{2,3},{3,2},{4,5},{5,4},{6,7},{7,6},{8,9},{9,8},{10,11... | collective-permute-start | bytes 3760136 | tf_op jit(solution)/shard_map/ppermute | solution.py:34
  192.1 21.6 %collective-permute-start.17 = (bf16[816,768]{1,0:T(8,128)(2,1)}, bf16[816,768]{1,0:T(8,128)(2,1)}, u32[]{:S(2)}, u32[]{:S(2)}) collective-permute-start(bf16[816,768]{1,0:T(8,128)(2,1)} %slice_dynamic-update-slice_fusion.1.refs_5_.refs_1_.refs_3_), channel_id=1, source_target_pairs={{0,2},{1,17},{2,0},{3,19},{4,6},{5,21},{6,4},{7,23},{8,10},{9,25},... | collective-permute-start | bytes 3760136 | tf_op jit(solution)/shard_map/ppermute | solution.py:598
  197.7 10.8 %collective-permute-start.19 = (bf16[1,2,96,768]{3,2,1,0:T(8,128)(2,1)S(1)}, bf16[1,2,96,768]{3,2,1,0:T(8,128)(2,1)S(1)}, u32[]{:S(2)}, u32[]{:S(2)}) collective-permute-start(bf16[1,2,96,768]{3,2,1,0:T(8,128)(2,1)S(1)} %fusion.3), channel_id=1, source_target_pairs={{0,8},{1,5},{2,10},{3,7},{4,12},{5,1},{6,14},{7,3},{8,0},{9,13},{1... | collective-permute-start | bytes 884744 | tf_op jit(solution)/shard_map/ppermute | solution.py:605
  199.0 9.5 %copy-start.14 = (bf16[2,2,96,768]{3,2,1,0:T(8,128)(2,1)S(1)}, bf16[2,2,96,768]{3,2,1,0:T(8,128)(2,1)}, u32[]{:S(2)}) copy-start(bf16[2,2,96,768]{3,2,1,0:T(8,128)(2,1)} %get-tuple-element.140) | copy-start | bytes 1769476
  213.8 3.4 %collective-permute-start.20 = (bf16[816,768]{1,0:T(8,128)(2,1)}, bf16[816,768]{1,0:T(8,128)(2,1)}, u32[]{:S(2)}, u32[]{:S(2)}) collective-permute-start(bf16[816,768]{1,0:T(8,128)(2,1)} %shard_map.425.refs_1_.refs_5_), channel_id=1, source_target_pairs={{0,1},{1,0},{2,3},{3,2},{4,5},{5,4},{6,7},{7,6},{8,9},{9,8},{10,11... | collective-permute-start | bytes 3760136 | tf_op jit(solution)/shard_map/ppermute | solution.py:34
  (24 other events, 43.2 us)

commit v2 on v1

--- a/solution.py
+++ b/solution.py
@@ -170,7 +170,7 @@
         ),
         out_shape=shapes,
         input_output_aliases=aliases or {},
-        compiler_params=pltpu.CompilerParams(vmem_limit_bytes=63 << 20),
+        compiler_params=pltpu.CompilerParams(vmem_limit_bytes=(63 << 20) + (960 << 10)),
         cost_estimate=pl.CostEstimate(flops=int(flops), bytes_accessed=sum(sizes), transcendentals=0),
     )(*scalars, *operands, *after)
 
@@ -187,6 +187,7 @@
         out_specs=[anywhere] * len(values),
         out_shape=[jax.ShapeDtypeStruct(value.shape, value.dtype) for value in values],
         input_output_aliases={k: k for k in range(len(values))},
+        compiler_params=pltpu.CompilerParams(vmem_limit_bytes=(63 << 20) + (960 << 10)),
     )(*values, *after)
 
 
@@ -207,8 +208,9 @@
     return jnp.sum(values, axis=0, keepdims=True)
 
 
-def prepare_body(bits, stamps, src_len, seq_len, flags, inner, inner_bias, outer, outer_bias, *outs):
-    features, inner_sum, middle, stamp, allowed, valid, masked = outs
+def prepare_body(bits, stamps, src_len, seq_len, flags, inner, inner_bias, outer, outer_bias, cotangent, *outs):
+    features, inner_sum, middle, stamp, allowed, valid, masked, cot_other = outs
+    cot_other[...] = cotangent[0]
     y = bits[2]
     lane = lax.broadcasted_iota(jnp.int32, (1, TDIM), 1)
     half = TDIM // 2
@@ -234,14 +236,15 @@
         masked[here] = (1.0 - inside * kept) * masked_score
 
 
-def prepare(bits, stamps, src_len, seq_len, flags, inner, inner_bias, outer, outer_bias):
+def prepare(bits, stamps, src_len, seq_len, flags, inner, inner_bias, outer, outer_bias, cotangent):
     return run(
         prepare_body,
         (1,),
-        (flags, inner, inner_bias, outer, outer_bias),
-        [whole(2, 2, CAP), whole(TDIM, TFF), vector(TFF), whole(TFF, D), vector(D)],
-        [((1, size), f32) for size in (TDIM, TFF, TFF, D)] + [((ROWS, 1), f32)] * 3,
-        [whole(1, size) for size in (TDIM, TFF, TFF, D)] + [whole(ROWS, 1)] * 3,
+        (flags, inner, inner_bias, outer, outer_bias, cotangent),
+        [whole(2, 2, CAP), whole(TDIM, TFF), vector(TFF), whole(TFF, D), vector(D)]
+        + [pl.BlockSpec((1, CAP, D), lambda j, bits, *at: (1 - bits[2], 0, 0))],
+        [((1, size), f32) for size in (TDIM, TFF, TFF, D)] + [((ROWS, 1), f32)] * 3 + [((CAP, D), bf16)],
+        [whole(1, size) for size in (TDIM, TFF, TFF, D)] + [whole(ROWS, 1)] * 3 + [whole(CAP, D)],
         0,
         scalars=(bits, stamps, src_len, seq_len),
     )
@@ -335,7 +338,7 @@
 
 def feed_forward_body(
     bits, attended, own, far, stamp, ow, ob, gain, shift, ew, eb, rw, rb, gain2, shift2, valid, cot_own, cot_far,
-    output, for_core, activated_own, expanded_own, mixed_low, d_reduced, bias_grad, d_first, d_branch, sums,
+    output, far_output, for_core, activated_own, expanded_own, mixed_low, d_reduced, bias_grad, d_first, d_branch, sums,
     total, normed, inverse, slope, columns,
 ):
     step = pl.program_id(0)
@@ -383,8 +386,9 @@
     def _():
         n2, inv = normalized(total[...])
         weight = valid[...]
-        output[...] = ((n2 * row(gain2) + row(shift2)) * weight).astype(bf16)
-        d_out = both(cot_own, cot_far).astype(f32) * weight
+        rows = ((n2 * row(gain2) + row(shift2)) * weight).astype(bf16)
+        output[...], far_output[...] = rows[:CAP], rows[CAP:]
+        d_out = jnp.concatenate([cot_own[0], cot_far[...]], axis=0).astype(f32) * weight
         back = norm_backward(d_out * row(gain2), n2, inv)
         low = back.astype(bf16)
         total[...] = back
@@ -427,10 +431,11 @@
         (attended, own, far, stamp, ow, ob, gain, shift, ew, eb, rw, rb, gain2, shift2, valid, cot_own, cot_far),
         [square, half, half, whole(1, D), whole(D, D), line, line, line]
         + [pl.BlockSpec((D, D), lambda j, *at: (0, j % tiles)), vector(FF), pl.BlockSpec((D, D), lambda j, *at: (j % tiles, 0))]
-        + [line, line, line, whole(ROWS, 1), half, half],
-        [((ROWS, D), bf16), (FOR_CORE, bf16), ((ROWS, FF // 2), bf16), ((ROWS, FF // 2), bf16), ((ROWS, D), bf16)]
+        + [line, line, line, whole(ROWS, 1), pl.BlockSpec((1, CAP, D), lambda j, bits: (bits[2], 0, 0)), half],
+        [((CAP, D), bf16)] * 2
+        + [(FOR_CORE, bf16), ((ROWS, FF // 2), bf16), ((ROWS, FF // 2), bf16), ((ROWS, D), bf16)]
         + [((ROWS, D), bf16), ((tiles, 1, D), f32), ((ROWS, D), f32), ((ROWS, D), bf16), ((8, D), f32)],
-        [square, whole(*FOR_CORE), forward, backward, square, square]
+        [half, half, whole(*FOR_CORE), forward, backward, square, square]
         + [pl.BlockSpec((1, 1, D), lambda j, *at: (jnp.maximum(j - tiles, 0), 0, 0)), square, square, whole(8, D)],
         2 * ROWS * D * (D + 4 * FF),
         scratch=[pltpu.VMEM((ROWS, D), f32)] * 2
@@ -564,9 +569,10 @@
     )
 
 
-def input_grad_body(grads, qw, kw, vw, d_first, d_rows, d_time):
+def input_grad_body(grads, qw, kw, vw, d_first, own_rows, far_rows, d_time):
     total = d_first[...] + nt(grads[0], qw[...]) + nt(grads[1], kw[...]) + nt(grads[2], vw[...])
-    d_rows[...] = total.astype(bf16)
+    low = total.astype(bf16)
+    own_rows[...], far_rows[...] = low[:CAP], low[CAP:]
     d_time[...] = row_sum(total)
 
 
@@ -577,8 +583,8 @@
         (D // tile,),
         (grads, qw, kw, vw, d_first),
         [whole(3, ROWS, D)] + [row_tile(tile, D)] * 3 + [column_tile(ROWS, tile)],
-        [((ROWS, D), bf16), ((1, D), f32)],
-        [column_tile(ROWS, tile), column_tile(1, tile)],
+        [((CAP, D), bf16)] * 2 + [((1, D), f32)],
+        [column_tile(CAP, tile)] * 2 + [column_tile(1, tile)],
         6 * ROWS * D * D,
         after=after,
     )
@@ -657,27 +663,29 @@
     return lax.reduce_precision(own.astype(f32) + got.astype(f32), 8, 7).astype(bf16)
 
 
-def longer(data, block, send, join):
+def longer(data, block, send):
     got = send(jnp.concatenate([data, block]))
     size = data.shape[0]
-    data, got = jnp.concatenate([data, got[:size]]), got[size:]
-    if not join:
-        return data, sum_rows(block, got)
-    return data, jnp.concatenate([sum_rows(block[:16], got[:16]), block[16:], got[16:]])
-
-
-def unpack_body(bits, own, got, outs):
-    for at in range(4):
-        here, there = (bits[6] % 4) ^ at, (bits[7] % 4) ^ at
-        for matrix in range(2):
-            rows = slice(at * SHARE + matrix * COLOUR, at * SHARE + (matrix + 1) * COLOUR)
-            mine, other = own[rows].astype(f32), got[rows].astype(f32)
-            outs[matrix][here] = jnp.where(bits[0] == 0, mine, other)
-            outs[2 + matrix][there] = jnp.where(bits[0] == 0, other, mine)
+    return jnp.concatenate([data, got[:size]]), sum_rows(block, got[size:])
+
+
+def unpack_body(bits, pieces, outs):
+    for turn in range(2):
+
+        @pl.when(pl.program_id(0) == turn)
+        def _():
+            own, got = pieces[turn], pieces[2 + turn]
+            for at in range(4):
+                here, there = (bits[6] % 4) ^ at, (bits[7] % 4) ^ at
+                for matrix in range(2):
+                    rows = slice(at * SHARE + matrix * COLOUR, at * SHARE + (matrix + 1) * COLOUR)
+                    mine, other = own[rows].astype(f32), got[rows].astype(f32)
+                    outs[matrix][here] = jnp.where(bits[0] == 0, mine, other)
+                    outs[2 + matrix][there] = jnp.where(bits[0] == 0, other, mine)
 
 
 def unpack_specs(turn):
-    part = pl.BlockSpec((4 * SHARE, D), lambda j, bits: (j, 0))
+    part = whole(4 * SHARE, D)
     spots = [
         pl.BlockSpec((4, COLOUR, D), lambda j, bits, at=at: ((bits[at] // 4) ^ (2 * turn + j), 0, 0)) for at in (6, 6, 7, 7)
     ]
@@ -687,24 +695,25 @@
 matrix_shapes = [((16, COLOUR, D), f32)] * 4
 
 
-def first_unpack(bits, own, got):
+def first_unpack(bits, pieces):
     part, spots = unpack_specs(0)
-    body = lambda bits, own, got, *outs: unpack_body(bits, own, got, outs)
-    return run(body, (2,), (own, got), [part] * 2, matrix_shapes, spots, 0, scalars=(bits,))
-
-
-def finish_body(bits, turned, turned_far, own, far, turned_last, turned_far_last, *refs):
-    outs = refs[-17:]
-    unpack_body(bits, turned, turned_far, outs[:4])
-
-    @pl.when(pl.program_id(0) == 0)
+    body = lambda bits, *refs: unpack_body(bits, refs[:4], refs[4:])
+    return run(body, (2,), pieces, [part] * 4, matrix_shapes, spots, 0, scalars=(bits,))
+
+
+def finish_body(bits, *refs):
+    unpack_body(bits, refs[:4], refs[16:20])
+
+    @pl.when(pl.program_id(0) == 1)
     def _():
-        vectors_body(own, turned_last, far, turned_far_last, *outs[4:])
-
-
-def vectors_body(own, turned, own_far, turned_far, *outs):
-    blocks = [ref[...].astype(f32) for ref in (own, turned, own_far, turned_far)]
-    sums = (blocks[0][:16] + blocks[1][:16]) + (blocks[2][:16] + blocks[3][:16])
+        vectors_body(refs[4:12], *refs[20:])
+
+
+def vectors_body(refs, *outs):
+    blocks = [ref[...].astype(f32) for ref in refs]
+    riders = [block[:16] for block in blocks]
+    pairs = [riders[at] + riders[at + 1] for at in range(0, 8, 2)]
+    sums = (pairs[0] + pairs[1]) + (pairs[2] + pairs[3])
     for at in range(8):
         outs[at][...] = sums[at]
     for at in range(4):
@@ -725,20 +734,20 @@
     inner_bias[...] = jnp.sum(d_inner, axis=0)
 
 
-def finish(bits, turned, turned_far, message, message_far, outs):
+def finish(bits, turned, turned_far, pieces, pieces_far, outs):
     part, spots = unpack_specs(1)
-    last = pl.BlockSpec((48, D), lambda j, *at: (D // 48, 0))
+    last = pl.BlockSpec((BLOCK, D), lambda j, *at: (4 * SHARE // BLOCK, 0))
     shapes = [(D,)] * 8 + [(4, 1, D), (TDIM, TFF), (TFF,), (TFF, D), (D,)]
     return run(
         finish_body,
         (2,),
-        (turned, turned_far, message, message_far, turned, turned_far, *outs),
-        [part] * 2 + [last] * 4 + [pl.BlockSpec(memory_space=pl.ANY)] * 4,
+        (*turned, *turned_far, *pieces, *turned, *pieces_far, *turned_far, *outs),
+        [part] * 4 + [last] * 8 + [pl.BlockSpec(memory_space=pl.ANY)] * 4,
         matrix_shapes + [(shape, f32) for shape in shapes],
         spots + [whole(*shape) for shape in shapes],
         0,
         scalars=(bits,),
-        aliases={7 + k: k for k in range(4)},
+        aliases={13 + k: k for k in range(4)},
     )
 
 
@@ -805,27 +814,29 @@
     def whole_sequence(rows):
         own = lax.dynamic_index_in_dim(rows[:, 0], stream, axis=0, keepdims=False)
         other = lax.dynamic_index_in_dim(rows[:, 0], 1 - stream, axis=0, keepdims=False)
-        return own, swapped(other, side)
+        return own, other
 
     def both_sequences(rows, far):
-        own = rows[:CAP]
+        own = rows
         return jnp.where(stream == 0, jnp.stack([own, far]), jnp.stack([far, own]))[:, None]
 
-    own, far = whole_sequence(layer_input)
-    features, inner_sum, middle, stamp, allowed, valid, masked = prepare(
-        bits, timesteps, src_len, seq_len, key_keep, time_inner, time_inner_bias, time_outer, time_outer_bias
+    own, other = whole_sequence(layer_input)
+    far = swapped(other, side)
+    cotangent = cotangent[:, 0]
+    features, inner_sum, middle, stamp, allowed, valid, masked, cot_other = prepare(
+        bits, timesteps, src_len, seq_len, key_keep, time_inner, time_inner_bias, time_outer, time_outer_bias, cotangent
     )
     weights = (query_weight, query_bias, key_weight, value_weight, value_bias)
     *first_rows, own_low = project(own, 0, stamp, allowed, *weights)
     (far,) = tie([far], first_rows[:1])
-    cotangent, far = lax.optimization_barrier((cotangent, far))
-    cot_own, cot_far = whole_sequence(cotangent)
+    cot_other, far = lax.optimization_barrier((cot_other, far))
+    cot_far = swapped(cot_other, side)
     *other_rows, far_low = project(far, 1, stamp, allowed, *weights)
     q, k, v = zip(first_rows, other_rows)
     low = (own_low, far_low)
     attended, lefts, probs = attend(q, k, v, low, masked)
     (lefts,) = tie([lefts], [cot_far])
-    output, for_core, activated, d_expanded, mixed_low, d_reduced, expand_bias_grad, d_first, d_branch, layer_sums = feed_forward(
+    output, far_output, for_core, activated, d_expanded, mixed_low, d_reduced, *others = feed_forward(
         bits,
         attended,
         own,
@@ -842,13 +853,14 @@
         second_gain,
         second_shift,
         valid,
-        cot_own,
+        cotangent,
         cot_far,
     )
+    expand_bias_grad, d_first, d_branch, layer_sums = others
     lefts_got = swapped(lefts, core)
-    (output,) = tie([output], [lefts_got])
-    output_got = swapped(output[CAP:], side)
-    grads, kept, sent, attend_sums = attend_back(bits, d_branch, output_weight, probs, q, k, v, allowed, [output])
+    (far_output,) = tie([far_output], [lefts_got])
+    output_got = swapped(far_output, side)
+    grads, kept, sent, attend_sums = attend_back(bits, d_branch, output_weight, probs, q, k, v, allowed, [far_output])
     block_parts = (inner_sum, middle, features, time_outer)
     if tuned:
         (sent,) = tie([sent], [output_got])
@@ -861,15 +873,17 @@
         hidden, hidden_sent = hidden_grad(bits, activated, d_reduced, d_expanded, mixed_low, hidden_got, [small_sent])
         (small_got,) = tie([small_got], [hidden])
         hidden_got = crossed(hidden_sent, True)
-        small, small_sent = halved(small, small_got, second)
+        small_sent = halved(small, small_got, second)[1]
+        (small_got,) = tie([small_got], [small_sent])
+        small = halved(small, small_got, second)[0]
         small_got = crossed(small_sent, False)
-        d_rows, d_time = input_grad(grads, query_weight, key_weight, value_weight, d_first, [small_sent])
-        (small_got,) = tie([small_got], [d_rows])
+        d_rows, far_grad, d_time = input_grad(grads, query_weight, key_weight, value_weight, d_first, [small_sent])
+        block = block_rows(bits, attend_sums, layer_sums, expand_bias_grad, d_time, *block_parts)
+        (small_got,) = tie([small_got], [block])
         small, small_sent = halved(small, small_got, third)
         small_got = lined(small_sent, True)
-        d_rows, d_time = tie([d_rows, d_time], [small_sent])
-        input_got = swapped(d_rows[CAP:], side)
-        block = block_rows(bits, attend_sums, layer_sums, expand_bias_grad, d_time, *block_parts)
+        (far_grad,) = tie([far_grad], [small_sent])
+        input_got = swapped(far_grad, side)
         small, small_sent = halved(small, small_got, fourth)
         small_got = lined(small_sent, False)
         hidden_got, input_got = tie([hidden_got, input_got], [small_sent])
@@ -877,32 +891,35 @@
         hidden_got = crossed(hidden_sent, False)
         (small_got,) = tie([small_got], [hidden_sent])
         share = plus(small, small_got).reshape(SHARE, D)
-        data, block = longer(share, block, lambda value: lined(value, False), False)
+        data, block = longer(share, block, lambda value: lined(value, False))
         (hidden_got,) = tie([hidden_got], [data])
         hidden, hidden_sent = halved(hidden, hidden_got, third)
         hidden_got = lined(hidden_sent, True)
         wait = lambda value: tie([value], [hidden_sent])[0]
-        data, block = longer(data, block, lambda value: wait(lined(value, True)), False)
-        data, block = longer(data, block, lambda value: crossed(value, False), True)
-        message = jnp.concatenate([data, block])
-        turned = crossed(message, True)
-        message_far = swapped(message, core)
-        hidden_got, output, output_got, d_rows, input_got = tie([hidden_got, output, output_got, d_rows, input_got], [message])
+        data, block = longer(data, block, lambda value: wait(lined(value, True)))
+        piece = jnp.concatenate([data, block])
+        cross_got = crossed(piece, False)
+        turned = crossed(piece, True)
         hidden, hidden_sent = halved(hidden, hidden_got, fourth)
         hidden_got = lined(hidden_sent, False)
-        outs = first_unpack(bits, message, message_far)
+        (cross_got,) = tie([cross_got], [hidden_sent, turned])
+        pieces, turned = (piece, cross_got), (turned, crossed(cross_got, True))
+        pieces_far = [swapped(value, core) for value in pieces]
+        output, output_got, d_rows, input_got = tie([output, output_got, d_rows, input_got], [cross_got])
+        outs = first_unpack(bits, (*pieces, *pieces_far))
         output, input_grad_rows = both_sequences(output, output_got), both_sequences(d_rows, input_got)
+        turned = tie(turned, [outs[0], output, input_grad_rows])
+        turned_far = [swapped(value, core) for value in turned]
+        (hidden_got,) = tie([hidden_got], turned)
         shares = (hidden.astype(f32) + hidden_got.astype(f32))[0]
         reduce_share, expand_share = shares[0], shares[1]
-        (turned,) = tie([turned], [outs[0], output, input_grad_rows, shares])
-        turned_far = swapped(turned, core)
         *matrices, expand_bias_grad, inner, inner_bias, outer, outer_bias = finish(
-            bits, turned, turned_far, message, message_far, outs
+            bits, turned, turned_far, pieces, pieces_far, outs
         )
         grad_query, grad_key, grad_value, grad_output = [out.reshape(D, D) for out in matrices[:4]]
         vectors = matrices[4:]
     else:
-        d_rows, d_time = input_grad(grads, query_weight, key_weight, value_weight, d_first, ())
+        d_rows, far_grad, d_time = input_grad(grads, query_weight, key_weight, value_weight, d_first, ())
         reduce_parts, expand_parts, pairs = [], [], []
         nothing_got = jnp.zeros_like(for_core)
         for core_bit, pair, left, right in (
@@ -925,7 +942,7 @@
         vectors, expand_bias_grad, inner, inner_bias, outer, outer_bias = everyones(
             attend_sums + layer_sums, expand_bias_grad, d_time, *block_parts
         )
-        input_grad_rows = both_sequences(d_rows, swapped(d_rows[CAP:], side))
+        input_grad_rows = both_sequences(d_rows, swapped(far_grad, side))
         output = both_sequences(output, output_got)
     return (
         output,

time: 224 us -> 212 us (0.946)
  local copies, waits for them, and re-layouts: 23.6 us -> 4.6 us
  waiting for transfers between devices: 49.2 us -> 39 us
  other arithmetic: 18 us -> 28.1 us
  starting transfers between devices: 24.1 us -> 30.7 us
    unnamed x58 -> x10, local copies, waits for them, and re-layouts: 13.8 us -> 0.03 us
    convert_element_type x7 -> x8, other arithmetic: 12 us -> 18.4 us  [plus(): return (left.astype(f32) + right.astype(f32)).astype(bf16)]
    ppermute x6, waiting for transfers between devices: 23.1 us -> 17.6 us  [lined(): return lax.ppermute(value, everywhere, pairs)]
    ppermute x6 -> x7, waiting for transfers between devices: 20 us -> 16.3 us  [crossed(): return lax.ppermute(value, everywhere, pairs)]
    ppermute x6 -> x7, starting transfers between devices: 7.12 us -> 10.4 us  [crossed(): return lax.ppermute(value, everywhere, pairs)]
    slice x3 -> x2, local copies, waits for them, and re-layouts: 3.77 us -> 1.05 us  [longer(): return (jnp.concatenate([data, got[:size]]), sum_rows(block, got[size:]))]
    ppermute x9 -> x11, starting transfers between devices: 7.43 us -> 9.69 us  [swapped(): lax.ppermute(value, axis, [(i, i ^ 1 << bit) for i in range(lax.axis_size...]
    ppermute x9 -> x11, waiting for transfers between devices: 6.06 us -> 5.12 us  [swapped(): lax.ppermute(value, axis, [(i, i ^ 1 << bit) for i in range(lax.axis_size...]
  transfers between devices with their start and end apart: 21 -> 24, of which waited for: 13 -> 15; matrix products, arithmetic and copies ran while one was open for 11% -> 15% of each run, Pallas kernels for 45% -> 48%
where the time goes in v2:
time: 212 us; the launch traced here: 211 us
  Pallas kernels  108 us (51%)
  waiting for transfers between devices  39 us (18%)
  starting transfers between devices  30.7 us (14%)
  other arithmetic  28.1 us (13%)
  local copies, waits for them, and re-layouts  4.6 us (2%)
    pallas_call x12, Pallas kernels, run(): pl.pallas_call(wrapped, grid_spec=pltpu.PrefetchScalarGridSpec(num_scalar...  108 us
    convert_element_type x8, other arithmetic, plus(): return (left.astype(f32) + right.astype(f32)).astype(bf16)  18.4 us
    ppermute x6, waiting for transfers between devices, lined(): return lax.ppermute(value, everywhere, pairs)  17.6 us
    ppermute x7, waiting for transfers between devices, crossed(): return lax.ppermute(value, everywhere, pairs)  16.3 us
    ppermute x6, starting transfers between devices, lined(): return lax.ppermute(value, everywhere, pairs)  10.6 us
    ppermute x7, starting transfers between devices, crossed(): return lax.ppermute(value, everywhere, pairs)  10.4 us
    ppermute x11, starting transfers between devices, swapped(): lax.ppermute(value, axis, [(i, i ^ 1 << bit) for i in range(lax.axis_size...  9.69 us
    ppermute x11, waiting for transfers between devices, swapped(): lax.ppermute(value, axis, [(i, i ^ 1 << bit) for i in range(lax.axis_size...  5.12 us
  transfers between devices with their start and end apart: 24, of which 15 were waited for; matrix products, arithmetic and copies ran while one was open for 15% of the time, Pallas kernels for 48%

profile of v2, /device:TPU:0, one launch (start us, length us, event | category | flops | bytes accessed | tf_op | source)
XLA Modules:
  0.0 211.0 jit_solution(17050218803051435829)
XLA Ops:
  2.7 3.0 %collective-permute-start = (bf16[256,768]{1,0:T(8,128)(2,1)}, bf16[256,768]{1,0:T(8,128)(2,1)}, u32[]{:S(2)}, u32[]{:S(2)}) collective-permute-start(bf16[256,768]{1,0:T(8,128)(2,1)} %get-tuple-element.171), channel_id=1, source_target_pairs={{0,16},{16,0},{1,17},{17,1},{2,18},{18,2},{3,19},{19,3},{4,20},{20... | collective-permute-start | bytes 1179656 | tf_op jit(solution)/shard_map/ppermute | solution.py:34
  6.3 4.0 %shard_map.400 = (f32[1,128]{1,0:T(1,128)}, f32[1,512]{1,0:T(1,128)}, f32[1,512]{1,0:T(1,128)}, f32[1,768]{1,0:T(1,128)}, f32[512,1]{1,0:T(8,128)}, /*index=5*/f...) custom-call(s32[8]{0:T(128)} %stack.63.refs_0_, s32[2]{0:T(128)} %refs_1_.2, s32[2]{0:T(128)} %refs_2_.2, ...), custom_call_target="tpu_custom_call" | custom-call | bytes 2120192 | tf_op jit(solution)/shard_map/pallas_call | solution.py:162
  10.3 4.7 %shard_map.401 = (bf16[256,768]{1,0:T(8,128)(2,1)}, bf16[256,768]{1,0:T(8,128)(2,1)}, bf16[256,768]{1,0:T(8,128)(2,1)}, bf16[256,768]{1,0:T(8,128)(2,1)}) custom-call(bf16[256,768]{1,0:T(8,128)(2,1)} %get-tuple-element.172.refs_0_.refs_2_, f32[1,768]{1,0:T(1,128)} %get-tuple-element.93.refs_1_.refs_4_, f32[512,1]{1,0:T(8,128)} %get-tuple-element.94.refs_2_.refs_11_, ...), custom_call_target="tpu_custom_call" | custom-call | flops 905969664 | bytes 5516288 | tf_op jit(solution)/shard_map/pallas_call | solution.py:162
  16.8 4.8 %shard_map.403 = (bf16[256,768]{1,0:T(8,128)(2,1)}, bf16[256,768]{1,0:T(8,128)(2,1)}, bf16[256,768]{1,0:T(8,128)(2,1)}, bf16[256,768]{1,0:T(8,128)(2,1)}) custom-call(bf16[256,768]{1,0:T(8,128)(2,1)} %shard_map.402.refs_0_.refs_3_, f32[1,768]{1,0:T(1,128)} %get-tuple-element.93.refs_1_.refs_4_, f32[512,1]{1,0:T(8,128)} %get-tuple-element.94.refs_2_.refs_11_, ...), custom_call_target="tpu_custom_call" | custom-call | flops 905969664 | bytes 5516288 | tf_op jit(solution)/shard_map/pallas_call | solution.py:162
  21.7 11.5 %shard_map.404 = (bf16[512,768]{1,0:T(8,128)(2,1)}, bf16[2,512,768]{2,1,0:T(8,128)(2,1)}, bf16[12,512,512]{2,1,0:T(8,128)(2,1)}) custom-call(bf16[256,768]{1,0:T(8,128)(2,1)} %get-tuple-element.95.refs_1_.refs_0_.refs_5_, bf16[256,768]{1,0:T(8,128)(2,1)} %get-tuple-element.98.refs_1_.refs_6_, bf16[256,768]{1,0:T(8,128)(2,1)} %get-tuple-element.99.refs_2_.refs_7_, ...), custom_call_target="tpu_custom_call" | custom-call | flops 3221225472 | bytes 11798528 | tf_op jit(solution)/shard_map/pallas_call | solution.py:162
  33.3 27.3 %shard_map.405 = (bf16[256,768]{1,0:T(8,128)(2,1)}, bf16[256,768]{1,0:T(8,128)(2,1)}, bf16[512,4608]{1,0:T(8,128)(2,1)}, bf16[512,1536]{1,0:T(8,128)(2,1)}, bf16...) custom-call(s32[8]{0:T(128)} %stack.63.refs_0_, ...), custom_call_target="tpu_custom_call" | custom-call | flops 10267656192 | bytes 26024960 | tf_op jit(solution)/shard_map/pallas_call | solution.py:162
  61.0 15.8 %shard_map.408 = (bf16[3,512,768]{2,1,0:T(8,128)(2,1)}, bf16[2,512,768]{2,1,0:T(8,128)(2,1)}, bf16[2,512,768]{2,1,0:T(8,128)(2,1)}, f32[8,768]{1,0:T(8,128)}) custom-call(s32[8]{0:T(128)} %stack.63.refs_0_, bf16[512,768]{1,0:T(8,128)(2,1)} %get-tuple-element.112.refs_1_.refs_2_, bf16[512,768]{1,0:T(8,128)(2,1)} %get-tuple-element.112.refs_1_.refs_2_, ...), custom_call_target="tpu_custom_call" | custom-call | flops 8053063680 | bytes 16934912 | tf_op jit(solution)/shard_map/pallas_call | solution.py:162
  77.3 3.4 %collective-permute-done.4.refs_1_.refs_4_ = bf16[2,512,768]{2,1,0:T(8,128)(2,1)} collective-permute-done((bf16[2,512,768]{2,1,0:T(8,128)(2,1)}, bf16[2,512,768]{2,1,0:T(8,128)(2,1)}, u32[]{:S(2)}, u32[]{:S(2)}) %collective-permute-start.4) | collective-permute-done | bytes 1572896 | tf_op jit(solution)/shard_map/ppermute | solution.py:34
  81.0 6.7 %shard_map.411 = (bf16[8,2,48,768]{3,2,1,0:T(8,128)(2,1)}, bf16[8,2,48,768]{3,2,1,0:T(8,128)(2,1)}) custom-call(s32[8]{0:T(128)} %stack.63.refs_0_, bf16[2,512,768]{2,1,0:T(8,128)(2,1)} %shard_map.406.refs_1_, bf16[2,512,768]{2,1,0:T(8,128)(2,1)} %get-tuple-element.116.refs_2_, bf16[2,512,768]{2,1,0:T(8,128)(2,1)} %collective-permute-done.2.refs_1_.refs_3_, ...), custom_call_target="tpu_custom_call" | custom-call | flops 2415919104 | bytes 8650752 | tf_op jit(solution)/shard_map/pallas_call | solution.py:162
  90.6 12.4 %shard_map.413 = (bf16[8,2,96,768]{3,2,1,0:T(8,128)(2,1)}, bf16[8,2,96,768]{3,2,1,0:T(8,128)(2,1)}) custom-call(s32[8]{0:T(128)} %stack.63.refs_0_, bf16[512,1536]{1,0:T(8,128)(2,1)} %get-tuple-element.121.refs_1_, bf16[512,768]{1,0:T(8,128)(2,1)} %get-tuple-element.122.refs_2_, bf16[512,1536]{1,0:T(8,128)(2,1)} %get-tuple-element.123.refs_3_, ...), custom_call_target="tpu_custom_call" | custom-call | flops 4831838208 | bytes 28311552 | tf_op jit(solution)/shard_map/pallas_call | solution.py:162
  109.3 6.2 %shard_map.415 = (bf16[256,768]{1,0:T(8,128)(2,1)}, bf16[256,768]{1,0:T(8,128)(2,1)}, f32[1,768]{1,0:T(1,128)}) custom-call(bf16[3,512,768]{2,1,0:T(8,128)(2,1)} %get-tuple-element.114.refs_0_, bf16[768,768]{1,0:T(8,128)(2,1)} %refs_1_.3, bf16[768,768]{1,0:T(8,128)(2,1)} %refs_2_.3, bf16[768,768]{1,0:T(8,128)(2,1)} %refs_3_.9, ...), custom_call_target="tpu_custom_call" | custom-call | flops 1811939328 | bytes 8260608 | tf_op jit(solution)/shard_map/pallas_call | solution.py:162
  115.5 3.9 %shard_map.417.refs_1_ = bf16[32,768]{1,0:T(8,128)(2,1)} custom-call(s32[8]{0:T(128)} %stack.63.refs_0_, f32[8,768]{1,0:T(8,128)} %get-tuple-element.129.refs_1_, f32[8,768]{1,0:T(8,128)} %get-tuple-element.130.refs_2_, f32[4,1,768]{2,1,0:T(1,128)} %get-tuple-element.131.refs_3_, f32[1,768]{1,0:T(1,128)} %get-tuple-element.132.refs_4_, ...), custom_call_target="tpu_custom_call" | custom-call | bytes 904704 | tf_op jit(solution)/shard_map/pallas_call | solution.py:162
  129.7 4.9 %collective-permute-done.10 = bf16[2,2,48,768]{3,2,1,0:T(8,128)(2,1)} collective-permute-done((bf16[2,2,48,768]{3,2,1,0:T(8,128)(2,1)}, bf16[2,2,48,768]{3,2,1,0:T(8,128)(2,1)}, u32[]{:S(2)}, u32[]{:S(2)}) %collective-permute-start.10) | collective-permute-done | bytes 294944 | tf_op jit(solution)/shard_map/ppermute | solution.py:611
  136.3 3.8 %collective-permute-start.11 = (bf16[1,2,48,768]{3,2,1,0:T(8,128)(2,1)}, bf16[1,2,48,768]{3,2,1,0:T(8,128)(2,1)}, u32[]{:S(2)}, u32[]{:S(2)}) collective-permute-start(bf16[1,2,48,768]{3,2,1,0:T(8,128)(2,1)} %fusion.7.refs_2_), channel_id=1, source_target_pairs={{0,8},{1,5},{2,10},{3,7},{4,12},{5,1},{6,14},{7,3},{8,0},{9,13},{1... | collective-permute-start | bytes 442376 | tf_op jit(solution)/shard_map/ppermute | solution.py:611
  140.5 4.4 %add_convert_fusion = (bf16[1,4,2,96,768]{4,3,2,1,0:T(8,128)(2,1)}, bf16[4,2,96,768]{3,2,1,0:T(8,128)(2,1)}) fusion(bf16[2,4,2,96,768]{4,3,2,1,0:T(8,128)(2,1)} %bitcast.21, s32[]{:T(128)S(6)} %select_n.94, bf16[2,4,2,96,768]{4,3,2,1,0:T(8,128)(2,1)} %bitcast.59, s32[]{:T(128)S(6)} %select_n.93), kind=kLoop, calls=%fused_computation | loop fusion | flops 4718592 | bytes 7077896 | tf_op jit(solution)/shard_map/convert_element_type | solution.py:615
  148.5 2.7 %collective-permute-start.12 = (bf16[128,768]{1,0:T(8,128)(2,1)S(1)}, bf16[128,768]{1,0:T(8,128)(2,1)S(1)}, u32[]{:S(2)}, u32[]{:S(2)}) collective-permute-start(bf16[128,768]{1,0:T(8,128)(2,1)S(1)} %pad_maximum_fusion.3), channel_id=1, source_target_pairs={{0,8},{1,5},{2,10},{3,7},{4,12},{5,1},{6,14},{7,3},{8,0},{9,13},{1... | collective-permute-start | bytes 589832 | tf_op jit(solution)/shard_map/ppermute | solution.py:611
  151.2 6.2 %collective-permute-done.12 = bf16[128,768]{1,0:T(8,128)(2,1)S(1)} collective-permute-done((bf16[128,768]{1,0:T(8,128)(2,1)S(1)}, bf16[128,768]{1,0:T(8,128)(2,1)S(1)}, u32[]{:S(2)}, u32[]{:S(2)}) %collective-permute-start.12) | collective-permute-done | bytes 196640 | tf_op jit(solution)/shard_map/ppermute | solution.py:611
  161.5 2.9 %add_convert_fusion.2 = (bf16[1,2,2,96,768]{4,3,2,1,0:T(8,128)(2,1)}, bf16[2,2,96,768]{3,2,1,0:T(8,128)(2,1)}) fusion(bf16[2,2,2,96,768]{4,3,2,1,0:T(8,128)(2,1)} %bitcast.25, s32[]{:T(128)S(6)} %select_n.97, bf16[2,2,2,96,768]{4,3,2,1,0:T(8,128)(2,1)} %bitcast.60, s32[]{:T(128)S(6)} %select_n.96), kind=kLoop, calls=%fused_computation.3 | loop fusion | flops 2359296 | bytes 3538952 | tf_op jit(solution)/shard_map/convert_element_type | solution.py:615
  176.4 3.3 %collective-permute-done.16 = bf16[2,2,96,768]{3,2,1,0:T(8,128)(2,1)} collective-permute-done((bf16[2,2,96,768]{3,2,1,0:T(8,128)(2,1)}, bf16[2,2,96,768]{3,2,1,0:T(8,128)(2,1)}, u32[]{:S(2)}, u32[]{:S(2)}) %collective-permute-start.16) | collective-permute-done | bytes 589856 | tf_op jit(solution)/shard_map/ppermute | solution.py:611
  181.4 5.0 %collective-permute-done.15.refs_0_ = bf16[416,768]{1,0:T(8,128)(2,1)} collective-permute-done((bf16[416,768]{1,0:T(8,128)(2,1)}, bf16[416,768]{1,0:T(8,128)(2,1)}, u32[]{:S(2)}, u32[]{:S(2)}) %collective-permute-start.15) | collective-permute-done | bytes 639008 | tf_op jit(solution)/shard_map/ppermute | solution.py:604
  186.4 3.8 %collective-permute-done.17.refs_2_.refs_0_ = bf16[416,768]{1,0:T(8,128)(2,1)} collective-permute-done((bf16[416,768]{1,0:T(8,128)(2,1)}, bf16[416,768]{1,0:T(8,128)(2,1)}, u32[]{:S(2)}, u32[]{:S(2)}) %collective-permute-start.17) | collective-permute-done | bytes 639008 | tf_op jit(solution)/shard_map/ppermute | solution.py:604
  193.0 3.4 %maximum_select_fusion = (bf16[2,1,256,768]{3,2,1,0:T(8,128)(2,1)}, bf16[2,1,256,768]{3,2,1,0:T(8,128)(2,1)}) fusion(bf16[1,1,256,768]{3,2,1,0:T(8,128)(2,1)} %bitcast.29, bf16[1,1,256,768]{3,2,1,0:T(8,128)(2,1)} %bitcast.69, pred[]{:T(512)S(6)} %eq.4, bf16[1,1,256,768]{3,2,1,0:T(8,128)(2,1)} %bitcast.70, bf16[1,1,256,768]{3,2,1,0:T(8,128)(2,1)} %bitcast.31), kind=kLoop, calls=%fused_computation.7 | loop fusion | flops 2359296 | bytes 3145729 | tf_op jit(solution)/shard_map/jit(_where)/select_n | solution.py:821
  196.4 4.8 %shard_map.426 = (f32[16,48,768]{2,1,0:T(8,128)}, f32[16,48,768]{2,1,0:T(8,128)}, f32[16,48,768]{2,1,0:T(8,128)}, f32[16,48,768]{2,1,0:T(8,128)}) custom-call(s32[8]{0:T(128)} %stack.63.refs_0_, bf16[416,768]{1,0:T(8,128)(2,1)} %pad_maximum_fusion.refs_1_.refs_5_, bf16[416,768]{1,0:T(8,128)(2,1)} %shard_map.424.refs_4_.refs_2_.refs_6_, ...), custom_call_target="tpu_custom_call" | custom-call | bytes 11993088 | tf_op jit(solution)/shard_map/pallas_call | solution.py:162
  205.3 5.5 %shard_map.428 = (f32[16,48,768]{2,1,0:T(8,128)}, f32[16,48,768]{2,1,0:T(8,128)}, f32[16,48,768]{2,1,0:T(8,128)}, f32[16,48,768]{2,1,0:T(8,128)}, f32[768]{0:T(1...) custom-call(s32[8]{0:T(128)} %stack.63.refs_0_, ...), custom_call_target="tpu_custom_call", output_to_operand_aliasing={{0}: (13, {}), {1}: (14, {}), {2}: (15, {}), {3}: (16, {})} | custom-call | bytes 28419072 | tf_op jit(solution)/shard_map/pallas_call | solution.py:162
  (85 shorter events, 55.8 us)
Async XLA Ops:
  2.7 12.4 %collective-permute-start = (bf16[256,768]{1,0:T(8,128)(2,1)}, bf16[256,768]{1,0:T(8,128)(2,1)}, u32[]{:S(2)}, u32[]{:S(2)}) collective-permute-start(bf16[256,768]{1,0:T(8,128)(2,1)} %get-tuple-element.171), channel_id=1, source_target_pairs={{0,16},{16,0},{1,17},{17,1},{2,18},{18,2},{3,19},{19,3},{4,20},{20... | collective-permute-start | bytes 1179656 | tf_op jit(solution)/shard_map/ppermute | solution.py:34
  15.1 18.1 %collective-permute-start.1 = (bf16[256,768]{1,0:T(8,128)(2,1)}, bf16[256,768]{1,0:T(8,128)(2,1)}, u32[]{:S(2)}, u32[]{:S(2)}) collective-permute-start(bf16[256,768]{1,0:T(8,128)(2,1)} %get-tuple-element.108), channel_id=1, source_target_pairs={{0,16},{16,0},{1,17},{17,1},{2,18},{18,2},{3,19},{19,3},{4,20},{20... | collective-permute-start | bytes 1179656 | tf_op jit(solution)/shard_map/ppermute | solution.py:34
  33.2 27.4 %collective-permute-start.2 = (bf16[2,512,768]{2,1,0:T(8,128)(2,1)}, bf16[2,512,768]{2,1,0:T(8,128)(2,1)}, u32[]{:S(2)}, u32[]{:S(2)}) collective-permute-start(bf16[2,512,768]{2,1,0:T(8,128)(2,1)} %shard_map.406.refs_1_), channel_id=1, source_target_pairs={{0,1},{1,0},{2,3},{3,2},{4,5},{5,4},{6,7},{7,6},{8,9},{9,8},{10,11... | collective-permute-start | bytes 4718600 | tf_op jit(solution)/shard_map/ppermute | solution.py:34
  60.6 16.1 %collective-permute-start.3 = (bf16[256,768]{1,0:T(8,128)(2,1)}, bf16[256,768]{1,0:T(8,128)(2,1)}, u32[]{:S(2)}, u32[]{:S(2)}) collective-permute-start(bf16[256,768]{1,0:T(8,128)(2,1)} %shard_map.407.refs_12_), channel_id=1, source_target_pairs={{0,16},{16,0},{1,17},{17,1},{2,18},{18,2},{3,19},{19,3},{4,20},{20... | collective-permute-start | bytes 1179656 | tf_op jit(solution)/shard_map/ppermute | solution.py:34
  76.8 3.9 %collective-permute-start.4 = (bf16[2,512,768]{2,1,0:T(8,128)(2,1)}, bf16[2,512,768]{2,1,0:T(8,128)(2,1)}, u32[]{:S(2)}, u32[]{:S(2)}) collective-permute-start(bf16[2,512,768]{2,1,0:T(8,128)(2,1)} %shard_map.409), channel_id=1, source_target_pairs={{0,1},{1,0},{2,3},{3,2},{4,5},{5,4},{6,7},{7,6},{8,9},{9,8},{10,11... | collective-permute-start | bytes 4718600 | tf_op jit(solution)/shard_map/ppermute | solution.py:34
  80.7 8.3 %collective-permute-start.5 = (bf16[512,4608]{1,0:T(8,128)(2,1)}, bf16[512,4608]{1,0:T(8,128)(2,1)}, u32[]{:S(2)}, u32[]{:S(2)}) collective-permute-start(bf16[512,4608]{1,0:T(8,128)(2,1)} %shard_map.410.refs_5_), channel_id=1, source_target_pairs={{0,1},{1,0},{2,3},{3,2},{4,5},{5,4},{6,7},{7,6},{8,9},{9,8},{10,11... | collective-permute-start | bytes 14155784 | tf_op jit(solution)/shard_map/ppermute | solution.py:34
  88.9 16.5 %collective-permute-start.6 = (bf16[8,2,48,768]{3,2,1,0:T(8,128)(2,1)}, bf16[8,2,48,768]{3,2,1,0:T(8,128)(2,1)}, u32[]{:S(2)}, u32[]{:S(2)}) collective-permute-start(bf16[8,2,48,768]{3,2,1,0:T(8,128)(2,1)} %shard_map.412.refs_9_), channel_id=1, source_target_pairs={{0,2},{1,17},{2,0},{3,19},{4,6},{5,21},{6,4},{7,23},{8,10},{9,25},... | collective-permute-start | bytes 3538952 | tf_op jit(solution)/shard_map/ppermute | solution.py:604
  103.0 37.6 %collective-permute-start.7 = (bf16[8,2,96,768]{3,2,1,0:T(8,128)(2,1)}, bf16[8,2,96,768]{3,2,1,0:T(8,128)(2,1)}, u32[]{:S(2)}, u32[]{:S(2)}) collective-permute-start(bf16[8,2,96,768]{3,2,1,0:T(8,128)(2,1)} %get-tuple-element.127), channel_id=1, source_target_pairs={{0,2},{1,17},{2,0},{3,19},{4,6},{5,21},{6,4},{7,23},{8,10},{9,25},... | collective-permute-start | bytes 7077896 | tf_op jit(solution)/shard_map/ppermute | solution.py:604
  107.6 16.6 %collective-permute-start.8 = (bf16[4,2,48,768]{3,2,1,0:T(8,128)(2,1)}, bf16[4,2,48,768]{3,2,1,0:T(8,128)(2,1)}, u32[]{:S(2)}, u32[]{:S(2)}) collective-permute-start(bf16[4,2,48,768]{3,2,1,0:T(8,128)(2,1)} %fusion.1.refs_5_.refs_1_), channel_id=1, source_target_pairs={{0,16},{1,3},{2,18},{3,1},{4,20},{5,7},{6,22},{7,5},{8,24},{9,11},... | collective-permute-start | bytes 1769480 | tf_op jit(solution)/shard_map/ppermute | solution.py:604
  126.4 8.2 %collective-permute-start.10 = (bf16[2,2,48,768]{3,2,1,0:T(8,128)(2,1)}, bf16[2,2,48,768]{3,2,1,0:T(8,128)(2,1)}, u32[]{:S(2)}, u32[]{:S(2)}) collective-permute-start(bf16[2,2,48,768]{3,2,1,0:T(8,128)(2,1)} %get-tuple-element.170.refs_1_), channel_id=1, source_target_pairs={{0,4},{1,9},{2,6},{3,11},{4,0},{5,13},{6,2},{7,15},{8,12},{9,1},{1... | collective-permute-start | bytes 884744 | tf_op jit(solution)/shard_map/ppermute | solution.py:611
  128.2 12.4 %collective-permute-start.9 = (bf16[256,768]{1,0:T(8,128)(2,1)}, bf16[256,768]{1,0:T(8,128)(2,1)}, u32[]{:S(2)}, u32[]{:S(2)}) collective-permute-start(bf16[256,768]{1,0:T(8,128)(2,1)} %shard_map.419), channel_id=1, source_target_pairs={{0,16},{16,0},{1,17},{17,1},{2,18},{18,2},{3,19},{19,3},{4,20},{20... | collective-permute-start | bytes 1179656 | tf_op jit(solution)/shard_map/ppermute | solution.py:34
  136.3 10.2 %collective-permute-start.11 = (bf16[1,2,48,768]{3,2,1,0:T(8,128)(2,1)}, bf16[1,2,48,768]{3,2,1,0:T(8,128)(2,1)}, u32[]{:S(2)}, u32[]{:S(2)}) collective-permute-start(bf16[1,2,48,768]{3,2,1,0:T(8,128)(2,1)} %fusion.7.refs_2_), channel_id=1, source_target_pairs={{0,8},{1,5},{2,10},{3,7},{4,12},{5,1},{6,14},{7,3},{8,0},{9,13},{1... | collective-permute-start | bytes 442376 | tf_op jit(solution)/shard_map/ppermute | solution.py:611
  145.0 16.5 %collective-permute-start.14 = (bf16[4,2,96,768]{3,2,1,0:T(8,128)(2,1)}, bf16[4,2,96,768]{3,2,1,0:T(8,128)(2,1)}, u32[]{:S(2)}, u32[]{:S(2)}) collective-permute-start(bf16[4,2,96,768]{3,2,1,0:T(8,128)(2,1)} %get-tuple-element.166.refs_1_), channel_id=1, source_target_pairs={{0,16},{1,3},{2,18},{3,1},{4,20},{5,7},{6,22},{7,5},{8,24},{9,11},... | collective-permute-start | bytes 3538952 | tf_op jit(solution)/shard_map/ppermute | solution.py:604
  148.5 8.8 %collective-permute-start.12 = (bf16[128,768]{1,0:T(8,128)(2,1)S(1)}, bf16[128,768]{1,0:T(8,128)(2,1)S(1)}, u32[]{:S(2)}, u32[]{:S(2)}) collective-permute-start(bf16[128,768]{1,0:T(8,128)(2,1)S(1)} %pad_maximum_fusion.3), channel_id=1, source_target_pairs={{0,8},{1,5},{2,10},{3,7},{4,12},{5,1},{6,14},{7,3},{8,0},{9,13},{1... | collective-permute-start | bytes 589832 | tf_op jit(solution)/shard_map/ppermute | solution.py:611
  158.2 10.1 %collective-permute-start.13 = (bf16[224,768]{1,0:T(8,128)(2,1)}, bf16[224,768]{1,0:T(8,128)(2,1)}, u32[]{:S(2)}, u32[]{:S(2)}) collective-permute-start(bf16[224,768]{1,0:T(8,128)(2,1)} %pad_maximum_fusion.1), channel_id=1, source_target_pairs={{0,4},{1,9},{2,6},{3,11},{4,0},{5,13},{6,2},{7,15},{8,12},{9,1},{1... | collective-permute-start | bytes 1032200 | tf_op jit(solution)/shard_map/ppermute | solution.py:611
  164.4 15.3 %collective-permute-start.16 = (bf16[2,2,96,768]{3,2,1,0:T(8,128)(2,1)}, bf16[2,2,96,768]{3,2,1,0:T(8,128)(2,1)}, u32[]{:S(2)}, u32[]{:S(2)}) collective-permute-start(bf16[2,2,96,768]{3,2,1,0:T(8,128)(2,1)} %get-tuple-element.168.refs_1_), channel_id=1, source_target_pairs={{0,4},{1,9},{2,6},{3,11},{4,0},{5,13},{6,2},{7,15},{8,12},{9,1},{1... | collective-permute-start | bytes 1769480 | tf_op jit(solution)/shard_map/ppermute | solution.py:611
  172.0 14.4 %collective-permute-start.15 = (bf16[416,768]{1,0:T(8,128)(2,1)}, bf16[416,768]{1,0:T(8,128)(2,1)}, u32[]{:S(2)}, u32[]{:S(2)}) collective-permute-start(bf16[416,768]{1,0:T(8,128)(2,1)} %pad_maximum_fusion.refs_1_.refs_5_), channel_id=1, source_target_pairs={{0,16},{1,3},{2,18},{3,1},{4,20},{5,7},{6,22},{7,5},{8,24},{9,11},... | collective-permute-start | bytes 1916936 | tf_op jit(solution)/shard_map/ppermute | solution.py:604
  173.2 16.9 %collective-permute-start.17 = (bf16[416,768]{1,0:T(8,128)(2,1)}, bf16[416,768]{1,0:T(8,128)(2,1)}, u32[]{:S(2)}, u32[]{:S(2)}) collective-permute-start(bf16[416,768]{1,0:T(8,128)(2,1)} %pad_maximum_fusion.refs_1_.refs_5_), channel_id=1, source_target_pairs={{0,2},{1,17},{2,0},{3,19},{4,6},{5,21},{6,4},{7,23},{8,10},{9,25},... | collective-permute-start | bytes 1916936 | tf_op jit(solution)/shard_map/ppermute | solution.py:604
  175.2 21.2 %collective-permute-start.19 = (bf16[416,768]{1,0:T(8,128)(2,1)}, bf16[416,768]{1,0:T(8,128)(2,1)}, u32[]{:S(2)}, u32[]{:S(2)}) collective-permute-start(bf16[416,768]{1,0:T(8,128)(2,1)} %pad_maximum_fusion.refs_1_.refs_5_), channel_id=1, source_target_pairs={{0,1},{1,0},{2,3},{3,2},{4,5},{5,4},{6,7},{7,6},{8,9},{9,8},{10,11... | collective-permute-start | bytes 1916936 | tf_op jit(solution)/shard_map/ppermute | solution.py:34
  190.2 6.2 %collective-permute-start.20 = (bf16[416,768]{1,0:T(8,128)(2,1)}, bf16[416,768]{1,0:T(8,128)(2,1)}, u32[]{:S(2)}, u32[]{:S(2)}) collective-permute-start(bf16[416,768]{1,0:T(8,128)(2,1)} %shard_map.424.refs_4_.refs_2_.refs_6_), channel_id=1, source_target_pairs={{0,1},{1,0},{2,3},{3,2},{4,5},{5,4},{6,7},{7,6},{8,9},{9,8},{10,11... | collective-permute-start | bytes 1916936 | tf_op jit(solution)/shard_map/ppermute | solution.py:34
  190.6 10.7 %collective-permute-start.18 = (bf16[416,768]{1,0:T(8,128)(2,1)}, bf16[416,768]{1,0:T(8,128)(2,1)}, u32[]{:S(2)}, u32[]{:S(2)}) collective-permute-start(bf16[416,768]{1,0:T(8,128)(2,1)} %shard_map.424.refs_4_.refs_2_.refs_6_), channel_id=1, source_target_pairs={{0,2},{1,17},{2,0},{3,19},{4,6},{5,21},{6,4},{7,23},{8,10},{9,25},... | collective-permute-start | bytes 1916936 | tf_op jit(solution)/shard_map/ppermute | solution.py:604
  192.6 10.6 %collective-permute-start.23 = (bf16[1,2,96,768]{3,2,1,0:T(8,128)(2,1)}, bf16[1,2,96,768]{3,2,1,0:T(8,128)(2,1)}, u32[]{:S(2)}, u32[]{:S(2)}) collective-permute-start(bf16[1,2,96,768]{3,2,1,0:T(8,128)(2,1)} %fusion.4.refs_1_), channel_id=1, source_target_pairs={{0,8},{1,5},{2,10},{3,7},{4,12},{5,1},{6,14},{7,3},{8,0},{9,13},{1... | collective-permute-start | bytes 884744 | tf_op jit(solution)/shard_map/ppermute | solution.py:611
  201.4 4.0 %collective-permute-start.21 = (bf16[416,768]{1,0:T(8,128)(2,1)}, bf16[416,768]{1,0:T(8,128)(2,1)}, u32[]{:S(2)}, u32[]{:S(2)}) collective-permute-start(bf16[416,768]{1,0:T(8,128)(2,1)} %get-tuple-element.143.refs_1_.refs_7_), channel_id=1, source_target_pairs={{0,1},{1,0},{2,3},{3,2},{4,5},{5,4},{6,7},{7,6},{8,9},{9,8},{10,11... | collective-permute-start | bytes 1916936 | tf_op jit(solution)/shard_map/ppermute | solution.py:34
  201.4 4.0 %collective-permute-start.22 = (bf16[416,768]{1,0:T(8,128)(2,1)}, bf16[416,768]{1,0:T(8,128)(2,1)}, u32[]{:S(2)}, u32[]{:S(2)}) collective-permute-start(bf16[416,768]{1,0:T(8,128)(2,1)} %get-tuple-element.144.refs_2_.refs_8_), channel_id=1, source_target_pairs={{0,1},{1,0},{2,3},{3,2},{4,5},{5,4},{6,7},{7,6},{8,9},{9,8},{10,11... | collective-permute-start | bytes 1916936 | tf_op jit(solution)/shard_map/ppermute | solution.py:34
  (5 other events, 35.9 us)

commit v3 on v2

--- a/solution.py
+++ b/solution.py
@@ -380,7 +380,7 @@
             product = nn(low, rw[cut, :])
             added_up = product if added_up is None else added_up + product
         total[...] += added_up
-        store(activated_own, step * (D // 2))
+        store(activated_own, step % 2 * (D // 2))
 
     @pl.when(step == tiles - 1)
     def _():
@@ -393,8 +393,6 @@
         low = back.astype(bf16)
         total[...] = back
         d_reduced[...] = low
-        for_core[:, 2 * D : 3 * D] = low
-        for_core[:, 3 * D : 4 * D] = mixed_low[...]
         sums[...] = jnp.concatenate(
             [jnp.zeros((5, D), f32), row_sum(low.astype(f32)), row_sum(d_out * n2), row_sum(d_out)], axis=0
         )
@@ -405,7 +403,13 @@
         columns[...] = d_expanded
         bias_grad[0] = row_sum(d_expanded.astype(f32))
         total[...] += nt(d_expanded, ew[...])
-        store(expanded_own, 4 * D + (step - tiles) * (D // 2))
+        store(expanded_own, 0)
+        for at in range(tiles):
+
+            @pl.when(step == tiles + at)
+            def _():
+                source = d_reduced if at < 2 else mixed_low
+                for_core[:, D // 2 :] = source[:, at % 2 * (D // 2) : (at % 2 + 1) * (D // 2)]
 
     @pl.when(step == 2 * tiles - 1)
     def _():
@@ -435,7 +439,8 @@
         [((CAP, D), bf16)] * 2
         + [(FOR_CORE, bf16), ((ROWS, FF // 2), bf16), ((ROWS, FF // 2), bf16), ((ROWS, D), bf16)]
         + [((ROWS, D), bf16), ((tiles, 1, D), f32), ((ROWS, D), f32), ((ROWS, D), bf16), ((8, D), f32)],
-        [half, half, whole(*FOR_CORE), forward, backward, square, square]
+        [half, half, pl.BlockSpec((ROWS, D), lambda j, *at: (0, jnp.where(j < tiles, j // 2, j - tiles // 2)))]
+        + [forward, backward, square, square]
         + [pl.BlockSpec((1, 1, D), lambda j, *at: (jnp.maximum(j - tiles, 0), 0, 0)), square, square, whole(8, D)],
         2 * ROWS * D * (D + 4 * FF),
         scratch=[pltpu.VMEM((ROWS, D), f32)] * 2
@@ -444,7 +449,9 @@
     )
 
 
-def hidden_grad_body(bits, activated, d_reduced, d_expanded, mixed, activated_got, reduced_got, mixed_got, expanded_got, kept, sent):
+def hidden_grad_body(bits, activated, d_reduced, d_expanded, mixed, activated_got, *refs):
+    halves, (kept, sent) = refs[:6], refs[6:]
+    reduced_got, mixed_got, expanded_got = [lambda at=at: jnp.concatenate([halves[at][...], halves[at + 1][...]], axis=1) for at in (0, 2, 4)]
     step = pl.program_id(0)
     tile = step % 2
 
@@ -466,22 +473,24 @@
 
     @pl.when(step < 2)
     def _():
-        store(0, tn(activated[...], d_reduced[...]) + tn(activated_got[...], reduced_got[...]))
+        store(0, tn(activated[...], d_reduced[...]) + tn(activated_got[...], reduced_got()))
 
     @pl.when(step >= 2)
     def _():
-        store(1, tn(d_expanded[...], mixed[...]) + tn(expanded_got[...], mixed_got[...]))
+        store(1, tn(d_expanded[...], mixed[...]) + tn(expanded_got(), mixed_got()))
 
 
 def hidden_grad(bits, activated, d_reduced, d_expanded, mixed, got, after):
     first = lambda start: pl.BlockSpec((ROWS, D), lambda j, bits: (0, start + jnp.minimum(j, 1)))
     second = lambda start: pl.BlockSpec((ROWS, D), lambda j, bits: (0, start + jnp.maximum(j - 2, 0)))
     square = lambda at: pl.BlockSpec((ROWS, D), lambda j, bits: (0, at))
+    unit = lambda at: pl.BlockSpec((ROWS, D // 2), lambda j, bits: (0, at))
+    turn = lambda start: pl.BlockSpec((ROWS, D // 2), lambda j, bits: (0, start + 4 * jnp.maximum(j - 2, 0)))
     return run(
         hidden_grad_body,
         (4,),
-        (activated, d_reduced, d_expanded, mixed, got, got, got, got),
-        [first(0), square(0), second(0), square(0), first(0), square(2), square(3), second(4)],
+        (activated, d_reduced, d_expanded, mixed) + (got,) * 7,
+        [first(0), square(0), second(0), square(0), first(0)] + [unit(at) for at in (5, 7, 9, 11)] + [turn(4), turn(6)],
         [((8, 2, SHARE, D), bf16)] * 2,
         [whole(8, 2, SHARE, D)] * 2,
         4 * ROWS * D * FF,
@@ -922,9 +931,10 @@
         d_rows, far_grad, d_time = input_grad(grads, query_weight, key_weight, value_weight, d_first, ())
         reduce_parts, expand_parts, pairs = [], [], []
         nothing_got = jnp.zeros_like(for_core)
+        expanded_other = jnp.concatenate([for_core[:, at * D // 2 : (at + 1) * D // 2] for at in (4, 6, 8, 10)], axis=1)
         for core_bit, pair, left, right in (
             (0, kept, activated, d_expanded),
-            (1, sent, for_core[:, : 2 * D], for_core[:, 4 * D :]),
+            (1, sent, for_core[:, : 2 * D], expanded_other),
         ):
             as_core = bits.at[0].set(core_bit)
             hidden = hidden_grad(as_core, left, d_reduced, right, mixed_low, nothing_got, ())

time: 212 us -> 212 us (level)
  no operation moved by 1% of the time
where the time goes in v3:
time: 212 us; the launch traced here: 210 us
  Pallas kernels  107 us (50%)
  waiting for transfers between devices  39.5 us (19%)
  starting transfers between devices  30 us (14%)
  other arithmetic  28.1 us (13%)
  local copies, waits for them, and re-layouts  4.6 us (2%)
    pallas_call x12, Pallas kernels, run(): pl.pallas_call(wrapped, grid_spec=pltpu.PrefetchScalarGridSpec(num_scalar...  107 us
    ppermute x6, waiting for transfers between devices, lined(): return lax.ppermute(value, everywhere, pairs)  18.5 us
    convert_element_type x8, other arithmetic, plus(): return (left.astype(f32) + right.astype(f32)).astype(bf16)  18.4 us
    ppermute x7, waiting for transfers between devices, crossed(): return lax.ppermute(value, everywhere, pairs)  15.9 us
    ppermute x7, starting transfers between devices, crossed(): return lax.ppermute(value, everywhere, pairs)  10.5 us
    ppermute x11, starting transfers between devices, swapped(): lax.ppermute(value, axis, [(i, i ^ 1 << bit) for i in range(lax.axis_size...  9.77 us
    ppermute x6, starting transfers between devices, lined(): return lax.ppermute(value, everywhere, pairs)  9.73 us
    ppermute x11, waiting for transfers between devices, swapped(): lax.ppermute(value, axis, [(i, i ^ 1 << bit) for i in range(lax.axis_size...  5.13 us
  transfers between devices with their start and end apart: 24, of which 15 were waited for; matrix products, arithmetic and copies ran while one was open for 15% of the time, Pallas kernels for 48%

profile of v3, /device:TPU:0, one launch (start us, length us, event | category | flops | bytes accessed | tf_op | source)
XLA Modules:
  0.0 210.3 jit_solution(9680821776267356560)
XLA Ops:
  2.7 3.0 %collective-permute-start = (bf16[256,768]{1,0:T(8,128)(2,1)}, bf16[256,768]{1,0:T(8,128)(2,1)}, u32[]{:S(2)}, u32[]{:S(2)}) collective-permute-start(bf16[256,768]{1,0:T(8,128)(2,1)} %get-tuple-element.171), channel_id=1, source_target_pairs={{0,16},{16,0},{1,17},{17,1},{2,18},{18,2},{3,19},{19,3},{4,20},{20... | collective-permute-start | bytes 1179656 | tf_op jit(solution)/shard_map/ppermute | solution.py:34
  6.3 4.0 %shard_map.400 = (f32[1,128]{1,0:T(1,128)}, f32[1,512]{1,0:T(1,128)}, f32[1,512]{1,0:T(1,128)}, f32[1,768]{1,0:T(1,128)}, f32[512,1]{1,0:T(8,128)}, /*index=5*/f...) custom-call(s32[8]{0:T(128)} %stack.63.refs_0_, s32[2]{0:T(128)} %refs_1_.2, s32[2]{0:T(128)} %refs_2_.2, ...), custom_call_target="tpu_custom_call" | custom-call | bytes 2120192 | tf_op jit(solution)/shard_map/pallas_call | solution.py:162
  10.3 4.7 %shard_map.401 = (bf16[256,768]{1,0:T(8,128)(2,1)}, bf16[256,768]{1,0:T(8,128)(2,1)}, bf16[256,768]{1,0:T(8,128)(2,1)}, bf16[256,768]{1,0:T(8,128)(2,1)}) custom-call(bf16[256,768]{1,0:T(8,128)(2,1)} %get-tuple-element.172.refs_0_.refs_2_, f32[1,768]{1,0:T(1,128)} %get-tuple-element.93.refs_1_.refs_4_, f32[512,1]{1,0:T(8,128)} %get-tuple-element.94.refs_2_.refs_11_, ...), custom_call_target="tpu_custom_call" | custom-call | flops 905969664 | bytes 5516288 | tf_op jit(solution)/shard_map/pallas_call | solution.py:162
  16.8 4.8 %shard_map.403 = (bf16[256,768]{1,0:T(8,128)(2,1)}, bf16[256,768]{1,0:T(8,128)(2,1)}, bf16[256,768]{1,0:T(8,128)(2,1)}, bf16[256,768]{1,0:T(8,128)(2,1)}) custom-call(bf16[256,768]{1,0:T(8,128)(2,1)} %shard_map.402.refs_0_.refs_3_, f32[1,768]{1,0:T(1,128)} %get-tuple-element.93.refs_1_.refs_4_, f32[512,1]{1,0:T(8,128)} %get-tuple-element.94.refs_2_.refs_11_, ...), custom_call_target="tpu_custom_call" | custom-call | flops 905969664 | bytes 5516288 | tf_op jit(solution)/shard_map/pallas_call | solution.py:162
  21.7 11.5 %shard_map.404 = (bf16[512,768]{1,0:T(8,128)(2,1)}, bf16[2,512,768]{2,1,0:T(8,128)(2,1)}, bf16[12,512,512]{2,1,0:T(8,128)(2,1)}) custom-call(bf16[256,768]{1,0:T(8,128)(2,1)} %get-tuple-element.95.refs_1_.refs_0_.refs_5_, bf16[256,768]{1,0:T(8,128)(2,1)} %get-tuple-element.98.refs_1_.refs_6_, bf16[256,768]{1,0:T(8,128)(2,1)} %get-tuple-element.99.refs_2_.refs_7_, ...), custom_call_target="tpu_custom_call" | custom-call | flops 3221225472 | bytes 11798528 | tf_op jit(solution)/shard_map/pallas_call | solution.py:162
  33.3 26.6 %shard_map.405 = (bf16[256,768]{1,0:T(8,128)(2,1)}, bf16[256,768]{1,0:T(8,128)(2,1)}, bf16[512,4608]{1,0:T(8,128)(2,1)}, bf16[512,1536]{1,0:T(8,128)(2,1)}, bf16...) custom-call(s32[8]{0:T(128)} %stack.63.refs_0_, ...), custom_call_target="tpu_custom_call" | custom-call | flops 10267656192 | bytes 26024960 | tf_op jit(solution)/shard_map/pallas_call | solution.py:162
  60.3 15.8 %shard_map.408 = (bf16[3,512,768]{2,1,0:T(8,128)(2,1)}, bf16[2,512,768]{2,1,0:T(8,128)(2,1)}, bf16[2,512,768]{2,1,0:T(8,128)(2,1)}, f32[8,768]{1,0:T(8,128)}) custom-call(s32[8]{0:T(128)} %stack.63.refs_0_, bf16[512,768]{1,0:T(8,128)(2,1)} %get-tuple-element.112.refs_1_.refs_2_, bf16[512,768]{1,0:T(8,128)(2,1)} %get-tuple-element.112.refs_1_.refs_2_, ...), custom_call_target="tpu_custom_call" | custom-call | flops 8053063680 | bytes 16934912 | tf_op jit(solution)/shard_map/pallas_call | solution.py:162
  76.6 3.4 %collective-permute-done.4.refs_1_.refs_4_ = bf16[2,512,768]{2,1,0:T(8,128)(2,1)} collective-permute-done((bf16[2,512,768]{2,1,0:T(8,128)(2,1)}, bf16[2,512,768]{2,1,0:T(8,128)(2,1)}, u32[]{:S(2)}, u32[]{:S(2)}) %collective-permute-start.4) | collective-permute-done | bytes 1572896 | tf_op jit(solution)/shard_map/ppermute | solution.py:34
  80.3 6.7 %shard_map.411 = (bf16[8,2,48,768]{3,2,1,0:T(8,128)(2,1)}, bf16[8,2,48,768]{3,2,1,0:T(8,128)(2,1)}) custom-call(s32[8]{0:T(128)} %stack.63.refs_0_, bf16[2,512,768]{2,1,0:T(8,128)(2,1)} %shard_map.406.refs_1_, bf16[2,512,768]{2,1,0:T(8,128)(2,1)} %get-tuple-element.116.refs_2_, bf16[2,512,768]{2,1,0:T(8,128)(2,1)} %collective-permute-done.2.refs_1_.refs_3_, ...), custom_call_target="tpu_custom_call" | custom-call | flops 2415919104 | bytes 8650752 | tf_op jit(solution)/shard_map/pallas_call | solution.py:162
  89.9 12.5 %shard_map.413 = (bf16[8,2,96,768]{3,2,1,0:T(8,128)(2,1)}, bf16[8,2,96,768]{3,2,1,0:T(8,128)(2,1)}) custom-call(s32[8]{0:T(128)} %stack.63.refs_0_, bf16[512,1536]{1,0:T(8,128)(2,1)} %get-tuple-element.121.refs_1_, bf16[512,768]{1,0:T(8,128)(2,1)} %get-tuple-element.122.refs_2_, bf16[512,1536]{1,0:T(8,128)(2,1)} %get-tuple-element.123.refs_3_, ...), custom_call_target="tpu_custom_call" | custom-call | flops 4831838208 | bytes 42467328 | tf_op jit(solution)/shard_map/pallas_call | solution.py:162
  108.6 6.2 %shard_map.415 = (bf16[256,768]{1,0:T(8,128)(2,1)}, bf16[256,768]{1,0:T(8,128)(2,1)}, f32[1,768]{1,0:T(1,128)}) custom-call(bf16[3,512,768]{2,1,0:T(8,128)(2,1)} %get-tuple-element.114.refs_0_, bf16[768,768]{1,0:T(8,128)(2,1)} %refs_1_.3, bf16[768,768]{1,0:T(8,128)(2,1)} %refs_2_.3, bf16[768,768]{1,0:T(8,128)(2,1)} %refs_3_.9, ...), custom_call_target="tpu_custom_call" | custom-call | flops 1811939328 | bytes 8260608 | tf_op jit(solution)/shard_map/pallas_call | solution.py:162
  114.8 3.9 %shard_map.417.refs_1_ = bf16[32,768]{1,0:T(8,128)(2,1)} custom-call(s32[8]{0:T(128)} %stack.63.refs_0_, f32[8,768]{1,0:T(8,128)} %get-tuple-element.129.refs_1_, f32[8,768]{1,0:T(8,128)} %get-tuple-element.130.refs_2_, f32[4,1,768]{2,1,0:T(1,128)} %get-tuple-element.131.refs_3_, f32[1,768]{1,0:T(1,128)} %get-tuple-element.132.refs_4_, ...), custom_call_target="tpu_custom_call" | custom-call | bytes 904704 | tf_op jit(solution)/shard_map/pallas_call | solution.py:162
  129.0 5.7 %collective-permute-done.10 = bf16[2,2,48,768]{3,2,1,0:T(8,128)(2,1)} collective-permute-done((bf16[2,2,48,768]{3,2,1,0:T(8,128)(2,1)}, bf16[2,2,48,768]{3,2,1,0:T(8,128)(2,1)}, u32[]{:S(2)}, u32[]{:S(2)}) %collective-permute-start.10) | collective-permute-done | bytes 294944 | tf_op jit(solution)/shard_map/ppermute | solution.py:620
  136.4 3.0 %collective-permute-start.11 = (bf16[1,2,48,768]{3,2,1,0:T(8,128)(2,1)}, bf16[1,2,48,768]{3,2,1,0:T(8,128)(2,1)}, u32[]{:S(2)}, u32[]{:S(2)}) collective-permute-start(bf16[1,2,48,768]{3,2,1,0:T(8,128)(2,1)} %fusion.7.refs_2_), channel_id=1, source_target_pairs={{0,8},{1,5},{2,10},{3,7},{4,12},{5,1},{6,14},{7,3},{8,0},{9,13},{1... | collective-permute-start | bytes 442376 | tf_op jit(solution)/shard_map/ppermute | solution.py:620
  139.8 4.4 %add_convert_fusion = (bf16[1,4,2,96,768]{4,3,2,1,0:T(8,128)(2,1)}, bf16[4,2,96,768]{3,2,1,0:T(8,128)(2,1)}) fusion(bf16[2,4,2,96,768]{4,3,2,1,0:T(8,128)(2,1)} %bitcast.21, s32[]{:T(128)S(6)} %select_n.94, bf16[2,4,2,96,768]{4,3,2,1,0:T(8,128)(2,1)} %bitcast.59, s32[]{:T(128)S(6)} %select_n.93), kind=kLoop, calls=%fused_computation | loop fusion | flops 4718592 | bytes 7077896 | tf_op jit(solution)/shard_map/convert_element_type | solution.py:624
  147.8 2.7 %collective-permute-start.12 = (bf16[128,768]{1,0:T(8,128)(2,1)S(1)}, bf16[128,768]{1,0:T(8,128)(2,1)S(1)}, u32[]{:S(2)}, u32[]{:S(2)}) collective-permute-start(bf16[128,768]{1,0:T(8,128)(2,1)S(1)} %pad_maximum_fusion.3), channel_id=1, source_target_pairs={{0,8},{1,5},{2,10},{3,7},{4,12},{5,1},{6,14},{7,3},{8,0},{9,13},{1... | collective-permute-start | bytes 589832 | tf_op jit(solution)/shard_map/ppermute | solution.py:620
  150.4 6.2 %collective-permute-done.12 = bf16[128,768]{1,0:T(8,128)(2,1)S(1)} collective-permute-done((bf16[128,768]{1,0:T(8,128)(2,1)S(1)}, bf16[128,768]{1,0:T(8,128)(2,1)S(1)}, u32[]{:S(2)}, u32[]{:S(2)}) %collective-permute-start.12) | collective-permute-done | bytes 196640 | tf_op jit(solution)/shard_map/ppermute | solution.py:620
  160.8 2.9 %add_convert_fusion.2 = (bf16[1,2,2,96,768]{4,3,2,1,0:T(8,128)(2,1)}, bf16[2,2,96,768]{3,2,1,0:T(8,128)(2,1)}) fusion(bf16[2,2,2,96,768]{4,3,2,1,0:T(8,128)(2,1)} %bitcast.25, s32[]{:T(128)S(6)} %select_n.97, bf16[2,2,2,96,768]{4,3,2,1,0:T(8,128)(2,1)} %bitcast.60, s32[]{:T(128)S(6)} %select_n.96), kind=kLoop, calls=%fused_computation.3 | loop fusion | flops 2359296 | bytes 3538952 | tf_op jit(solution)/shard_map/convert_element_type | solution.py:624
  175.7 3.4 %collective-permute-done.16 = bf16[2,2,96,768]{3,2,1,0:T(8,128)(2,1)} collective-permute-done((bf16[2,2,96,768]{3,2,1,0:T(8,128)(2,1)}, bf16[2,2,96,768]{3,2,1,0:T(8,128)(2,1)}, u32[]{:S(2)}, u32[]{:S(2)}) %collective-permute-start.16) | collective-permute-done | bytes 589856 | tf_op jit(solution)/shard_map/ppermute | solution.py:620
  180.9 4.5 %collective-permute-done.15.refs_0_ = bf16[416,768]{1,0:T(8,128)(2,1)} collective-permute-done((bf16[416,768]{1,0:T(8,128)(2,1)}, bf16[416,768]{1,0:T(8,128)(2,1)}, u32[]{:S(2)}, u32[]{:S(2)}) %collective-permute-start.15) | collective-permute-done | bytes 639008 | tf_op jit(solution)/shard_map/ppermute | solution.py:613
  185.4 3.9 %collective-permute-done.17.refs_2_.refs_0_ = bf16[416,768]{1,0:T(8,128)(2,1)} collective-permute-done((bf16[416,768]{1,0:T(8,128)(2,1)}, bf16[416,768]{1,0:T(8,128)(2,1)}, u32[]{:S(2)}, u32[]{:S(2)}) %collective-permute-start.17) | collective-permute-done | bytes 639008 | tf_op jit(solution)/shard_map/ppermute | solution.py:613
  192.2 3.4 %maximum_select_fusion = (bf16[2,1,256,768]{3,2,1,0:T(8,128)(2,1)}, bf16[2,1,256,768]{3,2,1,0:T(8,128)(2,1)}) fusion(bf16[1,1,256,768]{3,2,1,0:T(8,128)(2,1)} %bitcast.29, bf16[1,1,256,768]{3,2,1,0:T(8,128)(2,1)} %bitcast.69, pred[]{:T(512)S(6)} %eq.4, bf16[1,1,256,768]{3,2,1,0:T(8,128)(2,1)} %bitcast.70, bf16[1,1,256,768]{3,2,1,0:T(8,128)(2,1)} %bitcast.31), kind=kLoop, calls=%fused_computation.7 | loop fusion | flops 2359296 | bytes 3145729 | tf_op jit(solution)/shard_map/jit(_where)/select_n | solution.py:830
  195.6 4.8 %shard_map.426 = (f32[16,48,768]{2,1,0:T(8,128)}, f32[16,48,768]{2,1,0:T(8,128)}, f32[16,48,768]{2,1,0:T(8,128)}, f32[16,48,768]{2,1,0:T(8,128)}) custom-call(s32[8]{0:T(128)} %stack.63.refs_0_, bf16[416,768]{1,0:T(8,128)(2,1)} %pad_maximum_fusion.refs_1_.refs_5_, bf16[416,768]{1,0:T(8,128)(2,1)} %shard_map.424.refs_4_.refs_2_.refs_6_, ...), custom_call_target="tpu_custom_call" | custom-call | bytes 11993088 | tf_op jit(solution)/shard_map/pallas_call | solution.py:162
  204.6 5.5 %shard_map.428 = (f32[16,48,768]{2,1,0:T(8,128)}, f32[16,48,768]{2,1,0:T(8,128)}, f32[16,48,768]{2,1,0:T(8,128)}, f32[16,48,768]{2,1,0:T(8,128)}, f32[768]{0:T(1...) custom-call(s32[8]{0:T(128)} %stack.63.refs_0_, ...), custom_call_target="tpu_custom_call", output_to_operand_aliasing={{0}: (13, {}), {1}: (14, {}), {2}: (15, {}), {3}: (16, {})} | custom-call | bytes 28419072 | tf_op jit(solution)/shard_map/pallas_call | solution.py:162
  (85 shorter events, 55.8 us)
Async XLA Ops:
  2.7 12.4 %collective-permute-start = (bf16[256,768]{1,0:T(8,128)(2,1)}, bf16[256,768]{1,0:T(8,128)(2,1)}, u32[]{:S(2)}, u32[]{:S(2)}) collective-permute-start(bf16[256,768]{1,0:T(8,128)(2,1)} %get-tuple-element.171), channel_id=1, source_target_pairs={{0,16},{16,0},{1,17},{17,1},{2,18},{18,2},{3,19},{19,3},{4,20},{20... | collective-permute-start | bytes 1179656 | tf_op jit(solution)/shard_map/ppermute | solution.py:34
  15.1 18.1 %collective-permute-start.1 = (bf16[256,768]{1,0:T(8,128)(2,1)}, bf16[256,768]{1,0:T(8,128)(2,1)}, u32[]{:S(2)}, u32[]{:S(2)}) collective-permute-start(bf16[256,768]{1,0:T(8,128)(2,1)} %get-tuple-element.108), channel_id=1, source_target_pairs={{0,16},{16,0},{1,17},{17,1},{2,18},{18,2},{3,19},{19,3},{4,20},{20... | collective-permute-start | bytes 1179656 | tf_op jit(solution)/shard_map/ppermute | solution.py:34
  33.2 26.7 %collective-permute-start.2 = (bf16[2,512,768]{2,1,0:T(8,128)(2,1)}, bf16[2,512,768]{2,1,0:T(8,128)(2,1)}, u32[]{:S(2)}, u32[]{:S(2)}) collective-permute-start(bf16[2,512,768]{2,1,0:T(8,128)(2,1)} %shard_map.406.refs_1_), channel_id=1, source_target_pairs={{0,1},{1,0},{2,3},{3,2},{4,5},{5,4},{6,7},{7,6},{8,9},{9,8},{10,11... | collective-permute-start | bytes 4718600 | tf_op jit(solution)/shard_map/ppermute | solution.py:34
  59.9 16.2 %collective-permute-start.3 = (bf16[256,768]{1,0:T(8,128)(2,1)}, bf16[256,768]{1,0:T(8,128)(2,1)}, u32[]{:S(2)}, u32[]{:S(2)}) collective-permute-start(bf16[256,768]{1,0:T(8,128)(2,1)} %shard_map.407.refs_12_), channel_id=1, source_target_pairs={{0,16},{16,0},{1,17},{17,1},{2,18},{18,2},{3,19},{19,3},{4,20},{20... | collective-permute-start | bytes 1179656 | tf_op jit(solution)/shard_map/ppermute | solution.py:34
  76.1 3.8 %collective-permute-start.4 = (bf16[2,512,768]{2,1,0:T(8,128)(2,1)}, bf16[2,512,768]{2,1,0:T(8,128)(2,1)}, u32[]{:S(2)}, u32[]{:S(2)}) collective-permute-start(bf16[2,512,768]{2,1,0:T(8,128)(2,1)} %shard_map.409), channel_id=1, source_target_pairs={{0,1},{1,0},{2,3},{3,2},{4,5},{5,4},{6,7},{7,6},{8,9},{9,8},{10,11... | collective-permute-start | bytes 4718600 | tf_op jit(solution)/shard_map/ppermute | solution.py:34
  80.0 8.3 %collective-permute-start.5 = (bf16[512,4608]{1,0:T(8,128)(2,1)}, bf16[512,4608]{1,0:T(8,128)(2,1)}, u32[]{:S(2)}, u32[]{:S(2)}) collective-permute-start(bf16[512,4608]{1,0:T(8,128)(2,1)} %shard_map.410.refs_5_), channel_id=1, source_target_pairs={{0,1},{1,0},{2,3},{3,2},{4,5},{5,4},{6,7},{7,6},{8,9},{9,8},{10,11... | collective-permute-start | bytes 14155784 | tf_op jit(solution)/shard_map/ppermute | solution.py:34
  88.2 16.5 %collective-permute-start.6 = (bf16[8,2,48,768]{3,2,1,0:T(8,128)(2,1)}, bf16[8,2,48,768]{3,2,1,0:T(8,128)(2,1)}, u32[]{:S(2)}, u32[]{:S(2)}) collective-permute-start(bf16[8,2,48,768]{3,2,1,0:T(8,128)(2,1)} %shard_map.412.refs_12_), channel_id=1, source_target_pairs={{0,2},{1,17},{2,0},{3,19},{4,6},{5,21},{6,4},{7,23},{8,10},{9,25},... | collective-permute-start | bytes 3538952 | tf_op jit(solution)/shard_map/ppermute | solution.py:613
  102.3 37.5 %collective-permute-start.7 = (bf16[8,2,96,768]{3,2,1,0:T(8,128)(2,1)}, bf16[8,2,96,768]{3,2,1,0:T(8,128)(2,1)}, u32[]{:S(2)}, u32[]{:S(2)}) collective-permute-start(bf16[8,2,96,768]{3,2,1,0:T(8,128)(2,1)} %get-tuple-element.127), channel_id=1, source_target_pairs={{0,2},{1,17},{2,0},{3,19},{4,6},{5,21},{6,4},{7,23},{8,10},{9,25},... | collective-permute-start | bytes 7077896 | tf_op jit(solution)/shard_map/ppermute | solution.py:613
  106.9 16.6 %collective-permute-start.8 = (bf16[4,2,48,768]{3,2,1,0:T(8,128)(2,1)}, bf16[4,2,48,768]{3,2,1,0:T(8,128)(2,1)}, u32[]{:S(2)}, u32[]{:S(2)}) collective-permute-start(bf16[4,2,48,768]{3,2,1,0:T(8,128)(2,1)} %fusion.1.refs_5_.refs_1_), channel_id=1, source_target_pairs={{0,16},{1,3},{2,18},{3,1},{4,20},{5,7},{6,22},{7,5},{8,24},{9,11},... | collective-permute-start | bytes 1769480 | tf_op jit(solution)/shard_map/ppermute | solution.py:613
  125.7 9.0 %collective-permute-start.10 = (bf16[2,2,48,768]{3,2,1,0:T(8,128)(2,1)}, bf16[2,2,48,768]{3,2,1,0:T(8,128)(2,1)}, u32[]{:S(2)}, u32[]{:S(2)}) collective-permute-start(bf16[2,2,48,768]{3,2,1,0:T(8,128)(2,1)} %get-tuple-element.170.refs_1_), channel_id=1, source_target_pairs={{0,4},{1,9},{2,6},{3,11},{4,0},{5,13},{6,2},{7,15},{8,12},{9,1},{1... | collective-permute-start | bytes 884744 | tf_op jit(solution)/shard_map/ppermute | solution.py:620
  127.5 12.4 %collective-permute-start.9 = (bf16[256,768]{1,0:T(8,128)(2,1)}, bf16[256,768]{1,0:T(8,128)(2,1)}, u32[]{:S(2)}, u32[]{:S(2)}) collective-permute-start(bf16[256,768]{1,0:T(8,128)(2,1)} %shard_map.419), channel_id=1, source_target_pairs={{0,16},{16,0},{1,17},{17,1},{2,18},{18,2},{3,19},{19,3},{4,20},{20... | collective-permute-start | bytes 1179656 | tf_op jit(solution)/shard_map/ppermute | solution.py:34
  136.4 9.4 %collective-permute-start.11 = (bf16[1,2,48,768]{3,2,1,0:T(8,128)(2,1)}, bf16[1,2,48,768]{3,2,1,0:T(8,128)(2,1)}, u32[]{:S(2)}, u32[]{:S(2)}) collective-permute-start(bf16[1,2,48,768]{3,2,1,0:T(8,128)(2,1)} %fusion.7.refs_2_), channel_id=1, source_target_pairs={{0,8},{1,5},{2,10},{3,7},{4,12},{5,1},{6,14},{7,3},{8,0},{9,13},{1... | collective-permute-start | bytes 442376 | tf_op jit(solution)/shard_map/ppermute | solution.py:620
  144.3 16.5 %collective-permute-start.14 = (bf16[4,2,96,768]{3,2,1,0:T(8,128)(2,1)}, bf16[4,2,96,768]{3,2,1,0:T(8,128)(2,1)}, u32[]{:S(2)}, u32[]{:S(2)}) collective-permute-start(bf16[4,2,96,768]{3,2,1,0:T(8,128)(2,1)} %get-tuple-element.166.refs_1_), channel_id=1, source_target_pairs={{0,16},{1,3},{2,18},{3,1},{4,20},{5,7},{6,22},{7,5},{8,24},{9,11},... | collective-permute-start | bytes 3538952 | tf_op jit(solution)/shard_map/ppermute | solution.py:613
  147.8 8.8 %collective-permute-start.12 = (bf16[128,768]{1,0:T(8,128)(2,1)S(1)}, bf16[128,768]{1,0:T(8,128)(2,1)S(1)}, u32[]{:S(2)}, u32[]{:S(2)}) collective-permute-start(bf16[128,768]{1,0:T(8,128)(2,1)S(1)} %pad_maximum_fusion.3), channel_id=1, source_target_pairs={{0,8},{1,5},{2,10},{3,7},{4,12},{5,1},{6,14},{7,3},{8,0},{9,13},{1... | collective-permute-start | bytes 589832 | tf_op jit(solution)/shard_map/ppermute | solution.py:620
  157.5 10.0 %collective-permute-start.13 = (bf16[224,768]{1,0:T(8,128)(2,1)}, bf16[224,768]{1,0:T(8,128)(2,1)}, u32[]{:S(2)}, u32[]{:S(2)}) collective-permute-start(bf16[224,768]{1,0:T(8,128)(2,1)} %pad_maximum_fusion.1), channel_id=1, source_target_pairs={{0,4},{1,9},{2,6},{3,11},{4,0},{5,13},{6,2},{7,15},{8,12},{9,1},{1... | collective-permute-start | bytes 1032200 | tf_op jit(solution)/shard_map/ppermute | solution.py:620
  163.7 15.4 %collective-permute-start.16 = (bf16[2,2,96,768]{3,2,1,0:T(8,128)(2,1)}, bf16[2,2,96,768]{3,2,1,0:T(8,128)(2,1)}, u32[]{:S(2)}, u32[]{:S(2)}) collective-permute-start(bf16[2,2,96,768]{3,2,1,0:T(8,128)(2,1)} %get-tuple-element.168.refs_1_), channel_id=1, source_target_pairs={{0,4},{1,9},{2,6},{3,11},{4,0},{5,13},{6,2},{7,15},{8,12},{9,1},{1... | collective-permute-start | bytes 1769480 | tf_op jit(solution)/shard_map/ppermute | solution.py:620
  171.2 14.2 %collective-permute-start.15 = (bf16[416,768]{1,0:T(8,128)(2,1)}, bf16[416,768]{1,0:T(8,128)(2,1)}, u32[]{:S(2)}, u32[]{:S(2)}) collective-permute-start(bf16[416,768]{1,0:T(8,128)(2,1)} %pad_maximum_fusion.refs_1_.refs_5_), channel_id=1, source_target_pairs={{0,16},{1,3},{2,18},{3,1},{4,20},{5,7},{6,22},{7,5},{8,24},{9,11},... | collective-permute-start | bytes 1916936 | tf_op jit(solution)/shard_map/ppermute | solution.py:613
  172.4 16.9 %collective-permute-start.17 = (bf16[416,768]{1,0:T(8,128)(2,1)}, bf16[416,768]{1,0:T(8,128)(2,1)}, u32[]{:S(2)}, u32[]{:S(2)}) collective-permute-start(bf16[416,768]{1,0:T(8,128)(2,1)} %pad_maximum_fusion.refs_1_.refs_5_), channel_id=1, source_target_pairs={{0,2},{1,17},{2,0},{3,19},{4,6},{5,21},{6,4},{7,23},{8,10},{9,25},... | collective-permute-start | bytes 1916936 | tf_op jit(solution)/shard_map/ppermute | solution.py:613
  174.5 21.1 %collective-permute-start.19 = (bf16[416,768]{1,0:T(8,128)(2,1)}, bf16[416,768]{1,0:T(8,128)(2,1)}, u32[]{:S(2)}, u32[]{:S(2)}) collective-permute-start(bf16[416,768]{1,0:T(8,128)(2,1)} %pad_maximum_fusion.refs_1_.refs_5_), channel_id=1, source_target_pairs={{0,1},{1,0},{2,3},{3,2},{4,5},{5,4},{6,7},{7,6},{8,9},{9,8},{10,11... | collective-permute-start | bytes 1916936 | tf_op jit(solution)/shard_map/ppermute | solution.py:34
  189.3 6.3 %collective-permute-start.20 = (bf16[416,768]{1,0:T(8,128)(2,1)}, bf16[416,768]{1,0:T(8,128)(2,1)}, u32[]{:S(2)}, u32[]{:S(2)}) collective-permute-start(bf16[416,768]{1,0:T(8,128)(2,1)} %shard_map.424.refs_4_.refs_2_.refs_6_), channel_id=1, source_target_pairs={{0,1},{1,0},{2,3},{3,2},{4,5},{5,4},{6,7},{7,6},{8,9},{9,8},{10,11... | collective-permute-start | bytes 1916936 | tf_op jit(solution)/shard_map/ppermute | solution.py:34
  189.9 10.7 %collective-permute-start.18 = (bf16[416,768]{1,0:T(8,128)(2,1)}, bf16[416,768]{1,0:T(8,128)(2,1)}, u32[]{:S(2)}, u32[]{:S(2)}) collective-permute-start(bf16[416,768]{1,0:T(8,128)(2,1)} %shard_map.424.refs_4_.refs_2_.refs_6_), channel_id=1, source_target_pairs={{0,2},{1,17},{2,0},{3,19},{4,6},{5,21},{6,4},{7,23},{8,10},{9,25},... | collective-permute-start | bytes 1916936 | tf_op jit(solution)/shard_map/ppermute | solution.py:613
  191.9 10.6 %collective-permute-start.23 = (bf16[1,2,96,768]{3,2,1,0:T(8,128)(2,1)}, bf16[1,2,96,768]{3,2,1,0:T(8,128)(2,1)}, u32[]{:S(2)}, u32[]{:S(2)}) collective-permute-start(bf16[1,2,96,768]{3,2,1,0:T(8,128)(2,1)} %fusion.4.refs_1_), channel_id=1, source_target_pairs={{0,8},{1,5},{2,10},{3,7},{4,12},{5,1},{6,14},{7,3},{8,0},{9,13},{1... | collective-permute-start | bytes 884744 | tf_op jit(solution)/shard_map/ppermute | solution.py:620
  200.6 4.0 %collective-permute-start.21 = (bf16[416,768]{1,0:T(8,128)(2,1)}, bf16[416,768]{1,0:T(8,128)(2,1)}, u32[]{:S(2)}, u32[]{:S(2)}) collective-permute-start(bf16[416,768]{1,0:T(8,128)(2,1)} %get-tuple-element.143.refs_1_.refs_7_), channel_id=1, source_target_pairs={{0,1},{1,0},{2,3},{3,2},{4,5},{5,4},{6,7},{7,6},{8,9},{9,8},{10,11... | collective-permute-start | bytes 1916936 | tf_op jit(solution)/shard_map/ppermute | solution.py:34
  200.6 4.0 %collective-permute-start.22 = (bf16[416,768]{1,0:T(8,128)(2,1)}, bf16[416,768]{1,0:T(8,128)(2,1)}, u32[]{:S(2)}, u32[]{:S(2)}) collective-permute-start(bf16[416,768]{1,0:T(8,128)(2,1)} %get-tuple-element.144.refs_2_.refs_8_), channel_id=1, source_target_pairs={{0,1},{1,0},{2,3},{3,2},{4,5},{5,4},{6,7},{7,6},{8,9},{9,8},{10,11... | collective-permute-start | bytes 1916936 | tf_op jit(solution)/shard_map/ppermute | solution.py:34
  (5 other events, 36.2 us)

commit v4 on v3

--- a/solution.py
+++ b/solution.py
@@ -904,8 +904,7 @@
         (hidden_got,) = tie([hidden_got], [data])
         hidden, hidden_sent = halved(hidden, hidden_got, third)
         hidden_got = lined(hidden_sent, True)
-        wait = lambda value: tie([value], [hidden_sent])[0]
-        data, block = longer(data, block, lambda value: wait(lined(value, True)))
+        data, block = longer(data, block, lambda value: lined(value, True))
         piece = jnp.concatenate([data, block])
         cross_got = crossed(piece, False)
         turned = crossed(piece, True)

time: 212 us -> 211 us (level)
  waiting for transfers between devices: 39.5 us -> 44.2 us
  other arithmetic: 28.1 us -> 24.5 us
    ppermute x6, waiting for transfers between devices: 18.5 us -> 29.2 us  [lined(): return lax.ppermute(value, everywhere, pairs)]
    ppermute x7, waiting for transfers between devices: 15.9 us -> 9.77 us  [crossed(): return lax.ppermute(value, everywhere, pairs)]
  transfers between devices with their start and end apart: 24 -> 24, of which waited for: 15 -> 14; matrix products, arithmetic and copies ran while one was open for 15% -> 11% of each run, Pallas kernels for 48% -> 48%
where the time goes in v4:
time: 211 us; the launch traced here: 209 us
  Pallas kernels  107 us (51%)
  waiting for transfers between devices  44.2 us (21%)
  starting transfers between devices  28.9 us (14%)
  other arithmetic  24.5 us (12%)
  local copies, waits for them, and re-layouts  3.65 us (2%)
    pallas_call x12, Pallas kernels, run(): pl.pallas_call(wrapped, grid_spec=pltpu.PrefetchScalarGridSpec(num_scalar...  107 us
    ppermute x6, waiting for transfers between devices, lined(): return lax.ppermute(value, everywhere, pairs)  29.2 us
    convert_element_type x8, other arithmetic, plus(): return (left.astype(f32) + right.astype(f32)).astype(bf16)  16.6 us
    ppermute x6, starting transfers between devices, lined(): return lax.ppermute(value, everywhere, pairs)  10.2 us
    ppermute x7, starting transfers between devices, crossed(): return lax.ppermute(value, everywhere, pairs)  9.88 us
    ppermute x7, waiting for transfers between devices, crossed(): return lax.ppermute(value, everywhere, pairs)  9.77 us
    ppermute x11, starting transfers between devices, swapped(): lax.ppermute(value, axis, [(i, i ^ 1 << bit) for i in range(lax.axis_size...  8.87 us
    ppermute x11, waiting for transfers between devices, swapped(): lax.ppermute(value, axis, [(i, i ^ 1 << bit) for i in range(lax.axis_size...  5.26 us
  transfers between devices with their start and end apart: 24, of which 14 were waited for; matrix products, arithmetic and copies ran while one was open for 11% of the time, Pallas kernels for 48%

profile of v4, /device:TPU:0, one launch (start us, length us, event | category | flops | bytes accessed | tf_op | source)
XLA Modules:
  0.0 209.5 jit_solution(8303794367446810619)
XLA Ops:
  2.7 3.0 %collective-permute-start = (bf16[256,768]{1,0:T(8,128)(2,1)}, bf16[256,768]{1,0:T(8,128)(2,1)}, u32[]{:S(2)}, u32[]{:S(2)}) collective-permute-start(bf16[256,768]{1,0:T(8,128)(2,1)} %get-tuple-element.171), channel_id=1, source_target_pairs={{0,16},{16,0},{1,17},{17,1},{2,18},{18,2},{3,19},{19,3},{4,20},{20... | collective-permute-start | bytes 1179656 | tf_op jit(solution)/shard_map/ppermute | solution.py:34
  6.3 4.0 %shard_map.400 = (f32[1,128]{1,0:T(1,128)}, f32[1,512]{1,0:T(1,128)}, f32[1,512]{1,0:T(1,128)}, f32[1,768]{1,0:T(1,128)}, f32[512,1]{1,0:T(8,128)}, /*index=5*/f...) custom-call(s32[8]{0:T(128)} %stack.63.refs_0_, s32[2]{0:T(128)} %refs_1_.2, s32[2]{0:T(128)} %refs_2_.2, ...), custom_call_target="tpu_custom_call" | custom-call | bytes 2120192 | tf_op jit(solution)/shard_map/pallas_call | solution.py:162
  10.3 4.7 %shard_map.401 = (bf16[256,768]{1,0:T(8,128)(2,1)}, bf16[256,768]{1,0:T(8,128)(2,1)}, bf16[256,768]{1,0:T(8,128)(2,1)}, bf16[256,768]{1,0:T(8,128)(2,1)}) custom-call(bf16[256,768]{1,0:T(8,128)(2,1)} %get-tuple-element.172.refs_0_.refs_2_, f32[1,768]{1,0:T(1,128)} %get-tuple-element.93.refs_1_.refs_4_, f32[512,1]{1,0:T(8,128)} %get-tuple-element.94.refs_2_.refs_11_, ...), custom_call_target="tpu_custom_call" | custom-call | flops 905969664 | bytes 5516288 | tf_op jit(solution)/shard_map/pallas_call | solution.py:162
  16.8 4.8 %shard_map.403 = (bf16[256,768]{1,0:T(8,128)(2,1)}, bf16[256,768]{1,0:T(8,128)(2,1)}, bf16[256,768]{1,0:T(8,128)(2,1)}, bf16[256,768]{1,0:T(8,128)(2,1)}) custom-call(bf16[256,768]{1,0:T(8,128)(2,1)} %shard_map.402.refs_0_.refs_3_, f32[1,768]{1,0:T(1,128)} %get-tuple-element.93.refs_1_.refs_4_, f32[512,1]{1,0:T(8,128)} %get-tuple-element.94.refs_2_.refs_11_, ...), custom_call_target="tpu_custom_call" | custom-call | flops 905969664 | bytes 5516288 | tf_op jit(solution)/shard_map/pallas_call | solution.py:162
  21.7 11.5 %shard_map.404 = (bf16[512,768]{1,0:T(8,128)(2,1)}, bf16[2,512,768]{2,1,0:T(8,128)(2,1)}, bf16[12,512,512]{2,1,0:T(8,128)(2,1)}) custom-call(bf16[256,768]{1,0:T(8,128)(2,1)} %get-tuple-element.95.refs_1_.refs_0_.refs_5_, bf16[256,768]{1,0:T(8,128)(2,1)} %get-tuple-element.98.refs_1_.refs_6_, bf16[256,768]{1,0:T(8,128)(2,1)} %get-tuple-element.99.refs_2_.refs_7_, ...), custom_call_target="tpu_custom_call" | custom-call | flops 3221225472 | bytes 11798528 | tf_op jit(solution)/shard_map/pallas_call | solution.py:162
  33.3 26.7 %shard_map.405 = (bf16[256,768]{1,0:T(8,128)(2,1)}, bf16[256,768]{1,0:T(8,128)(2,1)}, bf16[512,4608]{1,0:T(8,128)(2,1)}, bf16[512,1536]{1,0:T(8,128)(2,1)}, bf16...) custom-call(s32[8]{0:T(128)} %stack.63.refs_0_, ...), custom_call_target="tpu_custom_call" | custom-call | flops 10267656192 | bytes 26024960 | tf_op jit(solution)/shard_map/pallas_call | solution.py:162
  60.3 15.8 %shard_map.408 = (bf16[3,512,768]{2,1,0:T(8,128)(2,1)}, bf16[2,512,768]{2,1,0:T(8,128)(2,1)}, bf16[2,512,768]{2,1,0:T(8,128)(2,1)}, f32[8,768]{1,0:T(8,128)}) custom-call(s32[8]{0:T(128)} %stack.63.refs_0_, bf16[512,768]{1,0:T(8,128)(2,1)} %get-tuple-element.112.refs_1_.refs_2_, bf16[512,768]{1,0:T(8,128)(2,1)} %get-tuple-element.112.refs_1_.refs_2_, ...), custom_call_target="tpu_custom_call" | custom-call | flops 8053063680 | bytes 16934912 | tf_op jit(solution)/shard_map/pallas_call | solution.py:162
  76.6 3.4 %collective-permute-done.4.refs_1_.refs_4_ = bf16[2,512,768]{2,1,0:T(8,128)(2,1)} collective-permute-done((bf16[2,512,768]{2,1,0:T(8,128)(2,1)}, bf16[2,512,768]{2,1,0:T(8,128)(2,1)}, u32[]{:S(2)}, u32[]{:S(2)}) %collective-permute-start.4) | collective-permute-done | bytes 1572896 | tf_op jit(solution)/shard_map/ppermute | solution.py:34
  80.4 6.7 %shard_map.411 = (bf16[8,2,48,768]{3,2,1,0:T(8,128)(2,1)}, bf16[8,2,48,768]{3,2,1,0:T(8,128)(2,1)}) custom-call(s32[8]{0:T(128)} %stack.63.refs_0_, bf16[2,512,768]{2,1,0:T(8,128)(2,1)} %shard_map.406.refs_1_, bf16[2,512,768]{2,1,0:T(8,128)(2,1)} %get-tuple-element.116.refs_2_, bf16[2,512,768]{2,1,0:T(8,128)(2,1)} %collective-permute-done.2.refs_1_.refs_3_, ...), custom_call_target="tpu_custom_call" | custom-call | flops 2415919104 | bytes 8650752 | tf_op jit(solution)/shard_map/pallas_call | solution.py:162
  89.9 12.5 %shard_map.413 = (bf16[8,2,96,768]{3,2,1,0:T(8,128)(2,1)}, bf16[8,2,96,768]{3,2,1,0:T(8,128)(2,1)}) custom-call(s32[8]{0:T(128)} %stack.63.refs_0_, bf16[512,1536]{1,0:T(8,128)(2,1)} %get-tuple-element.121.refs_1_, bf16[512,768]{1,0:T(8,128)(2,1)} %get-tuple-element.122.refs_2_, bf16[512,1536]{1,0:T(8,128)(2,1)} %get-tuple-element.123.refs_3_, ...), custom_call_target="tpu_custom_call" | custom-call | flops 4831838208 | bytes 42467328 | tf_op jit(solution)/shard_map/pallas_call | solution.py:162
  108.7 6.2 %shard_map.415 = (bf16[256,768]{1,0:T(8,128)(2,1)}, bf16[256,768]{1,0:T(8,128)(2,1)}, f32[1,768]{1,0:T(1,128)}) custom-call(bf16[3,512,768]{2,1,0:T(8,128)(2,1)} %get-tuple-element.114.refs_0_, bf16[768,768]{1,0:T(8,128)(2,1)} %refs_1_.3, bf16[768,768]{1,0:T(8,128)(2,1)} %refs_2_.3, bf16[768,768]{1,0:T(8,128)(2,1)} %refs_3_.9, ...), custom_call_target="tpu_custom_call" | custom-call | flops 1811939328 | bytes 8260608 | tf_op jit(solution)/shard_map/pallas_call | solution.py:162
  114.9 3.9 %shard_map.417.refs_1_ = bf16[32,768]{1,0:T(8,128)(2,1)} custom-call(s32[8]{0:T(128)} %stack.63.refs_0_, f32[8,768]{1,0:T(8,128)} %get-tuple-element.129.refs_1_, f32[8,768]{1,0:T(8,128)} %get-tuple-element.130.refs_2_, f32[4,1,768]{2,1,0:T(1,128)} %get-tuple-element.131.refs_3_, f32[1,768]{1,0:T(1,128)} %get-tuple-element.132.refs_4_, ...), custom_call_target="tpu_custom_call" | custom-call | bytes 904704 | tf_op jit(solution)/shard_map/pallas_call | solution.py:162
  120.9 2.6 %collective-permute-done.8.refs_0_ = bf16[4,2,48,768]{3,2,1,0:T(8,128)(2,1)} collective-permute-done((bf16[4,2,48,768]{3,2,1,0:T(8,128)(2,1)}, bf16[4,2,48,768]{3,2,1,0:T(8,128)(2,1)}, u32[]{:S(2)}, u32[]{:S(2)}) %collective-permute-start.8) | collective-permute-done | bytes 589856 | tf_op jit(solution)/shard_map/ppermute | solution.py:613
  129.0 4.9 %collective-permute-done.10 = bf16[2,2,48,768]{3,2,1,0:T(8,128)(2,1)} collective-permute-done((bf16[2,2,48,768]{3,2,1,0:T(8,128)(2,1)}, bf16[2,2,48,768]{3,2,1,0:T(8,128)(2,1)}, u32[]{:S(2)}, u32[]{:S(2)}) %collective-permute-start.10) | collective-permute-done | bytes 294944 | tf_op jit(solution)/shard_map/ppermute | solution.py:620
  135.6 3.8 %collective-permute-start.11 = (bf16[1,2,48,768]{3,2,1,0:T(8,128)(2,1)}, bf16[1,2,48,768]{3,2,1,0:T(8,128)(2,1)}, u32[]{:S(2)}, u32[]{:S(2)}) collective-permute-start(bf16[1,2,48,768]{3,2,1,0:T(8,128)(2,1)} %fusion.7.refs_2_), channel_id=1, source_target_pairs={{0,8},{1,5},{2,10},{3,7},{4,12},{5,1},{6,14},{7,3},{8,0},{9,13},{1... | collective-permute-start | bytes 442376 | tf_op jit(solution)/shard_map/ppermute | solution.py:620
  139.9 4.4 %add_convert_fusion = (bf16[1,4,2,96,768]{4,3,2,1,0:T(8,128)(2,1)}, bf16[4,2,96,768]{3,2,1,0:T(8,128)(2,1)}) fusion(bf16[2,4,2,96,768]{4,3,2,1,0:T(8,128)(2,1)} %bitcast.21, s32[]{:T(128)S(6)} %select_n.94, bf16[2,4,2,96,768]{4,3,2,1,0:T(8,128)(2,1)} %bitcast.59, s32[]{:T(128)S(6)} %select_n.93), kind=kLoop, calls=%fused_computation | loop fusion | flops 4718592 | bytes 7077896 | tf_op jit(solution)/shard_map/convert_element_type | solution.py:624
  147.8 2.7 %collective-permute-start.12 = (bf16[128,768]{1,0:T(8,128)(2,1)S(1)}, bf16[128,768]{1,0:T(8,128)(2,1)S(1)}, u32[]{:S(2)}, u32[]{:S(2)}) collective-permute-start(bf16[128,768]{1,0:T(8,128)(2,1)S(1)} %pad_maximum_fusion.3), channel_id=1, source_target_pairs={{0,8},{1,5},{2,10},{3,7},{4,12},{5,1},{6,14},{7,3},{8,0},{9,13},{1... | collective-permute-start | bytes 589832 | tf_op jit(solution)/shard_map/ppermute | solution.py:620
  150.5 6.2 %collective-permute-done.12 = bf16[128,768]{1,0:T(8,128)(2,1)S(1)} collective-permute-done((bf16[128,768]{1,0:T(8,128)(2,1)S(1)}, bf16[128,768]{1,0:T(8,128)(2,1)S(1)}, u32[]{:S(2)}, u32[]{:S(2)}) %collective-permute-start.12) | collective-permute-done | bytes 196640 | tf_op jit(solution)/shard_map/ppermute | solution.py:620
  157.6 8.9 %collective-permute-done.13 = bf16[224,768]{1,0:T(8,128)(2,1)S(1)} collective-permute-done((bf16[224,768]{1,0:T(8,128)(2,1)S(1)}, bf16[224,768]{1,0:T(8,128)(2,1)S(1)}, u32[]{:S(2)}, u32[]{:S(2)}) %collective-permute-start.13) | collective-permute-done | bytes 344096 | tf_op jit(solution)/shard_map/ppermute | solution.py:620
  173.9 8.6 %collective-permute-done.16 = bf16[2,2,96,768]{3,2,1,0:T(8,128)(2,1)S(1)} collective-permute-done((bf16[2,2,96,768]{3,2,1,0:T(8,128)(2,1)S(1)}, bf16[2,2,96,768]{3,2,1,0:T(8,128)(2,1)S(1)}, u32[]{:S(2)}, u32[]{:S(2)}) %collective-permute-start.16) | collective-permute-done | bytes 589856 | tf_op jit(solution)/shard_map/ppermute | solution.py:620
  185.6 3.0 %collective-permute-done.17.refs_2_.refs_0_ = bf16[416,768]{1,0:T(8,128)(2,1)} collective-permute-done((bf16[416,768]{1,0:T(8,128)(2,1)}, bf16[416,768]{1,0:T(8,128)(2,1)}, u32[]{:S(2)}, u32[]{:S(2)}) %collective-permute-start.17) | collective-permute-done | bytes 639008 | tf_op jit(solution)/shard_map/ppermute | solution.py:613
  192.2 3.4 %maximum_select_fusion = (bf16[2,1,256,768]{3,2,1,0:T(8,128)(2,1)}, bf16[2,1,256,768]{3,2,1,0:T(8,128)(2,1)}) fusion(bf16[1,1,256,768]{3,2,1,0:T(8,128)(2,1)} %bitcast.29, bf16[1,1,256,768]{3,2,1,0:T(8,128)(2,1)} %bitcast.69, pred[]{:T(512)S(6)} %eq.4, bf16[1,1,256,768]{3,2,1,0:T(8,128)(2,1)} %bitcast.70, bf16[1,1,256,768]{3,2,1,0:T(8,128)(2,1)} %bitcast.31), kind=kLoop, calls=%fused_computation.7 | loop fusion | flops 2359296 | bytes 3145729 | tf_op jit(solution)/shard_map/jit(_where)/select_n | solution.py:830
  195.6 4.8 %shard_map.425 = (f32[16,48,768]{2,1,0:T(8,128)}, f32[16,48,768]{2,1,0:T(8,128)}, f32[16,48,768]{2,1,0:T(8,128)}, f32[16,48,768]{2,1,0:T(8,128)}) custom-call(s32[8]{0:T(128)} %stack.63.refs_0_, bf16[416,768]{1,0:T(8,128)(2,1)} %pad_maximum_fusion.refs_1_.refs_5_, bf16[416,768]{1,0:T(8,128)(2,1)} %shard_map.423.refs_4_.refs_2_.refs_6_, ...), custom_call_target="tpu_custom_call" | custom-call | bytes 11993088 | tf_op jit(solution)/shard_map/pallas_call | solution.py:162
  203.8 5.5 %shard_map.427 = (f32[16,48,768]{2,1,0:T(8,128)}, f32[16,48,768]{2,1,0:T(8,128)}, f32[16,48,768]{2,1,0:T(8,128)}, f32[16,48,768]{2,1,0:T(8,128)}, f32[768]{0:T(1...) custom-call(s32[8]{0:T(128)} %stack.63.refs_0_, ...), custom_call_target="tpu_custom_call", output_to_operand_aliasing={{0}: (13, {}), {1}: (14, {}), {2}: (15, {}), {3}: (16, {})} | custom-call | bytes 28419072 | tf_op jit(solution)/shard_map/pallas_call | solution.py:162
  (93 shorter events, 46.4 us)
Async XLA Ops:
  2.7 12.4 %collective-permute-start = (bf16[256,768]{1,0:T(8,128)(2,1)}, bf16[256,768]{1,0:T(8,128)(2,1)}, u32[]{:S(2)}, u32[]{:S(2)}) collective-permute-start(bf16[256,768]{1,0:T(8,128)(2,1)} %get-tuple-element.171), channel_id=1, source_target_pairs={{0,16},{16,0},{1,17},{17,1},{2,18},{18,2},{3,19},{19,3},{4,20},{20... | collective-permute-start | bytes 1179656 | tf_op jit(solution)/shard_map/ppermute | solution.py:34
  15.1 18.1 %collective-permute-start.1 = (bf16[256,768]{1,0:T(8,128)(2,1)}, bf16[256,768]{1,0:T(8,128)(2,1)}, u32[]{:S(2)}, u32[]{:S(2)}) collective-permute-start(bf16[256,768]{1,0:T(8,128)(2,1)} %get-tuple-element.108), channel_id=1, source_target_pairs={{0,16},{16,0},{1,17},{17,1},{2,18},{18,2},{3,19},{19,3},{4,20},{20... | collective-permute-start | bytes 1179656 | tf_op jit(solution)/shard_map/ppermute | solution.py:34
  33.2 26.8 %collective-permute-start.2 = (bf16[2,512,768]{2,1,0:T(8,128)(2,1)}, bf16[2,512,768]{2,1,0:T(8,128)(2,1)}, u32[]{:S(2)}, u32[]{:S(2)}) collective-permute-start(bf16[2,512,768]{2,1,0:T(8,128)(2,1)} %shard_map.406.refs_1_), channel_id=1, source_target_pairs={{0,1},{1,0},{2,3},{3,2},{4,5},{5,4},{6,7},{7,6},{8,9},{9,8},{10,11... | collective-permute-start | bytes 4718600 | tf_op jit(solution)/shard_map/ppermute | solution.py:34
  60.0 16.1 %collective-permute-start.3 = (bf16[256,768]{1,0:T(8,128)(2,1)}, bf16[256,768]{1,0:T(8,128)(2,1)}, u32[]{:S(2)}, u32[]{:S(2)}) collective-permute-start(bf16[256,768]{1,0:T(8,128)(2,1)} %shard_map.407.refs_12_), channel_id=1, source_target_pairs={{0,16},{16,0},{1,17},{17,1},{2,18},{18,2},{3,19},{19,3},{4,20},{20... | collective-permute-start | bytes 1179656 | tf_op jit(solution)/shard_map/ppermute | solution.py:34
  76.1 3.8 %collective-permute-start.4 = (bf16[2,512,768]{2,1,0:T(8,128)(2,1)}, bf16[2,512,768]{2,1,0:T(8,128)(2,1)}, u32[]{:S(2)}, u32[]{:S(2)}) collective-permute-start(bf16[2,512,768]{2,1,0:T(8,128)(2,1)} %shard_map.409), channel_id=1, source_target_pairs={{0,1},{1,0},{2,3},{3,2},{4,5},{5,4},{6,7},{7,6},{8,9},{9,8},{10,11... | collective-permute-start | bytes 4718600 | tf_op jit(solution)/shard_map/ppermute | solution.py:34
  80.0 8.3 %collective-permute-start.5 = (bf16[512,4608]{1,0:T(8,128)(2,1)}, bf16[512,4608]{1,0:T(8,128)(2,1)}, u32[]{:S(2)}, u32[]{:S(2)}) collective-permute-start(bf16[512,4608]{1,0:T(8,128)(2,1)} %shard_map.410.refs_5_), channel_id=1, source_target_pairs={{0,1},{1,0},{2,3},{3,2},{4,5},{5,4},{6,7},{7,6},{8,9},{9,8},{10,11... | collective-permute-start | bytes 14155784 | tf_op jit(solution)/shard_map/ppermute | solution.py:34
  88.2 16.5 %collective-permute-start.6 = (bf16[8,2,48,768]{3,2,1,0:T(8,128)(2,1)}, bf16[8,2,48,768]{3,2,1,0:T(8,128)(2,1)}, u32[]{:S(2)}, u32[]{:S(2)}) collective-permute-start(bf16[8,2,48,768]{3,2,1,0:T(8,128)(2,1)} %shard_map.412.refs_12_), channel_id=1, source_target_pairs={{0,2},{1,17},{2,0},{3,19},{4,6},{5,21},{6,4},{7,23},{8,10},{9,25},... | collective-permute-start | bytes 3538952 | tf_op jit(solution)/shard_map/ppermute | solution.py:613
  102.4 37.5 %collective-permute-start.7 = (bf16[8,2,96,768]{3,2,1,0:T(8,128)(2,1)}, bf16[8,2,96,768]{3,2,1,0:T(8,128)(2,1)}, u32[]{:S(2)}, u32[]{:S(2)}) collective-permute-start(bf16[8,2,96,768]{3,2,1,0:T(8,128)(2,1)} %get-tuple-element.127), channel_id=1, source_target_pairs={{0,2},{1,17},{2,0},{3,19},{4,6},{5,21},{6,4},{7,23},{8,10},{9,25},... | collective-permute-start | bytes 7077896 | tf_op jit(solution)/shard_map/ppermute | solution.py:613
  107.0 16.6 %collective-permute-start.8 = (bf16[4,2,48,768]{3,2,1,0:T(8,128)(2,1)}, bf16[4,2,48,768]{3,2,1,0:T(8,128)(2,1)}, u32[]{:S(2)}, u32[]{:S(2)}) collective-permute-start(bf16[4,2,48,768]{3,2,1,0:T(8,128)(2,1)} %fusion.1.refs_5_.refs_1_), channel_id=1, source_target_pairs={{0,16},{1,3},{2,18},{3,1},{4,20},{5,7},{6,22},{7,5},{8,24},{9,11},... | collective-permute-start | bytes 1769480 | tf_op jit(solution)/shard_map/ppermute | solution.py:613
  125.7 8.2 %collective-permute-start.10 = (bf16[2,2,48,768]{3,2,1,0:T(8,128)(2,1)}, bf16[2,2,48,768]{3,2,1,0:T(8,128)(2,1)}, u32[]{:S(2)}, u32[]{:S(2)}) collective-permute-start(bf16[2,2,48,768]{3,2,1,0:T(8,128)(2,1)} %get-tuple-element.170.refs_1_), channel_id=1, source_target_pairs={{0,4},{1,9},{2,6},{3,11},{4,0},{5,13},{6,2},{7,15},{8,12},{9,1},{1... | collective-permute-start | bytes 884744 | tf_op jit(solution)/shard_map/ppermute | solution.py:620
  127.5 12.4 %collective-permute-start.9 = (bf16[256,768]{1,0:T(8,128)(2,1)}, bf16[256,768]{1,0:T(8,128)(2,1)}, u32[]{:S(2)}, u32[]{:S(2)}) collective-permute-start(bf16[256,768]{1,0:T(8,128)(2,1)} %shard_map.419), channel_id=1, source_target_pairs={{0,16},{16,0},{1,17},{17,1},{2,18},{18,2},{3,19},{19,3},{4,20},{20... | collective-permute-start | bytes 1179656 | tf_op jit(solution)/shard_map/ppermute | solution.py:34
  135.6 10.2 %collective-permute-start.11 = (bf16[1,2,48,768]{3,2,1,0:T(8,128)(2,1)}, bf16[1,2,48,768]{3,2,1,0:T(8,128)(2,1)}, u32[]{:S(2)}, u32[]{:S(2)}) collective-permute-start(bf16[1,2,48,768]{3,2,1,0:T(8,128)(2,1)} %fusion.7.refs_2_), channel_id=1, source_target_pairs={{0,8},{1,5},{2,10},{3,7},{4,12},{5,1},{6,14},{7,3},{8,0},{9,13},{1... | collective-permute-start | bytes 442376 | tf_op jit(solution)/shard_map/ppermute | solution.py:620
  144.3 22.9 %collective-permute-start.15 = (bf16[4,2,96,768]{3,2,1,0:T(8,128)(2,1)}, bf16[4,2,96,768]{3,2,1,0:T(8,128)(2,1)}, u32[]{:S(2)}, u32[]{:S(2)}) collective-permute-start(bf16[4,2,96,768]{3,2,1,0:T(8,128)(2,1)} %get-tuple-element.166.refs_1_), channel_id=1, source_target_pairs={{0,16},{1,3},{2,18},{3,1},{4,20},{5,7},{6,22},{7,5},{8,24},{9,11},... | collective-permute-start | bytes 3538952 | tf_op jit(solution)/shard_map/ppermute | solution.py:613
  147.8 8.8 %collective-permute-start.12 = (bf16[128,768]{1,0:T(8,128)(2,1)S(1)}, bf16[128,768]{1,0:T(8,128)(2,1)S(1)}, u32[]{:S(2)}, u32[]{:S(2)}) collective-permute-start(bf16[128,768]{1,0:T(8,128)(2,1)S(1)} %pad_maximum_fusion.3), channel_id=1, source_target_pairs={{0,8},{1,5},{2,10},{3,7},{4,12},{5,1},{6,14},{7,3},{8,0},{9,13},{1... | collective-permute-start | bytes 589832 | tf_op jit(solution)/shard_map/ppermute | solution.py:620
  156.8 9.7 %collective-permute-start.13 = (bf16[224,768]{1,0:T(8,128)(2,1)S(1)}, bf16[224,768]{1,0:T(8,128)(2,1)S(1)}, u32[]{:S(2)}, u32[]{:S(2)}) collective-permute-start(bf16[224,768]{1,0:T(8,128)(2,1)S(1)} %pad_maximum_fusion.1), channel_id=1, source_target_pairs={{0,4},{1,9},{2,6},{3,11},{4,0},{5,13},{6,2},{7,15},{8,12},{9,1},{1... | collective-permute-start | bytes 1032200 | tf_op jit(solution)/shard_map/ppermute | solution.py:620
  169.2 13.3 %collective-permute-start.16 = (bf16[2,2,96,768]{3,2,1,0:T(8,128)(2,1)S(1)}, bf16[2,2,96,768]{3,2,1,0:T(8,128)(2,1)S(1)}, u32[]{:S(2)}, u32[]{:S(2)}) collective-permute-start(bf16[2,2,96,768]{3,2,1,0:T(8,128)(2,1)S(1)} %get-tuple-element.168), channel_id=1, source_target_pairs={{0,4},{1,9},{2,6},{3,11},{4,0},{5,13},{6,2},{7,15},{8,12},{9,1},{1... | collective-permute-start | bytes 1769480 | tf_op jit(solution)/shard_map/ppermute | solution.py:620
  170.2 15.3 %collective-permute-start.14 = (bf16[416,768]{1,0:T(8,128)(2,1)}, bf16[416,768]{1,0:T(8,128)(2,1)}, u32[]{:S(2)}, u32[]{:S(2)}) collective-permute-start(bf16[416,768]{1,0:T(8,128)(2,1)} %pad_maximum_fusion.refs_1_.refs_5_), channel_id=1, source_target_pairs={{0,16},{1,3},{2,18},{3,1},{4,20},{5,7},{6,22},{7,5},{8,24},{9,11},... | collective-permute-start | bytes 1916936 | tf_op jit(solution)/shard_map/ppermute | solution.py:613
  171.5 17.1 %collective-permute-start.17 = (bf16[416,768]{1,0:T(8,128)(2,1)}, bf16[416,768]{1,0:T(8,128)(2,1)}, u32[]{:S(2)}, u32[]{:S(2)}) collective-permute-start(bf16[416,768]{1,0:T(8,128)(2,1)} %pad_maximum_fusion.refs_1_.refs_5_), channel_id=1, source_target_pairs={{0,2},{1,17},{2,0},{3,19},{4,6},{5,21},{6,4},{7,23},{8,10},{9,25},... | collective-permute-start | bytes 1916936 | tf_op jit(solution)/shard_map/ppermute | solution.py:613
  173.5 22.1 %collective-permute-start.19 = (bf16[416,768]{1,0:T(8,128)(2,1)}, bf16[416,768]{1,0:T(8,128)(2,1)}, u32[]{:S(2)}, u32[]{:S(2)}) collective-permute-start(bf16[416,768]{1,0:T(8,128)(2,1)} %pad_maximum_fusion.refs_1_.refs_5_), channel_id=1, source_target_pairs={{0,1},{1,0},{2,3},{3,2},{4,5},{5,4},{6,7},{7,6},{8,9},{9,8},{10,11... | collective-permute-start | bytes 1916936 | tf_op jit(solution)/shard_map/ppermute | solution.py:34
  188.6 7.0 %collective-permute-start.20 = (bf16[416,768]{1,0:T(8,128)(2,1)}, bf16[416,768]{1,0:T(8,128)(2,1)}, u32[]{:S(2)}, u32[]{:S(2)}) collective-permute-start(bf16[416,768]{1,0:T(8,128)(2,1)} %shard_map.423.refs_4_.refs_2_.refs_6_), channel_id=1, source_target_pairs={{0,1},{1,0},{2,3},{3,2},{4,5},{5,4},{6,7},{7,6},{8,9},{9,8},{10,11... | collective-permute-start | bytes 1916936 | tf_op jit(solution)/shard_map/ppermute | solution.py:34
  189.0 11.4 %collective-permute-start.18 = (bf16[416,768]{1,0:T(8,128)(2,1)}, bf16[416,768]{1,0:T(8,128)(2,1)}, u32[]{:S(2)}, u32[]{:S(2)}) collective-permute-start(bf16[416,768]{1,0:T(8,128)(2,1)} %shard_map.423.refs_4_.refs_2_.refs_6_), channel_id=1, source_target_pairs={{0,2},{1,17},{2,0},{3,19},{4,6},{5,21},{6,4},{7,23},{8,10},{9,25},... | collective-permute-start | bytes 1916936 | tf_op jit(solution)/shard_map/ppermute | solution.py:613
  190.4 11.1 %collective-permute-start.23 = (bf16[1,2,96,768]{3,2,1,0:T(8,128)(2,1)}, bf16[1,2,96,768]{3,2,1,0:T(8,128)(2,1)}, u32[]{:S(2)}, u32[]{:S(2)}) collective-permute-start(bf16[1,2,96,768]{3,2,1,0:T(8,128)(2,1)} %fusion.4.refs_1_), channel_id=1, source_target_pairs={{0,8},{1,5},{2,10},{3,7},{4,12},{5,1},{6,14},{7,3},{8,0},{9,13},{1... | collective-permute-start | bytes 884744 | tf_op jit(solution)/shard_map/ppermute | solution.py:620
  200.4 3.2 %collective-permute-start.21 = (bf16[416,768]{1,0:T(8,128)(2,1)}, bf16[416,768]{1,0:T(8,128)(2,1)}, u32[]{:S(2)}, u32[]{:S(2)}) collective-permute-start(bf16[416,768]{1,0:T(8,128)(2,1)} %get-tuple-element.143.refs_1_.refs_7_), channel_id=1, source_target_pairs={{0,1},{1,0},{2,3},{3,2},{4,5},{5,4},{6,7},{7,6},{8,9},{9,8},{10,11... | collective-permute-start | bytes 1916936 | tf_op jit(solution)/shard_map/ppermute | solution.py:34
  200.5 3.3 %collective-permute-start.22 = (bf16[416,768]{1,0:T(8,128)(2,1)}, bf16[416,768]{1,0:T(8,128)(2,1)}, u32[]{:S(2)}, u32[]{:S(2)}) collective-permute-start(bf16[416,768]{1,0:T(8,128)(2,1)} %get-tuple-element.144.refs_2_.refs_8_), channel_id=1, source_target_pairs={{0,1},{1,0},{2,3},{3,2},{4,5},{5,4},{6,7},{7,6},{8,9},{9,8},{10,11... | collective-permute-start | bytes 1916936 | tf_op jit(solution)/shard_map/ppermute | solution.py:34
  (10 other events, 64.2 us)
